TPU v7x, 128 devices: a whole 4x4x4 slice. The times are simulated.
128 devices in a mesh: dp: 8 (over z, y_hi), expert: 16 (over x, y_lo, core).
Axes of the slice: x: 4, y: 4 (y_hi: 2, y_lo: 2; y = y_hi * 2 + y_lo), z: 4, core: 2. Of those that a mesh axis runs over, the one named last changes fastest.
Arguments:
- tokens: bfloat16 [16384, 3072], P(('dp', 'expert')), may hold values from -64 to 64
- attn_param: bfloat16 [18432, 128], P('dp'), may hold values from -0.75 to 0.75
- expert_ids: int32 [16384, 1], P(('dp', 'expert')), may hold values from 0 to 15; in each aligned block of 128 rows (0 to 127, 128 to 255, ...) at most 10 rows name the same one
- gate_score: float32 [16384, 1], P(('dp', 'expert')), may hold values from 0.25 to 1
- w_in: bfloat16 [16, 3072, 2, 5376], P('expert', None, None, 'dp'), may hold values from -0.109375 to 0.109375
- w_out: bfloat16 [16, 5376, 3072], P('expert', 'dp'), may hold values from -0.078125 to 0.078125
- cotangent: bfloat16 [16384, 3072], P(('dp', 'expert')), may hold values from -24 to 24
Outputs:
- grad_tokens: bfloat16 [16384, 3072], P(('dp', 'expert'))
- attn_grad: float32 [18432, 128], P(('dp', 'expert'))
Inputs may be any that keep to these rules, and one draw needn't show every extreme that they name: `expert_ids`: each row names 1 different experts. In the rows of one device no expert is named more than 10 times, and in every draw some device's rows name some expert exactly 10 times.
All inputs are finite; a program needn't handle non-finite values.
Results may differ from a plain program's by a relative error of at most 0.02.
Values may be sent and summed in bfloat16 or wider, within the bound.
No kernel may reach another device: no remote copies, remote signals or barrier semaphores. Data moves between devices by JAX's collectives and lax.ppermute only.
A program may use at most 128 MiB of HBM per device.

v0:
```python
import jax
import jax.numpy as jnp
from jax import lax
from jax.experimental import pallas as pl
from jax.experimental.pallas import tpu as pltpu
from jax.sharding import Mesh, PartitionSpec as P

EPSILON = 1e-05
MASKED = -1e30
AXES = ("z", "yh", "x", "yl", "c")
DP = ("z", "yh")
EX = ("x", "yl", "c")
CHIPS = ("z", "yh", "x", "yl")
SIZES = (4, 2, 4, 2, 2)
EXPERTS = 16
N_DP = 8
CAP = 10
MAIN = 8
HEADS = 2
HALF = 96
PADDED = 768
F32 = jnp.float32
BF16 = jnp.bfloat16


def layer_norm(values):
    widened = values.astype(F32)
    center = widened - jnp.mean(widened, axis=-1, keepdims=True)
    inverse = lax.rsqrt(jnp.mean(center * center, axis=-1, keepdims=True) + EPSILON)
    return (center * inverse, inverse)


def norm_back(normed, inverse, upstream):
    mean_grad = jnp.mean(upstream, axis=-1, keepdims=True)
    mean_proj = jnp.mean(upstream * normed, axis=-1, keepdims=True)
    return inverse * (upstream - mean_grad - normed * mean_proj)


def contract(first_op, second_op, first_dim, second_dim):
    return lax.dot_general(
        first_op,
        second_op,
        (((first_dim,), (second_dim,)), ((), ())),
        preferred_element_type=F32,
    )


def swap(values, axis):
    return lax.ppermute(values, axis, [(0, 1), (1, 0)])


def along_z(values, shift):
    return lax.ppermute(values, "z", [(i, (i + shift) % 4) for i in range(4)])


def exchange(blocks, axes):
    return lax.all_to_all(blocks, axes, split_axis=0, concat_axis=0, tiled=True)


def after(value, *earlier):
    return lax.optimization_barrier((value,) + earlier)[0]


def add_round(first, *others):
    total = first.astype(F32)
    for other in others:
        total = total + other.astype(F32)
    return total.astype(BF16)


def slot_matrix(expert_ids, seq_len):
    flat = expert_ids.reshape(-1)
    one_hot = (flat[:, None] == jnp.arange(EXPERTS, dtype=jnp.int32)[None, :]).astype(F32)
    rows = jnp.arange(seq_len)
    earlier = (rows[:, None] > rows[None, :]).astype(F32)
    before = jnp.dot(earlier, one_hot, preferred_element_type=F32)
    position = jnp.sum(before * one_hot, axis=1).astype(jnp.int32)
    rest = CAP - MAIN
    target = jnp.where(
        position < MAIN, flat * MAIN + position, EXPERTS * MAIN + flat * rest + position - MAIN
    )
    return (jnp.arange(EXPERTS * CAP, dtype=jnp.int32)[:, None] == target[None, :]).astype(BF16)


def place_kernel(places, piece, at_ref, *refs):
    block_refs, out_ref, sems = refs[: len(places)], refs[-2], refs[-1]
    copies = []
    number = 0
    for ref, parts in zip(block_refs, places):
        for i, (s, r, half) in enumerate(parts):
            z = lax.rem(at_ref[0] - s + 4, 4)
            yh = lax.rem(at_ref[1] + r, 2)
            copy = pltpu.make_async_copy(
                ref.at[pl.ds(i * piece, piece)], out_ref.at[z * 2 + yh, pl.ds(half * piece, piece)], sems.at[number]
            )
            copy.start()
            copies.append(copy)
            number += 1
    for copy in copies:
        copy.wait()


def gather_params(attn_param, earlier):
    rows, head_dim = attn_param.shape
    half = rows // 2
    piece = half // 2
    core = lax.axis_index("c")
    own = lax.dynamic_slice_in_dim(attn_param, core * half, half, 0)
    first, second = own[:piece], own[piece:]
    around = [along_z(first, s) for s in (1, 3, 2)]
    own_y = swap(own, "yh")
    pair = after(jnp.concatenate([second, own_y[piece:]], axis=0), around[0], around[1])
    earlier = after(earlier, own_y, *around)
    around_y = [swap(block, "yh") for block in around]
    pairs = [along_z(pair, s) for s in (1, 3, 2)]
    blocks = [own, own_y] + around + around_y + pairs
    places = (
        [[(0, 0, 0), (0, 0, 1)], [(0, 1, 0), (0, 1, 1)]]
        + [[(s, 0, 0)] for s in (1, 3, 2)]
        + [[(s, 1, 0)] for s in (1, 3, 2)]
        + [[(s, 0, 1), (s, 1, 1)] for s in (1, 3, 2)]
    )
    spread = spread_near(earlier)
    at = jnp.stack([lax.axis_index("z"), lax.axis_index("yh")]).astype(jnp.int32)
    at = after(at, *spread[1:4])
    anywhere = pl.BlockSpec(memory_space=pl.ANY)
    own = pl.pallas_call(
        lambda *refs: place_kernel(places, piece, *refs),
        out_shape=jax.ShapeDtypeStruct((N_DP, half, head_dim), BF16),
        in_specs=[pl.BlockSpec(memory_space=pltpu.SMEM)] + [anywhere] * len(blocks),
        out_specs=pl.BlockSpec(memory_space=pltpu.VMEM),
        scratch_shapes=[pltpu.SemaphoreType.DMA((16,))],
        compiler_params=pltpu.CompilerParams(vmem_limit_bytes=60 * 1024 * 1024),
    )(at, *blocks)
    other = swap(own, "c")
    first = jnp.where(core == 0, own, other)
    second = jnp.where(core == 0, other, own)
    return jnp.stack([first, second], axis=1).reshape(N_DP * rows, head_dim), spread


def between_experts(rows):
    features = rows.shape[1]
    cut = EXPERTS * MAIN
    extra = rows[cut:].reshape(cut, -1)
    packed = jnp.concatenate([rows[:cut], extra], axis=1)
    width = packed.shape[1]
    packed = exchange(packed.reshape(EXPERTS, MAIN, width), EX).reshape(cut, width)
    extra = packed[:, features:].reshape(-1, features)
    return packed[:, :features], extra


def spread_near(own):
    one = own[:HALF]
    own_y = swap(own, "yh")
    return [own, own_y] + [along_z(one, s) for s in (1, 3, 2)]


def spread_far(near, between):
    own, own_y, near_z, far_z, across = near
    pair = after(jnp.concatenate([own[HALF:], own_y[HALF:]], axis=0), near_z, far_z)
    first = [swap(near_z, "yh"), swap(far_z, "yh")]
    second = [along_z(pair, 1), along_z(pair, 3)]
    return first + [swap(after(across, *between), "yh")] + second + [along_z(pair, 2)]


def collect(near, far):
    kept, one_y, two_y, *one_z = near
    early = [along_z(block, -s) for block, s in zip(one_z, (1, 3, 2))]
    early_y = swap(two_y, "yh")
    *one_yz, two_z, two_yz = far
    (*one_yz, two_yz), early, early_y = lax.optimization_barrier(([*one_yz, two_yz], early, early_y))
    late = [along_z(block, -s) for block, s in zip(one_yz, (1, 3, 2))]
    swapped = swap(two_yz, "yh")
    across = swap(add_round(one_y, *late), "yh")
    pairs = add_round(two_z, swapped)
    rest = kept.shape[0] - HALF
    back = [along_z(pairs[i * rest : (i + 1) * rest], -s) for i, s in enumerate((1, 3, 2))]
    one = add_round(kept[:HALF], across, *early)
    two = add_round(kept[HALF:], early_y, *back)
    return jnp.concatenate([one, two], axis=0)


def expert_kernel(counts, pieces_out, tall, *refs):
    count = len(counts)
    outs = len(pieces_out)
    normed_refs, cot_refs = refs[:count], refs[count : 2 * count]
    inner_ref, outer_ref = refs[2 * count : 2 * count + 2]
    out_refs = refs[2 * count + 2 : 2 * count + 2 + outs]
    (normed, cot, gate_map, up_map, outer_map, grad_gate, grad_up, result, row_sem, map_sem, out_sem) = refs[
        2 * count + 2 + outs :
    ]
    hidden, features = outer_ref.shape
    starts = [sum(counts[:i]) for i in range(count)]

    def load(source, target, sem):
        copy = pltpu.make_async_copy(source, target, sem)
        copy.start()
        return copy

    def load_rows(block_refs, target, side):
        return [
            load(ref, target.at[pl.ds(starts[i], counts[i])], row_sem.at[side, i])
            for i, ref in enumerate(block_refs)
        ]

    pieces = [(0, 256), (256, 256), (512, hidden - 512)]
    rows_in = load_rows(normed_refs, normed, 0)
    maps_in = []
    for i, (start, size) in enumerate(pieces):
        at = pl.ds(start, size)
        maps_in.append(
            [
                load(inner_ref.at[0, at], gate_map.at[at], map_sem.at[0, i]),
                load(inner_ref.at[1, at], up_map.at[at], map_sem.at[1, i]),
                load(outer_ref.at[at], outer_map.at[at], map_sem.at[2, i]),
            ]
        )
        if i == 0:
            rows_in += load_rows(cot_refs, cot, 1)
    blank = jnp.zeros((PADDED - hidden, features), BF16)
    for ref in (gate_map, up_map, outer_map):
        ref[pl.ds(hidden, PADDED - hidden)] = blank
    for copy in rows_in:
        copy.wait()
    steps = sum(counts) // tall

    for i in range(len(pieces)):
        for copy in maps_in[i]:
            copy.wait()
        at = pl.ds(i * 256, 256)

        @pl.loop(0, steps)
        def _(step):
            here = pl.ds(pl.multiple_of(step * tall, 16), tall)
            gate_part = contract(normed[here], gate_map[at], 1, 1)
            up_part = contract(normed[here], up_map[at], 1, 1)
            grad_act = contract(cot[here], outer_map[at], 1, 1)
            squash = 1.0 / (1.0 + jnp.exp(-gate_part))
            scaled = grad_act * squash
            grad_gate[here, at] = (scaled * up_part * (1.0 + gate_part * (1.0 - squash))).astype(BF16)
            grad_up[here, at] = (scaled * gate_part).astype(BF16)

    wide = 512
    copies = []
    for n in range(features // wide):
        lanes = pl.ds(n * wide, wide)

        @pl.loop(0, steps)
        def _(step):
            here = pl.ds(pl.multiple_of(step * tall, 16), tall)
            result[here, lanes] = (
                contract(grad_gate[here], gate_map[:, lanes], 1, 0)
                + contract(grad_up[here], up_map[:, lanes], 1, 0)
            ).astype(BF16)

        number = 0
        for ref, parts in zip(out_refs, pieces_out):
            at = 0
            for start, size in parts:
                copies.append(
                    load(
                        result.at[pl.ds(start, size), lanes],
                        ref.at[pl.ds(at, size), lanes],
                        out_sem.at[n, number],
                    )
                )
                at += size
                number += 1
    for copy in copies:
        copy.wait()


def experts(normed_blocks, cot_blocks, inner, outer, pieces_out, tall):
    counts = [block.shape[0] for block in normed_blocks]
    features = normed_blocks[0].shape[1]
    hidden = outer.shape[0]
    total = sum(counts)
    anywhere = pl.BlockSpec(memory_space=pl.ANY)
    return pl.pallas_call(
        lambda *refs: expert_kernel(counts, pieces_out, tall, *refs),
        out_shape=[
            jax.ShapeDtypeStruct((sum(size for _, size in parts), features), BF16) for parts in pieces_out
        ],
        in_specs=[anywhere] * (2 * len(counts) + 2),
        out_specs=[anywhere] * len(pieces_out),
        scratch_shapes=[
            pltpu.VMEM((total, features), BF16),
            pltpu.VMEM((total, features), BF16),
            pltpu.VMEM((PADDED, features), BF16),
            pltpu.VMEM((PADDED, features), BF16),
            pltpu.VMEM((PADDED, features), BF16),
            pltpu.VMEM((total, PADDED), BF16),
            pltpu.VMEM((total, PADDED), BF16),
            pltpu.VMEM((total, features), BF16),
            pltpu.SemaphoreType.DMA((2, len(counts))),
            pltpu.SemaphoreType.DMA((3, 3)),
            pltpu.SemaphoreType.DMA((features // 512, sum(len(parts) for parts in pieces_out))),
        ],
        compiler_params=pltpu.CompilerParams(vmem_limit_bytes=60 * 1024 * 1024),
        cost_estimate=pl.CostEstimate(
            flops=10 * total * features * hidden,
            bytes_accessed=6 * total * features + 6 * hidden * features,
            transcendentals=total * hidden,
        ),
    )(*normed_blocks, *cot_blocks, inner, outer)


def param_kernel(scale, head_dim, core_ref, normed_ref, hidden_ref, grads_ref, context_ref, out_ref, terms):
    features = normed_ref.shape[1]
    tile = 1024
    for block in range(6):
        left_ref = normed_ref if block < 4 else hidden_ref
        right = (grads_ref[:, block * head_dim : (block + 1) * head_dim] if block < 4
                 else context_ref[:, (block - 4) * head_dim : (block - 3) * head_dim])
        for start in range(0, features, tile):
            part = contract(left_ref[:, start : start + tile], right, 0, 0) * scale
            terms[pl.ds(block * features + start, tile)] = part.astype(BF16)
    core = core_ref[0]

    @pl.loop(0, out_ref.shape[0])
    def _(group):
        size = out_ref.shape[1]
        out_ref[group] = terms[pl.ds(pl.multiple_of((2 * group + core) * size, 16), size)]


def param_terms(core, normed, hidden, grads, context, scale, head_dim):
    features = normed.shape[1]
    rows = 6 * features
    whole = pl.BlockSpec(memory_space=pltpu.VMEM)
    return pl.pallas_call(
        lambda *refs: param_kernel(scale, head_dim, *refs),
        out_shape=jax.ShapeDtypeStruct((64, rows // 128, head_dim), BF16),
        in_specs=[pl.BlockSpec(memory_space=pltpu.SMEM)] + [whole] * 4,
        out_specs=whole,
        scratch_shapes=[pltpu.VMEM((rows, head_dim), BF16)],
        compiler_params=pltpu.CompilerParams(vmem_limit_bytes=40 * 1024 * 1024),
        cost_estimate=pl.CostEstimate(
            flops=2 * rows * head_dim * normed.shape[0], bytes_accessed=8 * 1024 * 1024, transcendentals=0
        ),
    )(core, normed, hidden, grads, context)


def per_device(tokens, attn_param, expert_ids, gate_score, w_in, w_out, cotangent):
    seq_len, features = tokens.shape
    head_dim = attn_param.shape[1]
    score_scale = head_dim ** (-0.5)
    devices = N_DP * EXPERTS
    slots = slot_matrix(expert_ids, seq_len)
    inner = jnp.transpose(w_in[0], (1, 2, 0))
    outer = w_out[0]

    cot_main, cot_extra = between_experts(contract(slots, cotangent, 1, 0).astype(BF16))
    cot_rows = jnp.concatenate([cot_main, cot_extra], axis=0)
    packed, cot_near = gather_params(attn_param, cot_rows)
    cot_far = spread_far(cot_near, ())

    normed_one, inverse_one = layer_norm(tokens)
    normed_one_b = normed_one.astype(BF16)
    normed_both = jnp.concatenate([normed_one_b, swap(normed_one_b, "c")], axis=0)
    blocks = packed.reshape(2 * HEADS + 2, features, head_dim)
    project = blocks[: HEADS + 2]
    out_blocks = blocks[HEADS + 2 :]
    projected = jnp.einsum(
        "td,jdc->tjc", normed_one_b, project, preferred_element_type=F32
    ).astype(BF16)
    queries = projected[:, :HEADS]
    key_rows = projected[:, HEADS]
    value_rows = projected[:, HEADS + 1]
    scores = jnp.einsum("qhc,kc->hqk", queries, key_rows, preferred_element_type=F32) * score_scale
    causal = lax.broadcasted_iota(jnp.int32, (seq_len, seq_len), 0) >= lax.broadcasted_iota(
        jnp.int32, (seq_len, seq_len), 1
    )
    scores = jnp.where(causal[None], scores, MASKED)
    row_max = jnp.max(scores, axis=2, keepdims=True)
    raised = jnp.exp(scores - row_max)
    attention = raised / jnp.sum(raised, axis=2, keepdims=True)
    attention_b = attention.astype(BF16)
    context = jnp.einsum(
        "hqk,kc->qhc", attention_b, value_rows, preferred_element_type=F32
    ).astype(BF16)
    context_flat = context.reshape(seq_len, HEADS * head_dim)
    context_both = jnp.concatenate([context_flat, swap(context_flat, "c")], axis=0)
    attn_out = jnp.einsum("thc,hdc->td", context, out_blocks, preferred_element_type=F32)
    residual = (tokens.astype(F32) + attn_out).astype(BF16)
    normed_two, inverse_two = layer_norm(residual)
    normed_two_b = after(normed_two.astype(BF16), cot_near[4], cot_far[0], cot_far[3], cot_far[4])
    main, extra = between_experts(contract(slots, normed_two_b, 1, 0).astype(BF16))
    own = after(jnp.concatenate([main, extra], axis=0), cot_far[1], cot_far[2], cot_far[5])
    near = spread_near(own)
    near[4], normed_both, context_both = lax.optimization_barrier((near[4], normed_both, context_both))
    h = HALF
    whole = EXPERTS * CAP
    rest = whole - h
    near_rows = experts(
        near,
        cot_near,
        inner,
        outer,
        [[(0, whole)], [(whole, h)], [(whole + h, rest)]] + [[(2 * whole + i * h, h)] for i in range(3)],
        2 * whole + 3 * h,
    )
    far = spread_far(near, (near_rows[0],))
    far_rows = experts(
        far,
        cot_far,
        inner,
        outer,
        [[(i * h, h)] for i in range(3)]
        + [[(3 * h + (2 * i + r) * rest, rest) for i in range(3)] for r in (0, 1)],
        (h + 2 * rest) * 3 // 2,
    )
    back_main, back_extra = between_experts(collect(near_rows, far_rows))
    cut = EXPERTS * MAIN
    back_rows = contract(slots[:cut], back_main, 0, 0) + contract(slots[cut:], back_extra, 0, 0)
    moe_grad = gate_score * back_rows
    grad_hidden = cotangent.astype(F32) + norm_back(normed_two, inverse_two, moe_grad)
    grad_hidden_b = grad_hidden.astype(BF16)
    hidden_both = jnp.concatenate([grad_hidden_b, swap(grad_hidden_b, "c")], axis=0)
    grad_context = jnp.einsum(
        "td,hdc->thc", grad_hidden_b, out_blocks, preferred_element_type=F32
    )
    grad_context_b = grad_context.astype(BF16)
    grad_attention = jnp.einsum(
        "qhc,kc->hqk", grad_context_b, value_rows, preferred_element_type=F32
    )
    grad_value = jnp.einsum("hqk,qhc->kc", attention_b, grad_context_b, preferred_element_type=F32)
    grad_scores = (
        attention
        * (grad_attention - jnp.sum(grad_attention * attention, axis=2, keepdims=True))
        * score_scale
    )
    grad_scores_b = grad_scores.astype(BF16)
    grad_query = jnp.einsum("hqk,kc->qhc", grad_scores_b, key_rows, preferred_element_type=F32)
    grad_key = jnp.einsum("hqk,qhc->kc", grad_scores_b, queries, preferred_element_type=F32)
    grad_qkv = jnp.concatenate([grad_query, grad_key[:, None], grad_value[:, None]], axis=1).astype(BF16)
    grads_flat = grad_qkv.reshape(seq_len, (HEADS + 2) * head_dim)
    grads_both = jnp.concatenate([grads_flat, swap(grads_flat, "c")], axis=0)
    core = lax.axis_index("c").astype(jnp.int32).reshape(1)
    terms = param_terms(
        core, normed_both, hidden_both, grads_both, context_both, (seq_len * devices) ** (-0.5), head_dim
    )
    attn_grad = jnp.sum(exchange(terms, CHIPS).astype(F32), axis=0)
    grad_normed = jnp.einsum("tjc,jdc->td", grad_qkv, project, preferred_element_type=F32)
    grad_tokens = (grad_hidden + norm_back(normed_one, inverse_one, grad_normed)).astype(BF16)
    return (grad_tokens, attn_grad)


def solution(mesh):
    fine = Mesh(mesh.devices.reshape(SIZES), AXES)
    rows = P(AXES, None)
    in_specs = (
        rows,
        P(DP, None),
        rows,
        rows,
        P(EX, None, None, DP),
        P(EX, DP, None),
        rows,
    )
    return jax.shard_map(
        per_device, mesh=fine, in_specs=in_specs, out_specs=(rows, rows), check_vma=False
    )
```

profile of v0, /device:TPU:0, one launch (start us, length us, event | category | flops | bytes accessed | tf_op | source)
XLA Modules:
  0.0 435.5 jit_solution(10639492772289298750)
XLA Ops:
  5.0 5.5 %all-to-all-start = ((bf16[16,8,3840]{2,1,0:T(8,128)(2,1)}), bf16[16,8,3840]{2,1,0:T(8,128)(2,1)S(1)}, u32[]{:S(2)}, u32[]{:S(2)}) async-start(bf16[16,8,3840]{2,1,0:T(8,128)(2,1)} %pad_maximum_fusion.3), calls=%async_computation | async-start | bytes 1966080 | tf_op jit(solution)/shard_map/all_to_all | solution.py:57
  16.6 3.0 collective-permute-start
  19.6 6.7 %all-to-all-done = bf16[16,8,3840]{2,1,0:T(8,128)(2,1)S(1)} async-done(((bf16[16,8,3840]{2,1,0:T(8,128)(2,1)}), bf16[16,8,3840]{2,1,0:T(8,128)(2,1)S(1)}, u32[]{:S(2)}, u32[]{:S(2)}) %all-to-all-start) | async-done | bytes 983072 | tf_op jit(solution)/shard_map/all_to_all | solution.py:57
  26.7 6.3 %collective-permute-done.refs_2_ = bf16[1152,128]{1,0:T(8,128)(2,1)S(1)} collective-permute-done((bf16[1152,128]{1,0:T(8,128)(2,1)S(1)}, bf16[1152,128]{1,0:T(8,128)(2,1)S(1)}, u32[]{:S(2)}, u32[]{:S(2)}) %collective-permute-start) | collective-permute-done | bytes 294944 | tf_op jit(solution)/shard_map/ppermute | solution.py:49
  41.1 20.3 %collective-permute-done.7.refs_6_ = bf16[576,128]{1,0:T(8,128)(2,1)} collective-permute-done((bf16[576,128]{1,0:T(8,128)(2,1)}, bf16[576,128]{1,0:T(8,128)(2,1)}, u32[]{:S(2)}, u32[]{:S(2)}) %collective-permute-start.7) | collective-permute-done | bytes 147488 | tf_op jit(solution)/shard_map/ppermute | solution.py:49
  67.0 2.6 collective-permute-start.9
  70.3 2.9 collective-permute-done.8.refs_7_
  76.3 3.9 shard_map.86
  88.0 3.6 collective-permute-start.16
  103.1 13.2 %collective-permute-done.16.refs_9_ = bf16[128,3072]{1,0:T(8,128)(2,1)} collective-permute-done((bf16[128,3072]{1,0:T(8,128)(2,1)}, bf16[128,3072]{1,0:T(8,128)(2,1)}, u32[]{:S(2)}, u32[]{:S(2)}) %collective-permute-start.16) | collective-permute-done | bytes 786464 | tf_op jit(solution)/shard_map/ppermute | solution.py:53
  118.5 18.8 %all-to-all-start.1 = ((bf16[16,8,3840]{2,1,0:T(8,128)(2,1)}), bf16[16,8,3840]{2,1,0:T(8,128)(2,1)S(1)}, u32[]{:S(2)}, u32[]{:S(2)}) async-start(bf16[16,8,3840]{2,1,0:T(8,128)(2,1)} %pad_maximum_fusion.5), calls=%async_computation.1 | async-start | bytes 1966080 | tf_op jit(solution)/shard_map/all_to_all | solution.py:57
  141.8 11.3 %all-to-all-done.1 = bf16[16,8,3840]{2,1,0:T(8,128)(2,1)S(1)} async-done(((bf16[16,8,3840]{2,1,0:T(8,128)(2,1)}), bf16[16,8,3840]{2,1,0:T(8,128)(2,1)S(1)}, u32[]{:S(2)}, u32[]{:S(2)}) %all-to-all-start.1) | async-done | bytes 983072 | tf_op jit(solution)/shard_map/all_to_all | solution.py:57
  154.3 9.9 %collective-permute-done.18.refs_7_ = bf16[96,3072]{1,0:T(8,128)(2,1)} collective-permute-done((bf16[96,3072]{1,0:T(8,128)(2,1)}, bf16[96,3072]{1,0:T(8,128)(2,1)}, u32[]{:S(2)}, u32[]{:S(2)}) %collective-permute-start.18) | collective-permute-done | bytes 589856 | tf_op jit(solution)/shard_map/ppermute | solution.py:49
  164.2 12.3 %collective-permute-done.19.refs_8_ = bf16[96,3072]{1,0:T(8,128)(2,1)} collective-permute-done((bf16[96,3072]{1,0:T(8,128)(2,1)}, bf16[96,3072]{1,0:T(8,128)(2,1)}, u32[]{:S(2)}, u32[]{:S(2)}) %collective-permute-start.19) | collective-permute-done | bytes 589856 | tf_op jit(solution)/shard_map/ppermute | solution.py:49
  187.9 10.3 %collective-permute-done.24.refs_4_ = bf16[96,3072]{1,0:T(8,128)(2,1)} collective-permute-done((bf16[96,3072]{1,0:T(8,128)(2,1)}, bf16[96,3072]{1,0:T(8,128)(2,1)}, u32[]{:S(2)}, u32[]{:S(2)}) %collective-permute-start.24) | collective-permute-done | bytes 589856 | tf_op jit(solution)/shard_map/ppermute | solution.py:53
  198.3 10.9 %collective-permute-done.22.refs_2_ = bf16[96,3072]{1,0:T(8,128)(2,1)} collective-permute-done((bf16[96,3072]{1,0:T(8,128)(2,1)}, bf16[96,3072]{1,0:T(8,128)(2,1)}, u32[]{:S(2)}, u32[]{:S(2)}) %collective-permute-start.22) | collective-permute-done | bytes 589856 | tf_op jit(solution)/shard_map/ppermute | solution.py:53
  215.3 2.6 collective-permute-start.31
  218.8 27.3 %shard_map.87 = (bf16[160,3072]{1,0:T(8,128)(2,1)}, bf16[96,3072]{1,0:T(8,128)(2,1)}, bf16[64,3072]{1,0:T(8,128)(2,1)}, bf16[96,3072]{1,0:T(8,128)(2,1)}, bf16[9...) custom-call(bf16[160,3072]{1,0:T(8,128)(2,1)} %pad_maximum_fusion.6.refs_0_, ...), custom_call_target="tpu_custom_call" | custom-call | flops 12551454720 | bytes 23592960 | tf_op jit(solution)/shard_map/pallas_call | solution.py:279
  249.1 12.7 %collective-permute-done.29.refs_2_ = bf16[96,3072]{1,0:T(8,128)(2,1)S(1)} collective-permute-done((bf16[96,3072]{1,0:T(8,128)(2,1)}, bf16[96,3072]{1,0:T(8,128)(2,1)S(1)}, u32[]{:S(2)}, u32[]{:S(2)}) %collective-permute-start.29) | collective-permute-done | bytes 589856 | tf_op jit(solution)/shard_map/ppermute | solution.py:49
  266.4 28.0 %shard_map.88 = (bf16[96,3072]{1,0:T(8,128)(2,1)}, bf16[96,3072]{1,0:T(8,128)(2,1)}, bf16[96,3072]{1,0:T(8,128)(2,1)}, bf16[192,3072]{1,0:T(8,128)(2,1)}, bf16[192,3072]{1,0:T(8,128)(2,1)}) custom-call(bf16[96,3072]{1,0:T(8,128)(2,1)} %collective-permute-done.27.refs_0_, bf16[96,3072]{1,0:T(8,128)(2,1)} %collective-permute-done.28.refs_1_, ...), custom_call_target="tpu_custom_call" | custom-call | flops 13872660480 | bytes 24772608 | tf_op jit(solution)/shard_map/pallas_call | solution.py:279
  300.4 12.1 %collective-permute-done.39 = bf16[96,3072]{1,0:T(8,128)(2,1)S(1)} collective-permute-done((bf16[96,3072]{1,0:T(8,128)(2,1)}, bf16[96,3072]{1,0:T(8,128)(2,1)S(1)}, u32[]{:S(2)}, u32[]{:S(2)}) %collective-permute-start.39) | collective-permute-done | bytes 589856 | tf_op jit(solution)/shard_map/ppermute | solution.py:53
  312.5 8.8 %collective-permute-done.38 = bf16[96,3072]{1,0:T(8,128)(2,1)S(1)} collective-permute-done((bf16[96,3072]{1,0:T(8,128)(2,1)}, bf16[96,3072]{1,0:T(8,128)(2,1)S(1)}, u32[]{:S(2)}, u32[]{:S(2)}) %collective-permute-start.38) | collective-permute-done | bytes 589856 | tf_op jit(solution)/shard_map/ppermute | solution.py:53
  330.1 9.5 %collective-permute-done.40 = bf16[96,3072]{1,0:T(8,128)(2,1)S(1)} collective-permute-done((bf16[96,3072]{1,0:T(8,128)(2,1)S(1)}, bf16[96,3072]{1,0:T(8,128)(2,1)S(1)}, u32[]{:S(2)}, u32[]{:S(2)}) %collective-permute-start.40) | collective-permute-done | bytes 589856 | tf_op jit(solution)/shard_map/ppermute | solution.py:49
  339.6 2.7 add_convert_fusion.1
  342.3 3.4 collective-permute-done.43
  349.7 5.7 %all-to-all-start.2 = ((bf16[16,8,3840]{2,1,0:T(8,128)(2,1)}), bf16[16,8,3840]{2,1,0:T(8,128)(2,1)}, u32[]{:S(2)}, u32[]{:S(2)}) async-start(bf16[16,8,3840]{2,1,0:T(8,128)(2,1)} %pad_maximum_fusion.7), calls=%async_computation.2 | async-start | bytes 1966080 | tf_op jit(solution)/shard_map/all_to_all | solution.py:57
  355.5 15.8 %all-to-all-done.2 = bf16[16,8,3840]{2,1,0:T(8,128)(2,1)} async-done(((bf16[16,8,3840]{2,1,0:T(8,128)(2,1)}), bf16[16,8,3840]{2,1,0:T(8,128)(2,1)}, u32[]{:S(2)}, u32[]{:S(2)}) %all-to-all-start.2) | async-done | bytes 983072 | tf_op jit(solution)/shard_map/all_to_all | solution.py:57
  372.9 2.7 fusion.39
  389.0 4.7 %shard_map.89 = bf16[64,144,128]{2,1,0:T(8,128)(2,1)} custom-call(s32[1]{0:T(128)} %bitcast.37.refs_0_, bf16[256,3072]{1,0:T(8,128)(2,1)S(1)} %pad_maximum_fusion.1.refs_1_, bf16[256,3072]{1,0:T(8,128)(2,1)S(1)} %pad_maximum_fusion.2.refs_2_, bf16[256,512]{1,0:T(8,128)(2,1)S(1)} %pad_maximum_fusion.12.refs_3_, bf16[256,256]{1,0:T(8,128)(2,1)S(1)} %pad_maximum_fusion.13.refs_4_), custom_call_target="tpu_custom_call" | custom-call | flops 1207959552 | bytes 8388608 | tf_op jit(solution)/shard_map/pallas_call | solution.py:330
  393.7 6.6 %all-to-all-start.3 = ((bf16[64,144,128]{2,1,0:T(8,128)(2,1)}), bf16[64,144,128]{2,1,0:T(8,128)(2,1)S(1)}, u32[]{:S(2)}, u32[]{:S(2)}) async-start(bf16[64,144,128]{2,1,0:T(8,128)(2,1)} %shard_map.89), calls=%async_computation.3 | async-start | bytes 4718592 | tf_op jit(solution)/shard_map/all_to_all | solution.py:57
  400.4 3.3 fusion.79
  405.3 29.1 %all-to-all-done.3 = bf16[64,144,128]{2,1,0:T(8,128)(2,1)S(1)} async-done(((bf16[64,144,128]{2,1,0:T(8,128)(2,1)}), bf16[64,144,128]{2,1,0:T(8,128)(2,1)S(1)}, u32[]{:S(2)}, u32[]{:S(2)}) %all-to-all-start.3) | async-done | bytes 2359328 | tf_op jit(solution)/shard_map/all_to_all | solution.py:57
  (233 shorter events, 117.5 us)
Async XLA Ops:
  5.0 21.3 %all-to-all-start = ((bf16[16,8,3840]{2,1,0:T(8,128)(2,1)}), bf16[16,8,3840]{2,1,0:T(8,128)(2,1)S(1)}, u32[]{:S(2)}, u32[]{:S(2)}) async-start(bf16[16,8,3840]{2,1,0:T(8,128)(2,1)} %pad_maximum_fusion.3), calls=%async_computation | async-start | bytes 1966080 | tf_op jit(solution)/shard_map/all_to_all | solution.py:57
  33.0 33.0 %collective-permute-start.4 = (bf16[160,3072]{1,0:T(8,128)(2,1)S(1)}, bf16[160,3072]{1,0:T(8,128)(2,1)S(1)}, u32[]{:S(2)}, u32[]{:S(2)}) collective-permute-start(bf16[160,3072]{1,0:T(8,128)(2,1)S(1)} %pad_maximum_fusion.4.refs_5_), channel_id=1, source_target_pairs={{0,16},{16,0},{1,17},{17,1},{2,18},{18,2},{3,19},{19,3},{4,20},{20... | collective-permute-start | bytes 2949128 | tf_op jit(solution)/shard_map/ppermute | solution.py:49
  33.9 29.7 %collective-permute-start.5 = (bf16[96,3072]{1,0:T(8,128)(2,1)S(1)}, bf16[96,3072]{1,0:T(8,128)(2,1)}, u32[]{:S(2)}, u32[]{:S(2)}) collective-permute-start(bf16[96,3072]{1,0:T(8,128)(2,1)S(1)} %slice.104), channel_id=1, source_target_pairs={{0,32},{32,64},{64,96},{96,0},{1,33},{33,65},{65,97},{97,1},{2,34}... | collective-permute-start | bytes 1769480 | tf_op jit(solution)/shard_map/ppermute | solution.py:53
  35.7 29.4 %collective-permute-start.6 = (bf16[96,3072]{1,0:T(8,128)(2,1)S(1)}, bf16[96,3072]{1,0:T(8,128)(2,1)}, u32[]{:S(2)}, u32[]{:S(2)}) collective-permute-start(bf16[96,3072]{1,0:T(8,128)(2,1)S(1)} %slice.104), channel_id=1, source_target_pairs={{0,96},{32,0},{64,32},{96,64},{1,97},{33,1},{65,33},{97,65},{2,98}... | collective-permute-start | bytes 1769480 | tf_op jit(solution)/shard_map/ppermute | solution.py:53
  37.7 23.8 %collective-permute-start.7 = (bf16[576,128]{1,0:T(8,128)(2,1)}, bf16[576,128]{1,0:T(8,128)(2,1)}, u32[]{:S(2)}, u32[]{:S(2)}) collective-permute-start(bf16[576,128]{1,0:T(8,128)(2,1)} %copy-done.20), channel_id=1, source_target_pairs={{0,16},{16,0},{1,17},{17,1},{2,18},{18,2},{3,19},{19,3},{4,20},{20... | collective-permute-start | bytes 442376 | tf_op jit(solution)/shard_map/ppermute | solution.py:49
  40.6 34.2 %collective-permute-start.10 = (bf16[1152,128]{1,0:T(8,128)(2,1)}, bf16[1152,128]{1,0:T(8,128)(2,1)S(1)}, u32[]{:S(2)}, u32[]{:S(2)}) collective-permute-start(bf16[1152,128]{1,0:T(8,128)(2,1)} %pad_maximum_fusion.11), channel_id=1, source_target_pairs={{0,32},{32,64},{64,96},{96,0},{1,33},{33,65},{65,97},{97,1},{2,34}... | collective-permute-start | bytes 884744 | tf_op jit(solution)/shard_map/ppermute | solution.py:53
  82.1 21.0 %collective-permute-start.14 = (bf16[96,3072]{1,0:T(8,128)(2,1)S(1)}, bf16[96,3072]{1,0:T(8,128)(2,1)}, u32[]{:S(2)}, u32[]{:S(2)}) collective-permute-start(bf16[96,3072]{1,0:T(8,128)(2,1)S(1)} %slice.104), channel_id=1, source_target_pairs={{0,64},{32,96},{64,0},{96,32},{1,65},{33,97},{65,1},{97,33},{2,66}... | collective-permute-start | bytes 1769480 | tf_op jit(solution)/shard_map/ppermute | solution.py:53
  88.0 28.3 %collective-permute-start.16 = (bf16[128,3072]{1,0:T(8,128)(2,1)}, bf16[128,3072]{1,0:T(8,128)(2,1)}, u32[]{:S(2)}, u32[]{:S(2)}) collective-permute-start(bf16[128,3072]{1,0:T(8,128)(2,1)} %pad_maximum_fusion.9), channel_id=1, source_target_pairs={{0,32},{32,64},{64,96},{96,0},{1,33},{33,65},{65,97},{97,1},{2,34}... | collective-permute-start | bytes 2359304 | tf_op jit(solution)/shard_map/ppermute | solution.py:53
  91.7 25.1 %collective-permute-start.17 = (bf16[128,3072]{1,0:T(8,128)(2,1)}, bf16[128,3072]{1,0:T(8,128)(2,1)}, u32[]{:S(2)}, u32[]{:S(2)}) collective-permute-start(bf16[128,3072]{1,0:T(8,128)(2,1)} %pad_maximum_fusion.9), channel_id=1, source_target_pairs={{0,96},{32,0},{64,32},{96,64},{1,97},{33,1},{65,33},{97,65},{2,98}... | collective-permute-start | bytes 2359304 | tf_op jit(solution)/shard_map/ppermute | solution.py:53
  118.5 34.5 %all-to-all-start.1 = ((bf16[16,8,3840]{2,1,0:T(8,128)(2,1)}), bf16[16,8,3840]{2,1,0:T(8,128)(2,1)S(1)}, u32[]{:S(2)}, u32[]{:S(2)}) async-start(bf16[16,8,3840]{2,1,0:T(8,128)(2,1)} %pad_maximum_fusion.5), calls=%async_computation.1 | async-start | bytes 1966080 | tf_op jit(solution)/shard_map/all_to_all | solution.py:57
  137.3 39.2 %collective-permute-start.20 = (bf16[128,3072]{1,0:T(8,128)(2,1)}, bf16[128,3072]{1,0:T(8,128)(2,1)}, u32[]{:S(2)}, u32[]{:S(2)}) collective-permute-start(bf16[128,3072]{1,0:T(8,128)(2,1)} %pad_maximum_fusion.9), channel_id=1, source_target_pairs={{0,64},{32,96},{64,0},{96,32},{1,65},{33,97},{65,1},{97,33},{2,66}... | collective-permute-start | bytes 2359304 | tf_op jit(solution)/shard_map/ppermute | solution.py:53
  138.2 26.0 %collective-permute-start.18 = (bf16[96,3072]{1,0:T(8,128)(2,1)}, bf16[96,3072]{1,0:T(8,128)(2,1)}, u32[]{:S(2)}, u32[]{:S(2)}) collective-permute-start(bf16[96,3072]{1,0:T(8,128)(2,1)} %collective-permute-done.6.refs_8_), channel_id=1, source_target_pairs={{0,16},{16,0},{1,17},{17,1},{2,18},{18,2},{3,19},{19,3},{4,20},{20... | collective-permute-start | bytes 1769480 | tf_op jit(solution)/shard_map/ppermute | solution.py:49
  140.1 36.4 %collective-permute-start.19 = (bf16[96,3072]{1,0:T(8,128)(2,1)}, bf16[96,3072]{1,0:T(8,128)(2,1)}, u32[]{:S(2)}, u32[]{:S(2)}) collective-permute-start(bf16[96,3072]{1,0:T(8,128)(2,1)} %collective-permute-done.14.refs_9_), channel_id=1, source_target_pairs={{0,16},{16,0},{1,17},{17,1},{2,18},{18,2},{3,19},{19,3},{4,20},{20... | collective-permute-start | bytes 1769480 | tf_op jit(solution)/shard_map/ppermute | solution.py:49
  141.8 43.6 %collective-permute-start.25 = (bf16[128,3072]{1,0:T(8,128)(2,1)}, bf16[128,3072]{1,0:T(8,128)(2,1)}, u32[]{:S(2)}, u32[]{:S(2)}) collective-permute-start(bf16[128,3072]{1,0:T(8,128)(2,1)} %fusion.13), channel_id=1, source_target_pairs={{0,1},{1,0},{2,3},{3,2},{4,5},{5,4},{6,7},{7,6},{8,9},{9,8},{10,11... | collective-permute-start | bytes 2359304 | tf_op jit(solution)/shard_map/ppermute | solution.py:49
  176.5 36.2 %collective-permute-start.21 = (bf16[160,3072]{1,0:T(8,128)(2,1)}, bf16[160,3072]{1,0:T(8,128)(2,1)}, u32[]{:S(2)}, u32[]{:S(2)}) collective-permute-start(bf16[160,3072]{1,0:T(8,128)(2,1)} %pad_maximum_fusion.6.refs_0_), channel_id=1, source_target_pairs={{0,16},{16,0},{1,17},{17,1},{2,18},{18,2},{3,19},{19,3},{4,20},{20... | collective-permute-start | bytes 2949128 | tf_op jit(solution)/shard_map/ppermute | solution.py:49
  182.0 27.2 %collective-permute-start.22 = (bf16[96,3072]{1,0:T(8,128)(2,1)}, bf16[96,3072]{1,0:T(8,128)(2,1)}, u32[]{:S(2)}, u32[]{:S(2)}) collective-permute-start(bf16[96,3072]{1,0:T(8,128)(2,1)} %slice.119), channel_id=1, source_target_pairs={{0,32},{32,64},{64,96},{96,0},{1,33},{33,65},{65,97},{97,1},{2,34}... | collective-permute-start | bytes 1769480 | tf_op jit(solution)/shard_map/ppermute | solution.py:53
  183.7 27.5 %collective-permute-start.23 = (bf16[96,3072]{1,0:T(8,128)(2,1)}, bf16[96,3072]{1,0:T(8,128)(2,1)}, u32[]{:S(2)}, u32[]{:S(2)}) collective-permute-start(bf16[96,3072]{1,0:T(8,128)(2,1)} %slice.119), channel_id=1, source_target_pairs={{0,96},{32,0},{64,32},{96,64},{1,97},{33,1},{65,33},{97,65},{2,98}... | collective-permute-start | bytes 1769480 | tf_op jit(solution)/shard_map/ppermute | solution.py:53
  209.2 36.9 %collective-permute-start.27 = (bf16[96,3072]{1,0:T(8,128)(2,1)}, bf16[96,3072]{1,0:T(8,128)(2,1)}, u32[]{:S(2)}, u32[]{:S(2)}) collective-permute-start(bf16[96,3072]{1,0:T(8,128)(2,1)} %collective-permute-done.22.refs_2_), channel_id=1, source_target_pairs={{0,16},{16,0},{1,17},{17,1},{2,18},{18,2},{3,19},{19,3},{4,20},{20... | collective-permute-start | bytes 1769480 | tf_op jit(solution)/shard_map/ppermute | solution.py:49
  211.2 36.7 %collective-permute-start.28 = (bf16[96,3072]{1,0:T(8,128)(2,1)}, bf16[96,3072]{1,0:T(8,128)(2,1)}, u32[]{:S(2)}, u32[]{:S(2)}) collective-permute-start(bf16[96,3072]{1,0:T(8,128)(2,1)} %collective-permute-done.23.refs_3_), channel_id=1, source_target_pairs={{0,16},{16,0},{1,17},{17,1},{2,18},{18,2},{3,19},{19,3},{4,20},{20... | collective-permute-start | bytes 1769480 | tf_op jit(solution)/shard_map/ppermute | solution.py:49
  214.7 47.3 %collective-permute-start.30 = (bf16[128,3072]{1,0:T(8,128)(2,1)}, bf16[128,3072]{1,0:T(8,128)(2,1)}, u32[]{:S(2)}, u32[]{:S(2)}) collective-permute-start(bf16[128,3072]{1,0:T(8,128)(2,1)} %pad_maximum_fusion.10), channel_id=1, source_target_pairs={{0,32},{32,64},{64,96},{96,0},{1,33},{33,65},{65,97},{97,1},{2,34}... | collective-permute-start | bytes 2359304 | tf_op jit(solution)/shard_map/ppermute | solution.py:53
  215.3 49.1 %collective-permute-start.31 = (bf16[128,3072]{1,0:T(8,128)(2,1)}, bf16[128,3072]{1,0:T(8,128)(2,1)}, u32[]{:S(2)}, u32[]{:S(2)}) collective-permute-start(bf16[128,3072]{1,0:T(8,128)(2,1)} %pad_maximum_fusion.10), channel_id=1, source_target_pairs={{0,96},{32,0},{64,32},{96,64},{1,97},{33,1},{65,33},{97,65},{2,98}... | collective-permute-start | bytes 2359304 | tf_op jit(solution)/shard_map/ppermute | solution.py:53
  217.9 48.6 %collective-permute-start.32 = (bf16[128,3072]{1,0:T(8,128)(2,1)}, bf16[128,3072]{1,0:T(8,128)(2,1)}, u32[]{:S(2)}, u32[]{:S(2)}) collective-permute-start(bf16[128,3072]{1,0:T(8,128)(2,1)} %pad_maximum_fusion.10), channel_id=1, source_target_pairs={{0,64},{32,96},{64,0},{96,32},{1,65},{33,97},{65,1},{97,33},{2,66}... | collective-permute-start | bytes 2359304 | tf_op jit(solution)/shard_map/ppermute | solution.py:53
  247.9 46.6 %collective-permute-start.33 = (bf16[96,3072]{1,0:T(8,128)(2,1)}, bf16[96,3072]{1,0:T(8,128)(2,1)}, u32[]{:S(2)}, u32[]{:S(2)}) collective-permute-start(bf16[96,3072]{1,0:T(8,128)(2,1)} %get-tuple-element.47), channel_id=1, source_target_pairs={{0,96},{32,0},{64,32},{96,64},{1,97},{33,1},{65,33},{97,65},{2,98}... | collective-permute-start | bytes 1769480 | tf_op jit(solution)/shard_map/ppermute | solution.py:53
  261.8 32.7 %collective-permute-start.34 = (bf16[96,3072]{1,0:T(8,128)(2,1)}, bf16[96,3072]{1,0:T(8,128)(2,1)}, u32[]{:S(2)}, u32[]{:S(2)}) collective-permute-start(bf16[96,3072]{1,0:T(8,128)(2,1)} %get-tuple-element.48), channel_id=1, source_target_pairs={{0,32},{32,64},{64,96},{96,0},{1,33},{33,65},{65,97},{97,1},{2,34}... | collective-permute-start | bytes 1769480 | tf_op jit(solution)/shard_map/ppermute | solution.py:53
  262.0 32.5 %collective-permute-start.35 = (bf16[96,3072]{1,0:T(8,128)(2,1)}, bf16[96,3072]{1,0:T(8,128)(2,1)}, u32[]{:S(2)}, u32[]{:S(2)}) collective-permute-start(bf16[96,3072]{1,0:T(8,128)(2,1)} %get-tuple-element.49), channel_id=1, source_target_pairs={{0,64},{32,96},{64,0},{96,32},{1,65},{33,97},{65,1},{97,33},{2,66}... | collective-permute-start | bytes 1769480 | tf_op jit(solution)/shard_map/ppermute | solution.py:53
  264.5 30.0 %collective-permute-start.36 = (bf16[64,3072]{1,0:T(8,128)(2,1)}, bf16[64,3072]{1,0:T(8,128)(2,1)S(1)}, u32[]{:S(2)}, u32[]{:S(2)}) collective-permute-start(bf16[64,3072]{1,0:T(8,128)(2,1)} %get-tuple-element.50), channel_id=1, source_target_pairs={{0,16},{16,0},{1,17},{17,1},{2,18},{18,2},{3,19},{19,3},{4,20},{20... | collective-permute-start | bytes 1179656 | tf_op jit(solution)/shard_map/ppermute | solution.py:49
  295.6 25.7 %collective-permute-start.38 = (bf16[96,3072]{1,0:T(8,128)(2,1)}, bf16[96,3072]{1,0:T(8,128)(2,1)S(1)}, u32[]{:S(2)}, u32[]{:S(2)}) collective-permute-start(bf16[96,3072]{1,0:T(8,128)(2,1)} %get-tuple-element.52), channel_id=1, source_target_pairs={{0,32},{32,64},{64,96},{96,0},{1,33},{33,65},{65,97},{97,1},{2,34}... | collective-permute-start | bytes 1769480 | tf_op jit(solution)/shard_map/ppermute | solution.py:53
  298.0 23.3 %collective-permute-start.37 = (bf16[96,3072]{1,0:T(8,128)(2,1)}, bf16[96,3072]{1,0:T(8,128)(2,1)S(1)}, u32[]{:S(2)}, u32[]{:S(2)}) collective-permute-start(bf16[96,3072]{1,0:T(8,128)(2,1)} %get-tuple-element.51), channel_id=1, source_target_pairs={{0,96},{32,0},{64,32},{96,64},{1,97},{33,1},{65,33},{97,65},{2,98}... | collective-permute-start | bytes 1769480 | tf_op jit(solution)/shard_map/ppermute | solution.py:53
  298.9 25.9 %collective-permute-start.41 = (bf16[192,3072]{1,0:T(8,128)(2,1)}, bf16[192,3072]{1,0:T(8,128)(2,1)S(1)}, u32[]{:S(2)}, u32[]{:S(2)}) collective-permute-start(bf16[192,3072]{1,0:T(8,128)(2,1)} %get-tuple-element.59), channel_id=1, source_target_pairs={{0,16},{16,0},{1,17},{17,1},{2,18},{18,2},{3,19},{19,3},{4,20},{20... | collective-permute-start | bytes 3538952 | tf_op jit(solution)/shard_map/ppermute | solution.py:49
  326.7 18.9 %collective-permute-start.43 = (bf16[64,3072]{1,0:T(8,128)(2,1)S(1)}, bf16[64,3072]{1,0:T(8,128)(2,1)S(1)}, u32[]{:S(2)}, u32[]{:S(2)}) collective-permute-start(bf16[64,3072]{1,0:T(8,128)(2,1)S(1)} %get-tuple-element.72), channel_id=1, source_target_pairs={{0,32},{32,64},{64,96},{96,0},{1,33},{33,65},{65,97},{97,1},{2,34}... | collective-permute-start | bytes 1179656 | tf_op jit(solution)/shard_map/ppermute | solution.py:53
  349.7 21.5 %all-to-all-start.2 = ((bf16[16,8,3840]{2,1,0:T(8,128)(2,1)}), bf16[16,8,3840]{2,1,0:T(8,128)(2,1)}, u32[]{:S(2)}, u32[]{:S(2)}) async-start(bf16[16,8,3840]{2,1,0:T(8,128)(2,1)} %pad_maximum_fusion.7), calls=%async_computation.2 | async-start | bytes 1966080 | tf_op jit(solution)/shard_map/all_to_all | solution.py:57
  393.7 40.6 %all-to-all-start.3 = ((bf16[64,144,128]{2,1,0:T(8,128)(2,1)}), bf16[64,144,128]{2,1,0:T(8,128)(2,1)S(1)}, u32[]{:S(2)}, u32[]{:S(2)}) async-start(bf16[64,144,128]{2,1,0:T(8,128)(2,1)} %shard_map.89), calls=%async_computation.3 | async-start | bytes 4718592 | tf_op jit(solution)/shard_map/all_to_all | solution.py:57
  (57 other events, 561.9 us)
where the time goes:
time: 439 us; the launch traced here: 436 us
  waiting for transfers between devices  199 us (45%)
  starting transfers between devices  107 us (24%)
  Pallas kernels  63.8 us (15%)
  other arithmetic  26.2 us (6%)
  matrix products  21.1 us (5%)
  local copies, waits for them, and re-layouts  16.3 us (4%)
    ppermute x20, waiting for transfers between devices, swap(): return lax.ppermute(values, axis, [(0, 1), (1, 0)])  76.9 us
    all_to_all x4, waiting for transfers between devices, exchange(): return lax.all_to_all(blocks, axes, split_axis=0, concat_axis=0, tiled=True)  62.9 us
    ppermute x27, waiting for transfers between devices, along_z(): return lax.ppermute(values, 'z', [(i, (i + shift) % 4) for i in range(4)])  59.2 us
    pallas_call x2, Pallas kernels, experts(): pl.pallas_call(lambda *refs: expert_kernel(counts, pieces_out, tall, *ref...  55.2 us
    ppermute x27, starting transfers between devices, along_z(): return lax.ppermute(values, 'z', [(i, (i + shift) % 4) for i in range(4)])  43.3 us
    all_to_all x4, starting transfers between devices, exchange(): return lax.all_to_all(blocks, axes, split_axis=0, concat_axis=0, tiled=True)  36.5 us
    ppermute x20, starting transfers between devices, swap(): return lax.ppermute(values, axis, [(0, 1), (1, 0)])  27.5 us
  transfers between devices with their start and end apart: 51, of which 21 were waited for; matrix products, arithmetic and copies ran while one was open for 8% of the time, Pallas kernels for 13%

commit v1 on v0

--- a/solution.py
+++ b/solution.py
@@ -100,7 +100,7 @@
         copy.wait()
 
 
-def gather_params(attn_param, earlier):
+def gather_params(attn_param, earlier, normed):
     rows, head_dim = attn_param.shape
     half = rows // 2
     piece = half // 2
@@ -110,7 +110,8 @@
     around = [along_z(first, s) for s in (1, 3, 2)]
     own_y = swap(own, "yh")
     pair = after(jnp.concatenate([second, own_y[piece:]], axis=0), around[0], around[1])
-    earlier = after(earlier, own_y, *around)
+    normed = swap(normed, "c")
+    earlier = after(earlier, own_y, normed, *around)
     around_y = [swap(block, "yh") for block in around]
     pairs = [along_z(pair, s) for s in (1, 3, 2)]
     blocks = [own, own_y] + around + around_y + pairs
@@ -135,7 +136,7 @@
     other = swap(own, "c")
     first = jnp.where(core == 0, own, other)
     second = jnp.where(core == 0, other, own)
-    return jnp.stack([first, second], axis=1).reshape(N_DP * rows, head_dim), spread
+    return jnp.stack([first, second], axis=1).reshape(N_DP * rows, head_dim), spread, normed
 
 
 def between_experts(rows):
@@ -155,12 +156,11 @@
     return [own, own_y] + [along_z(one, s) for s in (1, 3, 2)]
 
 
-def spread_far(near, between):
+def spread_far(near):
     own, own_y, near_z, far_z, across = near
     pair = after(jnp.concatenate([own[HALF:], own_y[HALF:]], axis=0), near_z, far_z)
-    first = [swap(near_z, "yh"), swap(far_z, "yh")]
-    second = [along_z(pair, 1), along_z(pair, 3)]
-    return first + [swap(after(across, *between), "yh")] + second + [along_z(pair, 2)]
+    first = [swap(block, "yh") for block in (near_z, far_z, across)]
+    return first + [along_z(pair, s) for s in (1, 3, 2)]
 
 
 def collect(near, far):
@@ -305,13 +305,12 @@
     )(*normed_blocks, *cot_blocks, inner, outer)
 
 
-def param_kernel(scale, head_dim, core_ref, normed_ref, hidden_ref, grads_ref, context_ref, out_ref, terms):
+def param_kernel(scale, head_dim, core_ref, normed_ref, hidden_ref, grads_ref, out_ref, terms):
     features = normed_ref.shape[1]
     tile = 1024
     for block in range(6):
         left_ref = normed_ref if block < 4 else hidden_ref
-        right = (grads_ref[:, block * head_dim : (block + 1) * head_dim] if block < 4
-                 else context_ref[:, (block - 4) * head_dim : (block - 3) * head_dim])
+        right = grads_ref[:, block * head_dim : (block + 1) * head_dim]
         for start in range(0, features, tile):
             part = contract(left_ref[:, start : start + tile], right, 0, 0) * scale
             terms[pl.ds(block * features + start, tile)] = part.astype(BF16)
@@ -323,21 +322,21 @@
         out_ref[group] = terms[pl.ds(pl.multiple_of((2 * group + core) * size, 16), size)]
 
 
-def param_terms(core, normed, hidden, grads, context, scale, head_dim):
+def param_terms(core, normed, hidden, grads, scale, head_dim):
     features = normed.shape[1]
     rows = 6 * features
     whole = pl.BlockSpec(memory_space=pltpu.VMEM)
     return pl.pallas_call(
         lambda *refs: param_kernel(scale, head_dim, *refs),
         out_shape=jax.ShapeDtypeStruct((64, rows // 128, head_dim), BF16),
-        in_specs=[pl.BlockSpec(memory_space=pltpu.SMEM)] + [whole] * 4,
+        in_specs=[pl.BlockSpec(memory_space=pltpu.SMEM)] + [whole] * 3,
         out_specs=whole,
         scratch_shapes=[pltpu.VMEM((rows, head_dim), BF16)],
         compiler_params=pltpu.CompilerParams(vmem_limit_bytes=40 * 1024 * 1024),
         cost_estimate=pl.CostEstimate(
             flops=2 * rows * head_dim * normed.shape[0], bytes_accessed=8 * 1024 * 1024, transcendentals=0
         ),
-    )(core, normed, hidden, grads, context)
+    )(core, normed, hidden, grads)
 
 
 def per_device(tokens, attn_param, expert_ids, gate_score, w_in, w_out, cotangent):
@@ -351,12 +350,12 @@
 
     cot_main, cot_extra = between_experts(contract(slots, cotangent, 1, 0).astype(BF16))
     cot_rows = jnp.concatenate([cot_main, cot_extra], axis=0)
-    packed, cot_near = gather_params(attn_param, cot_rows)
-    cot_far = spread_far(cot_near, ())
-
     normed_one, inverse_one = layer_norm(tokens)
     normed_one_b = normed_one.astype(BF16)
-    normed_both = jnp.concatenate([normed_one_b, swap(normed_one_b, "c")], axis=0)
+    packed, cot_near, normed_other = gather_params(attn_param, cot_rows, normed_one_b)
+    cot_far = spread_far(cot_near)
+
+    normed_both = jnp.concatenate([normed_one_b, normed_other], axis=0)
     blocks = packed.reshape(2 * HEADS + 2, features, head_dim)
     project = blocks[: HEADS + 2]
     out_blocks = blocks[HEADS + 2 :]
@@ -379,15 +378,13 @@
         "hqk,kc->qhc", attention_b, value_rows, preferred_element_type=F32
     ).astype(BF16)
     context_flat = context.reshape(seq_len, HEADS * head_dim)
-    context_both = jnp.concatenate([context_flat, swap(context_flat, "c")], axis=0)
     attn_out = jnp.einsum("thc,hdc->td", context, out_blocks, preferred_element_type=F32)
     residual = (tokens.astype(F32) + attn_out).astype(BF16)
     normed_two, inverse_two = layer_norm(residual)
-    normed_two_b = after(normed_two.astype(BF16), cot_near[4], cot_far[0], cot_far[3], cot_far[4])
+    normed_two_b = after(normed_two.astype(BF16), cot_near[4], cot_far[0], cot_far[1], cot_far[3], cot_far[4])
     main, extra = between_experts(contract(slots, normed_two_b, 1, 0).astype(BF16))
-    own = after(jnp.concatenate([main, extra], axis=0), cot_far[1], cot_far[2], cot_far[5])
-    near = spread_near(own)
-    near[4], normed_both, context_both = lax.optimization_barrier((near[4], normed_both, context_both))
+    near = spread_near(jnp.concatenate([main, extra], axis=0))
+    near[4] = after(near[4], cot_far[2], cot_far[5])
     h = HALF
     whole = EXPERTS * CAP
     rest = whole - h
@@ -399,7 +396,8 @@
         [[(0, whole)], [(whole, h)], [(whole + h, rest)]] + [[(2 * whole + i * h, h)] for i in range(3)],
         2 * whole + 3 * h,
     )
-    far = spread_far(near, (near_rows[0],))
+    far = spread_far(near)
+    far[0] = after(far[0], near_rows[0])
     far_rows = experts(
         far,
         cot_far,
@@ -433,11 +431,11 @@
     grad_query = jnp.einsum("hqk,kc->qhc", grad_scores_b, key_rows, preferred_element_type=F32)
     grad_key = jnp.einsum("hqk,qhc->kc", grad_scores_b, queries, preferred_element_type=F32)
     grad_qkv = jnp.concatenate([grad_query, grad_key[:, None], grad_value[:, None]], axis=1).astype(BF16)
-    grads_flat = grad_qkv.reshape(seq_len, (HEADS + 2) * head_dim)
+    grads_flat = jnp.concatenate([grad_qkv.reshape(seq_len, (HEADS + 2) * head_dim), context_flat], axis=1)
     grads_both = jnp.concatenate([grads_flat, swap(grads_flat, "c")], axis=0)
     core = lax.axis_index("c").astype(jnp.int32).reshape(1)
     terms = param_terms(
-        core, normed_both, hidden_both, grads_both, context_both, (seq_len * devices) ** (-0.5), head_dim
+        core, normed_both, hidden_both, grads_both, (seq_len * devices) ** (-0.5), head_dim
     )
     attn_grad = jnp.sum(exchange(terms, CHIPS).astype(F32), axis=0)
     grad_normed = jnp.einsum("tjc,jdc->td", grad_qkv, project, preferred_element_type=F32)

time: 439 us -> 404 us (0.920)
  waiting for transfers between devices: 199 us -> 178 us
  starting transfers between devices: 107 us -> 93.3 us
    ppermute x20 -> x19, waiting for transfers between devices: 76.9 us -> 51 us  [swap(): return lax.ppermute(values, axis, [(0, 1), (1, 0)])]
    all_to_all x4, starting transfers between devices: 36.5 us -> 20.1 us  [exchange(): return lax.all_to_all(blocks, axes, split_axis=0, concat_axis=0, tiled=True)]
    ppermute x27, waiting for transfers between devices: 59.2 us -> 66.7 us  [along_z(): return lax.ppermute(values, 'z', [(i, (i + shift) % 4) for i in range(4)])]
    ppermute x20 -> x19, starting transfers between devices: 27.5 us -> 29.6 us  [swap(): return lax.ppermute(values, axis, [(0, 1), (1, 0)])]
  transfers between devices with their start and end apart: 51 -> 50, of which waited for: 21 -> 20; matrix products, arithmetic and copies ran while one was open for 8% -> 8% of each run, Pallas kernels for 13% -> 14%
where the time goes in v1:
time: 404 us; the launch traced here: 397 us
  waiting for transfers between devices  178 us (44%)
  starting transfers between devices  93.3 us (23%)
  Pallas kernels  63.6 us (16%)
  other arithmetic  24.4 us (6%)
  matrix products  19.4 us (5%)
  local copies, waits for them, and re-layouts  15.4 us (4%)
    ppermute x27, waiting for transfers between devices, along_z(): return lax.ppermute(values, 'z', [(i, (i + shift) % 4) for i in range(4)])  66.7 us
    all_to_all x4, waiting for transfers between devices, exchange(): return lax.all_to_all(blocks, axes, split_axis=0, concat_axis=0, tiled=True)  60.6 us
    pallas_call x2, Pallas kernels, experts(): pl.pallas_call(lambda *refs: expert_kernel(counts, pieces_out, tall, *ref...  55.1 us
    ppermute x19, waiting for transfers between devices, swap(): return lax.ppermute(values, axis, [(0, 1), (1, 0)])  51 us
    ppermute x27, starting transfers between devices, along_z(): return lax.ppermute(values, 'z', [(i, (i + shift) % 4) for i in range(4)])  43.7 us
    ppermute x19, starting transfers between devices, swap(): return lax.ppermute(values, axis, [(0, 1), (1, 0)])  29.6 us
    all_to_all x4, starting transfers between devices, exchange(): return lax.all_to_all(blocks, axes, split_axis=0, concat_axis=0, tiled=True)  20.1 us
  transfers between devices with their start and end apart: 50, of which 20 were waited for; matrix products, arithmetic and copies ran while one was open for 8% of the time, Pallas kernels for 14%

profile of v1, /device:TPU:0, one launch (start us, length us, event | category | flops | bytes accessed | tf_op | source)
XLA Modules:
  0.0 396.5 jit_solution(12544942202332339107)
XLA Ops:
  5.6 5.5 %all-to-all-start = ((bf16[16,8,3840]{2,1,0:T(8,128)(2,1)}), bf16[16,8,3840]{2,1,0:T(8,128)(2,1)S(1)}, u32[]{:S(2)}, u32[]{:S(2)}) async-start(bf16[16,8,3840]{2,1,0:T(8,128)(2,1)} %pad_maximum_fusion.4), calls=%async_computation | async-start | bytes 1966080 | tf_op jit(solution)/shard_map/all_to_all | solution.py:57
  19.9 2.9 collective-permute-start
  22.8 4.1 %all-to-all-done = bf16[16,8,3840]{2,1,0:T(8,128)(2,1)S(1)} async-done(((bf16[16,8,3840]{2,1,0:T(8,128)(2,1)}), bf16[16,8,3840]{2,1,0:T(8,128)(2,1)S(1)}, u32[]{:S(2)}, u32[]{:S(2)}) %all-to-all-start) | async-done | bytes 983072 | tf_op jit(solution)/shard_map/all_to_all | solution.py:57
  28.9 5.2 %collective-permute-done.refs_2_ = bf16[1152,128]{1,0:T(8,128)(2,1)} collective-permute-done((bf16[1152,128]{1,0:T(8,128)(2,1)}, bf16[1152,128]{1,0:T(8,128)(2,1)}, u32[]{:S(2)}, u32[]{:S(2)}) %collective-permute-start) | collective-permute-done | bytes 294944 | tf_op jit(solution)/shard_map/ppermute | solution.py:49
  43.1 18.5 %collective-permute-done.8.refs_6_ = bf16[576,128]{1,0:T(8,128)(2,1)S(1)} collective-permute-done((bf16[576,128]{1,0:T(8,128)(2,1)}, bf16[576,128]{1,0:T(8,128)(2,1)S(1)}, u32[]{:S(2)}, u32[]{:S(2)}) %collective-permute-start.8) | collective-permute-done | bytes 147488 | tf_op jit(solution)/shard_map/ppermute | solution.py:49
  61.6 4.1 %collective-permute-start.12 = (bf16[1152,128]{1,0:T(8,128)(2,1)}, bf16[1152,128]{1,0:T(8,128)(2,1)}, u32[]{:S(2)}, u32[]{:S(2)}) collective-permute-start(bf16[1152,128]{1,0:T(8,128)(2,1)} %pad_maximum_fusion.12), channel_id=1, source_target_pairs={{0,96},{32,0},{64,32},{96,64},{1,97},{33,1},{65,33},{97,65},{2,98}... | collective-permute-start | bytes 884744 | tf_op jit(solution)/shard_map/ppermute | solution.py:53
  71.0 3.2 collective-permute-done.9.refs_7_
  77.9 3.9 shard_map.86
  87.5 3.7 collective-permute-start.18
  102.0 11.0 %collective-permute-done.17.refs_7_ = bf16[96,3072]{1,0:T(8,128)(2,1)} collective-permute-done((bf16[96,3072]{1,0:T(8,128)(2,1)}, bf16[96,3072]{1,0:T(8,128)(2,1)}, u32[]{:S(2)}, u32[]{:S(2)}) %collective-permute-start.17) | collective-permute-done | bytes 589856 | tf_op jit(solution)/shard_map/ppermute | solution.py:49
  113.0 3.5 collective-permute-done.18.refs_9_
  119.2 3.9 all-to-all-start.1
  124.9 14.0 %all-to-all-done.1 = bf16[16,8,3840]{2,1,0:T(8,128)(2,1)S(1)} async-done(((bf16[16,8,3840]{2,1,0:T(8,128)(2,1)}), bf16[16,8,3840]{2,1,0:T(8,128)(2,1)S(1)}, u32[]{:S(2)}, u32[]{:S(2)}) %all-to-all-start.1) | async-done | bytes 983072 | tf_op jit(solution)/shard_map/all_to_all | solution.py:57
  143.7 3.6 collective-permute-start.25
  152.4 7.4 %collective-permute-done.21.refs_2_ = bf16[96,3072]{1,0:T(8,128)(2,1)S(1)} collective-permute-done((bf16[96,3072]{1,0:T(8,128)(2,1)S(1)}, bf16[96,3072]{1,0:T(8,128)(2,1)S(1)}, u32[]{:S(2)}, u32[]{:S(2)}) %collective-permute-start.21) | collective-permute-done | bytes 589856 | tf_op jit(solution)/shard_map/ppermute | solution.py:53
  161.6 16.8 %collective-permute-done.25.refs_11_ = bf16[128,3072]{1,0:T(8,128)(2,1)S(1)} collective-permute-done((bf16[128,3072]{1,0:T(8,128)(2,1)}, bf16[128,3072]{1,0:T(8,128)(2,1)S(1)}, u32[]{:S(2)}, u32[]{:S(2)}) %collective-permute-start.25) | collective-permute-done | bytes 786464 | tf_op jit(solution)/shard_map/ppermute | solution.py:53
  178.4 11.1 %collective-permute-done.23.refs_4_ = bf16[96,3072]{1,0:T(8,128)(2,1)} collective-permute-done((bf16[96,3072]{1,0:T(8,128)(2,1)S(1)}, bf16[96,3072]{1,0:T(8,128)(2,1)}, u32[]{:S(2)}, u32[]{:S(2)}) %collective-permute-start.23) | collective-permute-done | bytes 589856 | tf_op jit(solution)/shard_map/ppermute | solution.py:53
  194.3 3.2 collective-permute-start.30
  198.3 27.2 %shard_map.87 = (bf16[160,3072]{1,0:T(8,128)(2,1)}, bf16[96,3072]{1,0:T(8,128)(2,1)}, bf16[64,3072]{1,0:T(8,128)(2,1)}, bf16[96,3072]{1,0:T(8,128)(2,1)}, bf16[9...) custom-call(bf16[160,3072]{1,0:T(8,128)(2,1)} %copy-done.13, bf16[160,3072]{1,0:T(8,128)(2,1)} %copy-done.21, ...), custom_call_target="tpu_custom_call" | custom-call | flops 12551454720 | bytes 23592960 | tf_op jit(solution)/shard_map/pallas_call | solution.py:279
  232.3 27.9 %shard_map.88 = (bf16[96,3072]{1,0:T(8,128)(2,1)}, bf16[96,3072]{1,0:T(8,128)(2,1)}, bf16[96,3072]{1,0:T(8,128)(2,1)}, bf16[192,3072]{1,0:T(8,128)(2,1)}, bf16[192,3072]{1,0:T(8,128)(2,1)}) custom-call(bf16[96,3072]{1,0:T(8,128)(2,1)} %copy-done.40, bf16[96,3072]{1,0:T(8,128)(2,1)} %collective-permute-done.27.refs_1_, ...), custom_call_target="tpu_custom_call" | custom-call | flops 13872660480 | bytes 24772608 | tf_op jit(solution)/shard_map/pallas_call | solution.py:279
  261.1 3.0 collective-permute-start.37
  266.4 12.0 %collective-permute-done.38 = bf16[96,3072]{1,0:T(8,128)(2,1)S(1)} collective-permute-done((bf16[96,3072]{1,0:T(8,128)(2,1)}, bf16[96,3072]{1,0:T(8,128)(2,1)S(1)}, u32[]{:S(2)}, u32[]{:S(2)}) %collective-permute-start.38) | collective-permute-done | bytes 589856 | tf_op jit(solution)/shard_map/ppermute | solution.py:53
  278.4 8.7 %collective-permute-done.37 = bf16[96,3072]{1,0:T(8,128)(2,1)S(1)} collective-permute-done((bf16[96,3072]{1,0:T(8,128)(2,1)}, bf16[96,3072]{1,0:T(8,128)(2,1)S(1)}, u32[]{:S(2)}, u32[]{:S(2)}) %collective-permute-start.37) | collective-permute-done | bytes 589856 | tf_op jit(solution)/shard_map/ppermute | solution.py:53
  293.2 2.9 collective-permute-start.41
  296.1 9.0 %collective-permute-done.39 = bf16[96,3072]{1,0:T(8,128)(2,1)S(1)} collective-permute-done((bf16[96,3072]{1,0:T(8,128)(2,1)S(1)}, bf16[96,3072]{1,0:T(8,128)(2,1)S(1)}, u32[]{:S(2)}, u32[]{:S(2)}) %collective-permute-start.39) | collective-permute-done | bytes 589856 | tf_op jit(solution)/shard_map/ppermute | solution.py:49
  307.0 4.3 %collective-permute-done.42 = bf16[64,3072]{1,0:T(8,128)(2,1)S(1)} collective-permute-done((bf16[64,3072]{1,0:T(8,128)(2,1)S(1)}, bf16[64,3072]{1,0:T(8,128)(2,1)S(1)}, u32[]{:S(2)}, u32[]{:S(2)}) %collective-permute-start.42) | collective-permute-done | bytes 393248 | tf_op jit(solution)/shard_map/ppermute | solution.py:53
  314.4 4.2 %all-to-all-start.2 = ((bf16[16,8,3840]{2,1,0:T(8,128)(2,1)}), bf16[16,8,3840]{2,1,0:T(8,128)(2,1)S(1)}, u32[]{:S(2)}, u32[]{:S(2)}) async-start(bf16[16,8,3840]{2,1,0:T(8,128)(2,1)} %pad_maximum_fusion.7), calls=%async_computation.2 | async-start | bytes 1966080 | tf_op jit(solution)/shard_map/all_to_all | solution.py:57
  320.0 14.4 %all-to-all-done.2 = bf16[16,8,3840]{2,1,0:T(8,128)(2,1)S(1)} async-done(((bf16[16,8,3840]{2,1,0:T(8,128)(2,1)}), bf16[16,8,3840]{2,1,0:T(8,128)(2,1)S(1)}, u32[]{:S(2)}, u32[]{:S(2)}) %all-to-all-start.2) | async-done | bytes 983072 | tf_op jit(solution)/shard_map/all_to_all | solution.py:57
  349.3 4.6 %shard_map.89 = bf16[64,144,128]{2,1,0:T(8,128)(2,1)} custom-call(s32[1]{0:T(128)} %bitcast.35.refs_0_, bf16[256,3072]{1,0:T(8,128)(2,1)S(1)} %pad_maximum_fusion.1.refs_1_, bf16[256,3072]{1,0:T(8,128)(2,1)S(1)} %pad_maximum_fusion.2.refs_2_, bf16[256,768]{1,0:T(8,128)(2,1)S(1)} %pad_maximum_fusion.11.refs_3_), custom_call_target="tpu_custom_call" | custom-call | flops 1207959552 | bytes 8388608 | tf_op jit(solution)/shard_map/pallas_call | solution.py:329
  354.0 6.4 %all-to-all-start.3 = ((bf16[64,144,128]{2,1,0:T(8,128)(2,1)}), bf16[64,144,128]{2,1,0:T(8,128)(2,1)}, u32[]{:S(2)}, u32[]{:S(2)}) async-start(bf16[64,144,128]{2,1,0:T(8,128)(2,1)} %shard_map.89), calls=%async_computation.3 | async-start | bytes 4718592 | tf_op jit(solution)/shard_map/all_to_all | solution.py:57
  360.4 3.3 fusion.80
  365.3 28.1 %all-to-all-done.3 = bf16[64,144,128]{2,1,0:T(8,128)(2,1)} async-done(((bf16[64,144,128]{2,1,0:T(8,128)(2,1)}), bf16[64,144,128]{2,1,0:T(8,128)(2,1)}, u32[]{:S(2)}, u32[]{:S(2)}) %all-to-all-start.3) | async-done | bytes 2359328 | tf_op jit(solution)/shard_map/all_to_all | solution.py:57
  (244 shorter events, 113.0 us)
Async XLA Ops:
  5.6 21.3 %all-to-all-start = ((bf16[16,8,3840]{2,1,0:T(8,128)(2,1)}), bf16[16,8,3840]{2,1,0:T(8,128)(2,1)S(1)}, u32[]{:S(2)}, u32[]{:S(2)}) async-start(bf16[16,8,3840]{2,1,0:T(8,128)(2,1)} %pad_maximum_fusion.4), calls=%async_computation | async-start | bytes 1966080 | tf_op jit(solution)/shard_map/all_to_all | solution.py:57
  12.0 22.0 %collective-permute-start.1 = (bf16[128,3072]{1,0:T(8,128)(2,1)S(1)}, bf16[128,3072]{1,0:T(8,128)(2,1)}, u32[]{:S(2)}, u32[]{:S(2)}) collective-permute-start(bf16[128,3072]{1,0:T(8,128)(2,1)S(1)} %fusion.13), channel_id=1, source_target_pairs={{0,1},{1,0},{2,3},{3,2},{4,5},{5,4},{6,7},{7,6},{8,9},{9,8},{10,11... | collective-permute-start | bytes 2359304 | tf_op jit(solution)/shard_map/ppermute | solution.py:49
  34.0 33.6 %collective-permute-start.5 = (bf16[160,3072]{1,0:T(8,128)(2,1)S(1)}, bf16[160,3072]{1,0:T(8,128)(2,1)S(1)}, u32[]{:S(2)}, u32[]{:S(2)}) collective-permute-start(bf16[160,3072]{1,0:T(8,128)(2,1)S(1)} %pad_maximum_fusion.5.refs_5_), channel_id=1, source_target_pairs={{0,16},{16,0},{1,17},{17,1},{2,18},{18,2},{3,19},{19,3},{4,20},{20... | collective-permute-start | bytes 2949128 | tf_op jit(solution)/shard_map/ppermute | solution.py:49
  35.4 30.4 %collective-permute-start.6 = (bf16[96,3072]{1,0:T(8,128)(2,1)S(1)}, bf16[96,3072]{1,0:T(8,128)(2,1)S(1)}, u32[]{:S(2)}, u32[]{:S(2)}) collective-permute-start(bf16[96,3072]{1,0:T(8,128)(2,1)S(1)} %slice.105), channel_id=1, source_target_pairs={{0,32},{32,64},{64,96},{96,0},{1,33},{33,65},{65,97},{97,1},{2,34}... | collective-permute-start | bytes 1769480 | tf_op jit(solution)/shard_map/ppermute | solution.py:53
  37.4 28.6 %collective-permute-start.7 = (bf16[96,3072]{1,0:T(8,128)(2,1)S(1)}, bf16[96,3072]{1,0:T(8,128)(2,1)S(1)}, u32[]{:S(2)}, u32[]{:S(2)}) collective-permute-start(bf16[96,3072]{1,0:T(8,128)(2,1)S(1)} %slice.105), channel_id=1, source_target_pairs={{0,96},{32,0},{64,32},{96,64},{1,97},{33,1},{65,33},{97,65},{2,98}... | collective-permute-start | bytes 1769480 | tf_op jit(solution)/shard_map/ppermute | solution.py:53
  38.7 22.9 %collective-permute-start.8 = (bf16[576,128]{1,0:T(8,128)(2,1)}, bf16[576,128]{1,0:T(8,128)(2,1)S(1)}, u32[]{:S(2)}, u32[]{:S(2)}) collective-permute-start(bf16[576,128]{1,0:T(8,128)(2,1)} %collective-permute-done.2.refs_3_), channel_id=1, source_target_pairs={{0,16},{16,0},{1,17},{17,1},{2,18},{18,2},{3,19},{19,3},{4,20},{20... | collective-permute-start | bytes 442376 | tf_op jit(solution)/shard_map/ppermute | solution.py:49
  43.0 33.0 %collective-permute-start.11 = (bf16[1152,128]{1,0:T(8,128)(2,1)}, bf16[1152,128]{1,0:T(8,128)(2,1)}, u32[]{:S(2)}, u32[]{:S(2)}) collective-permute-start(bf16[1152,128]{1,0:T(8,128)(2,1)} %pad_maximum_fusion.12), channel_id=1, source_target_pairs={{0,32},{32,64},{64,96},{96,0},{1,33},{33,65},{65,97},{97,1},{2,34}... | collective-permute-start | bytes 884744 | tf_op jit(solution)/shard_map/ppermute | solution.py:53
  82.0 20.0 %collective-permute-start.15 = (bf16[96,3072]{1,0:T(8,128)(2,1)}, bf16[96,3072]{1,0:T(8,128)(2,1)}, u32[]{:S(2)}, u32[]{:S(2)}) collective-permute-start(bf16[96,3072]{1,0:T(8,128)(2,1)} %copy-done.16), channel_id=1, source_target_pairs={{0,64},{32,96},{64,0},{96,32},{1,65},{33,97},{65,1},{97,33},{2,66}... | collective-permute-start | bytes 1769480 | tf_op jit(solution)/shard_map/ppermute | solution.py:53
  85.1 27.9 %collective-permute-start.17 = (bf16[96,3072]{1,0:T(8,128)(2,1)}, bf16[96,3072]{1,0:T(8,128)(2,1)}, u32[]{:S(2)}, u32[]{:S(2)}) collective-permute-start(bf16[96,3072]{1,0:T(8,128)(2,1)} %copy-done.39), channel_id=1, source_target_pairs={{0,16},{16,0},{1,17},{17,1},{2,18},{18,2},{3,19},{19,3},{4,20},{20... | collective-permute-start | bytes 1769480 | tf_op jit(solution)/shard_map/ppermute | solution.py:49
  87.5 28.9 %collective-permute-start.18 = (bf16[128,3072]{1,0:T(8,128)(2,1)}, bf16[128,3072]{1,0:T(8,128)(2,1)}, u32[]{:S(2)}, u32[]{:S(2)}) collective-permute-start(bf16[128,3072]{1,0:T(8,128)(2,1)} %pad_maximum_fusion.9), channel_id=1, source_target_pairs={{0,32},{32,64},{64,96},{96,0},{1,33},{33,65},{65,97},{97,1},{2,34}... | collective-permute-start | bytes 2359304 | tf_op jit(solution)/shard_map/ppermute | solution.py:53
  91.2 26.3 %collective-permute-start.19 = (bf16[128,3072]{1,0:T(8,128)(2,1)}, bf16[128,3072]{1,0:T(8,128)(2,1)}, u32[]{:S(2)}, u32[]{:S(2)}) collective-permute-start(bf16[128,3072]{1,0:T(8,128)(2,1)} %pad_maximum_fusion.9), channel_id=1, source_target_pairs={{0,96},{32,0},{64,32},{96,64},{1,97},{33,1},{65,33},{97,65},{2,98}... | collective-permute-start | bytes 2359304 | tf_op jit(solution)/shard_map/ppermute | solution.py:53
  119.2 19.7 %all-to-all-start.1 = ((bf16[16,8,3840]{2,1,0:T(8,128)(2,1)}), bf16[16,8,3840]{2,1,0:T(8,128)(2,1)S(1)}, u32[]{:S(2)}, u32[]{:S(2)}) async-start(bf16[16,8,3840]{2,1,0:T(8,128)(2,1)} %pad_maximum_fusion.6), calls=%async_computation.1 | async-start | bytes 1966080 | tf_op jit(solution)/shard_map/all_to_all | solution.py:57
  123.1 26.7 %collective-permute-start.24 = (bf16[96,3072]{1,0:T(8,128)(2,1)}, bf16[96,3072]{1,0:T(8,128)(2,1)}, u32[]{:S(2)}, u32[]{:S(2)}) collective-permute-start(bf16[96,3072]{1,0:T(8,128)(2,1)} %collective-permute-done.15.refs_9_), channel_id=1, source_target_pairs={{0,16},{16,0},{1,17},{17,1},{2,18},{18,2},{3,19},{19,3},{4,20},{20... | collective-permute-start | bytes 1769480 | tf_op jit(solution)/shard_map/ppermute | solution.py:49
  141.3 51.7 %collective-permute-start.20 = (bf16[160,3072]{1,0:T(8,128)(2,1)S(1)}, bf16[160,3072]{1,0:T(8,128)(2,1)S(1)}, u32[]{:S(2)}, u32[]{:S(2)}) collective-permute-start(bf16[160,3072]{1,0:T(8,128)(2,1)S(1)} %pad_maximum_fusion.3.refs_0_), channel_id=1, source_target_pairs={{0,16},{16,0},{1,17},{17,1},{2,18},{18,2},{3,19},{19,3},{4,20},{20... | collective-permute-start | bytes 2949128 | tf_op jit(solution)/shard_map/ppermute | solution.py:49
  143.7 34.7 %collective-permute-start.25 = (bf16[128,3072]{1,0:T(8,128)(2,1)}, bf16[128,3072]{1,0:T(8,128)(2,1)S(1)}, u32[]{:S(2)}, u32[]{:S(2)}) collective-permute-start(bf16[128,3072]{1,0:T(8,128)(2,1)} %pad_maximum_fusion.9), channel_id=1, source_target_pairs={{0,64},{32,96},{64,0},{96,32},{1,65},{33,97},{65,1},{97,33},{2,66}... | collective-permute-start | bytes 2359304 | tf_op jit(solution)/shard_map/ppermute | solution.py:53
  147.3 42.2 %collective-permute-start.23 = (bf16[96,3072]{1,0:T(8,128)(2,1)S(1)}, bf16[96,3072]{1,0:T(8,128)(2,1)}, u32[]{:S(2)}, u32[]{:S(2)}) collective-permute-start(bf16[96,3072]{1,0:T(8,128)(2,1)S(1)} %slice.149), channel_id=1, source_target_pairs={{0,64},{32,96},{64,0},{96,32},{1,65},{33,97},{65,1},{97,33},{2,66}... | collective-permute-start | bytes 1769480 | tf_op jit(solution)/shard_map/ppermute | solution.py:53
  149.8 41.5 %collective-permute-start.22 = (bf16[96,3072]{1,0:T(8,128)(2,1)S(1)}, bf16[96,3072]{1,0:T(8,128)(2,1)}, u32[]{:S(2)}, u32[]{:S(2)}) collective-permute-start(bf16[96,3072]{1,0:T(8,128)(2,1)S(1)} %slice.149), channel_id=1, source_target_pairs={{0,96},{32,0},{64,32},{96,64},{1,97},{33,1},{65,33},{97,65},{2,98}... | collective-permute-start | bytes 1769480 | tf_op jit(solution)/shard_map/ppermute | solution.py:53
  159.8 37.6 %collective-permute-start.26 = (bf16[96,3072]{1,0:T(8,128)(2,1)S(1)}, bf16[96,3072]{1,0:T(8,128)(2,1)S(1)}, u32[]{:S(2)}, u32[]{:S(2)}) collective-permute-start(bf16[96,3072]{1,0:T(8,128)(2,1)S(1)} %collective-permute-done.21.refs_2_), channel_id=1, source_target_pairs={{0,16},{16,0},{1,17},{17,1},{2,18},{18,2},{3,19},{19,3},{4,20},{20... | collective-permute-start | bytes 1769480 | tf_op jit(solution)/shard_map/ppermute | solution.py:49
  189.5 37.0 %collective-permute-start.28 = (bf16[96,3072]{1,0:T(8,128)(2,1)}, bf16[96,3072]{1,0:T(8,128)(2,1)}, u32[]{:S(2)}, u32[]{:S(2)}) collective-permute-start(bf16[96,3072]{1,0:T(8,128)(2,1)} %collective-permute-done.23.refs_4_), channel_id=1, source_target_pairs={{0,16},{16,0},{1,17},{17,1},{2,18},{18,2},{3,19},{19,3},{4,20},{20... | collective-permute-start | bytes 1769480 | tf_op jit(solution)/shard_map/ppermute | solution.py:49
  191.3 34.1 %collective-permute-start.27 = (bf16[96,3072]{1,0:T(8,128)(2,1)}, bf16[96,3072]{1,0:T(8,128)(2,1)}, u32[]{:S(2)}, u32[]{:S(2)}) collective-permute-start(bf16[96,3072]{1,0:T(8,128)(2,1)} %collective-permute-done.22.refs_3_), channel_id=1, source_target_pairs={{0,16},{16,0},{1,17},{17,1},{2,18},{18,2},{3,19},{19,3},{4,20},{20... | collective-permute-start | bytes 1769480 | tf_op jit(solution)/shard_map/ppermute | solution.py:49
  194.2 33.4 %collective-permute-start.29 = (bf16[128,3072]{1,0:T(8,128)(2,1)S(1)}, bf16[128,3072]{1,0:T(8,128)(2,1)}, u32[]{:S(2)}, u32[]{:S(2)}) collective-permute-start(bf16[128,3072]{1,0:T(8,128)(2,1)S(1)} %pad_maximum_fusion.10), channel_id=1, source_target_pairs={{0,32},{32,64},{64,96},{96,0},{1,33},{33,65},{65,97},{97,1},{2,34}... | collective-permute-start | bytes 2359304 | tf_op jit(solution)/shard_map/ppermute | solution.py:53
  194.3 36.2 %collective-permute-start.30 = (bf16[128,3072]{1,0:T(8,128)(2,1)S(1)}, bf16[128,3072]{1,0:T(8,128)(2,1)}, u32[]{:S(2)}, u32[]{:S(2)}) collective-permute-start(bf16[128,3072]{1,0:T(8,128)(2,1)S(1)} %pad_maximum_fusion.10), channel_id=1, source_target_pairs={{0,96},{32,0},{64,32},{96,64},{1,97},{33,1},{65,33},{97,65},{2,98}... | collective-permute-start | bytes 2359304 | tf_op jit(solution)/shard_map/ppermute | solution.py:53
  197.5 34.8 %collective-permute-start.31 = (bf16[128,3072]{1,0:T(8,128)(2,1)S(1)}, bf16[128,3072]{1,0:T(8,128)(2,1)}, u32[]{:S(2)}, u32[]{:S(2)}) collective-permute-start(bf16[128,3072]{1,0:T(8,128)(2,1)S(1)} %pad_maximum_fusion.10), channel_id=1, source_target_pairs={{0,64},{32,96},{64,0},{96,32},{1,65},{33,97},{65,1},{97,33},{2,66}... | collective-permute-start | bytes 2359304 | tf_op jit(solution)/shard_map/ppermute | solution.py:53
  225.5 34.8 %collective-permute-start.32 = (bf16[96,3072]{1,0:T(8,128)(2,1)}, bf16[96,3072]{1,0:T(8,128)(2,1)}, u32[]{:S(2)}, u32[]{:S(2)}) collective-permute-start(bf16[96,3072]{1,0:T(8,128)(2,1)} %get-tuple-element.43), channel_id=1, source_target_pairs={{0,96},{32,0},{64,32},{96,64},{1,97},{33,1},{65,33},{97,65},{2,98}... | collective-permute-start | bytes 1769480 | tf_op jit(solution)/shard_map/ppermute | solution.py:53
  226.4 33.9 %collective-permute-start.33 = (bf16[96,3072]{1,0:T(8,128)(2,1)}, bf16[96,3072]{1,0:T(8,128)(2,1)}, u32[]{:S(2)}, u32[]{:S(2)}) collective-permute-start(bf16[96,3072]{1,0:T(8,128)(2,1)} %get-tuple-element.44), channel_id=1, source_target_pairs={{0,32},{32,64},{64,96},{96,0},{1,33},{33,65},{65,97},{97,1},{2,34}... | collective-permute-start | bytes 1769480 | tf_op jit(solution)/shard_map/ppermute | solution.py:53
  227.6 32.8 %collective-permute-start.34 = (bf16[96,3072]{1,0:T(8,128)(2,1)}, bf16[96,3072]{1,0:T(8,128)(2,1)}, u32[]{:S(2)}, u32[]{:S(2)}) collective-permute-start(bf16[96,3072]{1,0:T(8,128)(2,1)} %get-tuple-element.45), channel_id=1, source_target_pairs={{0,64},{32,96},{64,0},{96,32},{1,65},{33,97},{65,1},{97,33},{2,66}... | collective-permute-start | bytes 1769480 | tf_op jit(solution)/shard_map/ppermute | solution.py:53
  230.4 29.8 %collective-permute-start.35 = (bf16[64,3072]{1,0:T(8,128)(2,1)}, bf16[64,3072]{1,0:T(8,128)(2,1)S(1)}, u32[]{:S(2)}, u32[]{:S(2)}) collective-permute-start(bf16[64,3072]{1,0:T(8,128)(2,1)} %get-tuple-element.46), channel_id=1, source_target_pairs={{0,16},{16,0},{1,17},{17,1},{2,18},{18,2},{3,19},{19,3},{4,20},{20... | collective-permute-start | bytes 1179656 | tf_op jit(solution)/shard_map/ppermute | solution.py:49
  261.1 26.0 %collective-permute-start.37 = (bf16[96,3072]{1,0:T(8,128)(2,1)}, bf16[96,3072]{1,0:T(8,128)(2,1)S(1)}, u32[]{:S(2)}, u32[]{:S(2)}) collective-permute-start(bf16[96,3072]{1,0:T(8,128)(2,1)} %get-tuple-element.48), channel_id=1, source_target_pairs={{0,32},{32,64},{64,96},{96,0},{1,33},{33,65},{65,97},{97,1},{2,34}... | collective-permute-start | bytes 1769480 | tf_op jit(solution)/shard_map/ppermute | solution.py:53
  264.1 23.0 %collective-permute-start.36 = (bf16[96,3072]{1,0:T(8,128)(2,1)}, bf16[96,3072]{1,0:T(8,128)(2,1)S(1)}, u32[]{:S(2)}, u32[]{:S(2)}) collective-permute-start(bf16[96,3072]{1,0:T(8,128)(2,1)} %get-tuple-element.47), channel_id=1, source_target_pairs={{0,96},{32,0},{64,32},{96,64},{1,97},{33,1},{65,33},{97,65},{2,98}... | collective-permute-start | bytes 1769480 | tf_op jit(solution)/shard_map/ppermute | solution.py:53
  264.6 25.7 %collective-permute-start.40 = (bf16[192,3072]{1,0:T(8,128)(2,1)}, bf16[192,3072]{1,0:T(8,128)(2,1)S(1)}, u32[]{:S(2)}, u32[]{:S(2)}) collective-permute-start(bf16[192,3072]{1,0:T(8,128)(2,1)} %get-tuple-element.55), channel_id=1, source_target_pairs={{0,16},{16,0},{1,17},{17,1},{2,18},{18,2},{3,19},{19,3},{4,20},{20... | collective-permute-start | bytes 3538952 | tf_op jit(solution)/shard_map/ppermute | solution.py:49
  314.4 20.0 %all-to-all-start.2 = ((bf16[16,8,3840]{2,1,0:T(8,128)(2,1)}), bf16[16,8,3840]{2,1,0:T(8,128)(2,1)S(1)}, u32[]{:S(2)}, u32[]{:S(2)}) async-start(bf16[16,8,3840]{2,1,0:T(8,128)(2,1)} %pad_maximum_fusion.7), calls=%async_computation.2 | async-start | bytes 1966080 | tf_op jit(solution)/shard_map/all_to_all | solution.py:57
  354.0 39.5 %all-to-all-start.3 = ((bf16[64,144,128]{2,1,0:T(8,128)(2,1)}), bf16[64,144,128]{2,1,0:T(8,128)(2,1)}, u32[]{:S(2)}, u32[]{:S(2)}) async-start(bf16[64,144,128]{2,1,0:T(8,128)(2,1)} %shard_map.89), calls=%async_computation.3 | async-start | bytes 4718592 | tf_op jit(solution)/shard_map/all_to_all | solution.py:57
  (63 other events, 741.5 us)

commit v2 on v1

--- a/solution.py
+++ b/solution.py
@@ -123,7 +123,7 @@
     )
     spread = spread_near(earlier)
     at = jnp.stack([lax.axis_index("z"), lax.axis_index("yh")]).astype(jnp.int32)
-    at = after(at, *spread[1:4])
+    at = after(at, *spread[2:4])
     anywhere = pl.BlockSpec(memory_space=pl.ANY)
     own = pl.pallas_call(
         lambda *refs: place_kernel(places, piece, *refs),
@@ -381,10 +381,9 @@
     attn_out = jnp.einsum("thc,hdc->td", context, out_blocks, preferred_element_type=F32)
     residual = (tokens.astype(F32) + attn_out).astype(BF16)
     normed_two, inverse_two = layer_norm(residual)
-    normed_two_b = after(normed_two.astype(BF16), cot_near[4], cot_far[0], cot_far[1], cot_far[3], cot_far[4])
+    normed_two_b = after(normed_two.astype(BF16), cot_near[4], cot_far[0], cot_far[3], cot_far[4])
     main, extra = between_experts(contract(slots, normed_two_b, 1, 0).astype(BF16))
-    near = spread_near(jnp.concatenate([main, extra], axis=0))
-    near[4] = after(near[4], cot_far[2], cot_far[5])
+    near = spread_near(after(jnp.concatenate([main, extra], axis=0), cot_far[1], cot_far[2], cot_far[5]))
     h = HALF
     whole = EXPERTS * CAP
     rest = whole - h

time: 404 us -> 410 us (1.015)
    ppermute x19, waiting for transfers between devices: 51 us -> 63.9 us  [swap(): return lax.ppermute(values, axis, [(0, 1), (1, 0)])]
    ppermute x27, waiting for transfers between devices: 66.7 us -> 61.9 us  [along_z(): return lax.ppermute(values, 'z', [(i, (i + shift) % 4) for i in range(4)])]
    all_to_all x4, waiting for transfers between devices: 60.6 us -> 56 us  [exchange(): return lax.all_to_all(blocks, axes, split_axis=0, concat_axis=0, tiled=True)]
  transfers between devices with their start and end apart: 50 -> 50, of which waited for: 20 -> 25; matrix products, arithmetic and copies ran while one was open for 8% -> 8% of each run, Pallas kernels for 14% -> 14%
where the time goes in v2:
time: 410 us; the launch traced here: 403 us
  waiting for transfers between devices  182 us (44%)
  starting transfers between devices  95.9 us (23%)
  Pallas kernels  63.8 us (16%)
  other arithmetic  25.5 us (6%)
  matrix products  19.4 us (5%)
  local copies, waits for them, and re-layouts  14.5 us (4%)
    ppermute x19, waiting for transfers between devices, swap(): return lax.ppermute(values, axis, [(0, 1), (1, 0)])  63.9 us
    ppermute x27, waiting for transfers between devices, along_z(): return lax.ppermute(values, 'z', [(i, (i + shift) % 4) for i in range(4)])  61.9 us
    all_to_all x4, waiting for transfers between devices, exchange(): return lax.all_to_all(blocks, axes, split_axis=0, concat_axis=0, tiled=True)  56 us
    pallas_call x2, Pallas kernels, experts(): pl.pallas_call(lambda *refs: expert_kernel(counts, pieces_out, tall, *ref...  55.1 us
    ppermute x27, starting transfers between devices, along_z(): return lax.ppermute(values, 'z', [(i, (i + shift) % 4) for i in range(4)])  46.3 us
    ppermute x19, starting transfers between devices, swap(): return lax.ppermute(values, axis, [(0, 1), (1, 0)])  28.4 us
    all_to_all x4, starting transfers between devices, exchange(): return lax.all_to_all(blocks, axes, split_axis=0, concat_axis=0, tiled=True)  21.2 us
  transfers between devices with their start and end apart: 50, of which 25 were waited for; matrix products, arithmetic and copies ran while one was open for 8% of the time, Pallas kernels for 14%

profile of v2, /device:TPU:0, one launch (start us, length us, event | category | flops | bytes accessed | tf_op | source)
XLA Modules:
  0.0 402.9 jit_solution(17922882999851283291)
XLA Ops:
  5.5 5.5 %all-to-all-start = ((bf16[16,8,3840]{2,1,0:T(8,128)(2,1)}), bf16[16,8,3840]{2,1,0:T(8,128)(2,1)S(1)}, u32[]{:S(2)}, u32[]{:S(2)}) async-start(bf16[16,8,3840]{2,1,0:T(8,128)(2,1)} %pad_maximum_fusion.3), calls=%async_computation | async-start | bytes 1966080 | tf_op jit(solution)/shard_map/all_to_all | solution.py:57
  19.8 2.9 collective-permute-start
  22.7 4.1 %all-to-all-done = bf16[16,8,3840]{2,1,0:T(8,128)(2,1)S(1)} async-done(((bf16[16,8,3840]{2,1,0:T(8,128)(2,1)}), bf16[16,8,3840]{2,1,0:T(8,128)(2,1)S(1)}, u32[]{:S(2)}, u32[]{:S(2)}) %all-to-all-start) | async-done | bytes 983072 | tf_op jit(solution)/shard_map/all_to_all | solution.py:57
  28.8 5.2 %collective-permute-done.refs_2_ = bf16[1152,128]{1,0:T(8,128)(2,1)} collective-permute-done((bf16[1152,128]{1,0:T(8,128)(2,1)}, bf16[1152,128]{1,0:T(8,128)(2,1)}, u32[]{:S(2)}, u32[]{:S(2)}) %collective-permute-start) | collective-permute-done | bytes 294944 | tf_op jit(solution)/shard_map/ppermute | solution.py:49
  47.3 5.5 %collective-permute-done.5.refs_7_ = bf16[96,3072]{1,0:T(8,128)(2,1)} collective-permute-done((bf16[96,3072]{1,0:T(8,128)(2,1)}, bf16[96,3072]{1,0:T(8,128)(2,1)}, u32[]{:S(2)}, u32[]{:S(2)}) %collective-permute-start.5) | collective-permute-done | bytes 589856 | tf_op jit(solution)/shard_map/ppermute | solution.py:53
  57.0 3.5 collective-permute-done.8.refs_7_
  65.9 4.0 shard_map.86
  72.0 3.1 collective-permute-start.15
  75.2 21.1 %collective-permute-done.16.refs_6_ = bf16[160,3072]{1,0:T(8,128)(2,1)} collective-permute-done((bf16[160,3072]{1,0:T(8,128)(2,1)S(1)}, bf16[160,3072]{1,0:T(8,128)(2,1)}, u32[]{:S(2)}, u32[]{:S(2)}) %collective-permute-start.16) | collective-permute-done | bytes 983072 | tf_op jit(solution)/shard_map/ppermute | solution.py:49
  112.2 6.1 %collective-permute-done.17.refs_9_ = bf16[128,3072]{1,0:T(8,128)(2,1)} collective-permute-done((bf16[128,3072]{1,0:T(8,128)(2,1)}, bf16[128,3072]{1,0:T(8,128)(2,1)}, u32[]{:S(2)}, u32[]{:S(2)}) %collective-permute-start.17) | collective-permute-done | bytes 786464 | tf_op jit(solution)/shard_map/ppermute | solution.py:53
  120.1 3.7 all-to-all-start.1
  123.9 2.8 collective-permute-start.21
  130.2 9.5 %all-to-all-done.1 = bf16[16,8,3840]{2,1,0:T(8,128)(2,1)S(1)} async-done(((bf16[16,8,3840]{2,1,0:T(8,128)(2,1)}), bf16[16,8,3840]{2,1,0:T(8,128)(2,1)S(1)}, u32[]{:S(2)}, u32[]{:S(2)}) %all-to-all-start.1) | async-done | bytes 983072 | tf_op jit(solution)/shard_map/all_to_all | solution.py:57
  142.0 9.5 %collective-permute-done.19.refs_7_ = bf16[96,3072]{1,0:T(8,128)(2,1)} collective-permute-done((bf16[96,3072]{1,0:T(8,128)(2,1)}, bf16[96,3072]{1,0:T(8,128)(2,1)}, u32[]{:S(2)}, u32[]{:S(2)}) %collective-permute-start.19) | collective-permute-done | bytes 589856 | tf_op jit(solution)/shard_map/ppermute | solution.py:49
  151.5 12.4 %collective-permute-done.20.refs_8_ = bf16[96,3072]{1,0:T(8,128)(2,1)} collective-permute-done((bf16[96,3072]{1,0:T(8,128)(2,1)}, bf16[96,3072]{1,0:T(8,128)(2,1)}, u32[]{:S(2)}, u32[]{:S(2)}) %collective-permute-start.20) | collective-permute-done | bytes 589856 | tf_op jit(solution)/shard_map/ppermute | solution.py:49
  169.7 13.1 %collective-permute-done.23.refs_2_ = bf16[96,3072]{1,0:T(8,128)(2,1)S(1)} collective-permute-done((bf16[96,3072]{1,0:T(8,128)(2,1)S(1)}, bf16[96,3072]{1,0:T(8,128)(2,1)S(1)}, u32[]{:S(2)}, u32[]{:S(2)}) %collective-permute-start.23) | collective-permute-done | bytes 589856 | tf_op jit(solution)/shard_map/ppermute | solution.py:53
  184.5 9.4 %collective-permute-done.24.refs_3_ = bf16[96,3072]{1,0:T(8,128)(2,1)} collective-permute-done((bf16[96,3072]{1,0:T(8,128)(2,1)S(1)}, bf16[96,3072]{1,0:T(8,128)(2,1)}, u32[]{:S(2)}, u32[]{:S(2)}) %collective-permute-start.24) | collective-permute-done | bytes 589856 | tf_op jit(solution)/shard_map/ppermute | solution.py:53
  199.4 3.1 collective-permute-start.30
  204.7 27.1 %shard_map.87 = (bf16[160,3072]{1,0:T(8,128)(2,1)}, bf16[96,3072]{1,0:T(8,128)(2,1)}, bf16[64,3072]{1,0:T(8,128)(2,1)}, bf16[96,3072]{1,0:T(8,128)(2,1)}, bf16[9...) custom-call(bf16[160,3072]{1,0:T(8,128)(2,1)} %copy-done.4, bf16[160,3072]{1,0:T(8,128)(2,1)} %copy-done.19, ...), custom_call_target="tpu_custom_call" | custom-call | flops 12551454720 | bytes 23592960 | tf_op jit(solution)/shard_map/pallas_call | solution.py:279
  237.4 28.0 %shard_map.88 = (bf16[96,3072]{1,0:T(8,128)(2,1)}, bf16[96,3072]{1,0:T(8,128)(2,1)}, bf16[96,3072]{1,0:T(8,128)(2,1)}, bf16[192,3072]{1,0:T(8,128)(2,1)}, bf16[192,3072]{1,0:T(8,128)(2,1)}) custom-call(bf16[96,3072]{1,0:T(8,128)(2,1)} %copy-done.35, bf16[96,3072]{1,0:T(8,128)(2,1)} %collective-permute-done.27.refs_1_, ...), custom_call_target="tpu_custom_call" | custom-call | flops 13872660480 | bytes 24772608 | tf_op jit(solution)/shard_map/pallas_call | solution.py:279
  272.8 10.8 %collective-permute-done.38 = bf16[96,3072]{1,0:T(8,128)(2,1)S(1)} collective-permute-done((bf16[96,3072]{1,0:T(8,128)(2,1)}, bf16[96,3072]{1,0:T(8,128)(2,1)S(1)}, u32[]{:S(2)}, u32[]{:S(2)}) %collective-permute-start.38) | collective-permute-done | bytes 589856 | tf_op jit(solution)/shard_map/ppermute | solution.py:53
  283.6 8.3 %collective-permute-done.37 = bf16[96,3072]{1,0:T(8,128)(2,1)S(1)} collective-permute-done((bf16[96,3072]{1,0:T(8,128)(2,1)}, bf16[96,3072]{1,0:T(8,128)(2,1)S(1)}, u32[]{:S(2)}, u32[]{:S(2)}) %collective-permute-start.37) | collective-permute-done | bytes 589856 | tf_op jit(solution)/shard_map/ppermute | solution.py:53
  299.3 2.8 collective-permute-start.41
  302.0 8.1 %collective-permute-done.39 = bf16[96,3072]{1,0:T(8,128)(2,1)S(1)} collective-permute-done((bf16[96,3072]{1,0:T(8,128)(2,1)S(1)}, bf16[96,3072]{1,0:T(8,128)(2,1)S(1)}, u32[]{:S(2)}, u32[]{:S(2)}) %collective-permute-start.39) | collective-permute-done | bytes 589856 | tf_op jit(solution)/shard_map/ppermute | solution.py:49
  312.0 4.4 %collective-permute-done.42 = bf16[64,3072]{1,0:T(8,128)(2,1)S(1)} collective-permute-done((bf16[64,3072]{1,0:T(8,128)(2,1)S(1)}, bf16[64,3072]{1,0:T(8,128)(2,1)S(1)}, u32[]{:S(2)}, u32[]{:S(2)}) %collective-permute-start.42) | collective-permute-done | bytes 393248 | tf_op jit(solution)/shard_map/ppermute | solution.py:53
  319.5 5.3 %all-to-all-start.2 = ((bf16[16,8,3840]{2,1,0:T(8,128)(2,1)}), bf16[16,8,3840]{2,1,0:T(8,128)(2,1)S(1)}, u32[]{:S(2)}, u32[]{:S(2)}) async-start(bf16[16,8,3840]{2,1,0:T(8,128)(2,1)} %pad_maximum_fusion.7), calls=%async_computation.2 | async-start | bytes 1966080 | tf_op jit(solution)/shard_map/all_to_all | solution.py:57
  326.2 14.4 %all-to-all-done.2 = bf16[16,8,3840]{2,1,0:T(8,128)(2,1)S(1)} async-done(((bf16[16,8,3840]{2,1,0:T(8,128)(2,1)}), bf16[16,8,3840]{2,1,0:T(8,128)(2,1)S(1)}, u32[]{:S(2)}, u32[]{:S(2)}) %all-to-all-start.2) | async-done | bytes 983072 | tf_op jit(solution)/shard_map/all_to_all | solution.py:57
  355.5 4.6 %shard_map.89 = bf16[64,144,128]{2,1,0:T(8,128)(2,1)} custom-call(s32[1]{0:T(128)} %bitcast.35.refs_0_, bf16[256,3072]{1,0:T(8,128)(2,1)S(1)} %pad_maximum_fusion.1.refs_1_, bf16[256,3072]{1,0:T(8,128)(2,1)S(1)} %pad_maximum_fusion.2.refs_2_, bf16[256,768]{1,0:T(8,128)(2,1)S(1)} %pad_maximum_fusion.11.refs_3_), custom_call_target="tpu_custom_call" | custom-call | flops 1207959552 | bytes 8388608 | tf_op jit(solution)/shard_map/pallas_call | solution.py:329
  360.2 6.6 %all-to-all-start.3 = ((bf16[64,144,128]{2,1,0:T(8,128)(2,1)}), bf16[64,144,128]{2,1,0:T(8,128)(2,1)}, u32[]{:S(2)}, u32[]{:S(2)}) async-start(bf16[64,144,128]{2,1,0:T(8,128)(2,1)} %shard_map.89), calls=%async_computation.3 | async-start | bytes 4718592 | tf_op jit(solution)/shard_map/all_to_all | solution.py:57
  366.8 3.3 fusion.79
  371.7 28.1 %all-to-all-done.3 = bf16[64,144,128]{2,1,0:T(8,128)(2,1)} async-done(((bf16[64,144,128]{2,1,0:T(8,128)(2,1)}), bf16[64,144,128]{2,1,0:T(8,128)(2,1)}, u32[]{:S(2)}, u32[]{:S(2)}) %all-to-all-start.3) | async-done | bytes 2359328 | tf_op jit(solution)/shard_map/all_to_all | solution.py:57
  399.8 2.6 convert_reduce_fusion
  (233 shorter events, 121.8 us)
Async XLA Ops:
  5.5 21.3 %all-to-all-start = ((bf16[16,8,3840]{2,1,0:T(8,128)(2,1)}), bf16[16,8,3840]{2,1,0:T(8,128)(2,1)S(1)}, u32[]{:S(2)}, u32[]{:S(2)}) async-start(bf16[16,8,3840]{2,1,0:T(8,128)(2,1)} %pad_maximum_fusion.3), calls=%async_computation | async-start | bytes 1966080 | tf_op jit(solution)/shard_map/all_to_all | solution.py:57
  11.9 22.1 %collective-permute-start.1 = (bf16[128,3072]{1,0:T(8,128)(2,1)S(1)}, bf16[128,3072]{1,0:T(8,128)(2,1)}, u32[]{:S(2)}, u32[]{:S(2)}) collective-permute-start(bf16[128,3072]{1,0:T(8,128)(2,1)S(1)} %fusion.13), channel_id=1, source_target_pairs={{0,1},{1,0},{2,3},{3,2},{4,5},{5,4},{6,7},{7,6},{8,9},{9,8},{10,11... | collective-permute-start | bytes 2359304 | tf_op jit(solution)/shard_map/ppermute | solution.py:49
  41.1 21.1 %collective-permute-start.10 = (bf16[1152,128]{1,0:T(8,128)(2,1)}, bf16[1152,128]{1,0:T(8,128)(2,1)S(1)}, u32[]{:S(2)}, u32[]{:S(2)}) collective-permute-start(bf16[1152,128]{1,0:T(8,128)(2,1)} %pad_maximum_fusion.12), channel_id=1, source_target_pairs={{0,32},{32,64},{64,96},{96,0},{1,33},{33,65},{65,97},{97,1},{2,34}... | collective-permute-start | bytes 884744 | tf_op jit(solution)/shard_map/ppermute | solution.py:53
  41.8 22.2 %collective-permute-start.11 = (bf16[1152,128]{1,0:T(8,128)(2,1)}, bf16[1152,128]{1,0:T(8,128)(2,1)S(1)}, u32[]{:S(2)}, u32[]{:S(2)}) collective-permute-start(bf16[1152,128]{1,0:T(8,128)(2,1)} %pad_maximum_fusion.12), channel_id=1, source_target_pairs={{0,96},{32,0},{64,32},{96,64},{1,97},{33,1},{65,33},{97,65},{2,98}... | collective-permute-start | bytes 884744 | tf_op jit(solution)/shard_map/ppermute | solution.py:53
  45.5 20.4 %collective-permute-start.12 = (bf16[1152,128]{1,0:T(8,128)(2,1)}, bf16[1152,128]{1,0:T(8,128)(2,1)}, u32[]{:S(2)}, u32[]{:S(2)}) collective-permute-start(bf16[1152,128]{1,0:T(8,128)(2,1)} %pad_maximum_fusion.12), channel_id=1, source_target_pairs={{0,64},{32,96},{64,0},{96,32},{1,65},{33,97},{65,1},{97,33},{2,66}... | collective-permute-start | bytes 884744 | tf_op jit(solution)/shard_map/ppermute | solution.py:53
  69.9 32.0 %collective-permute-start.13 = (bf16[8,1152,128]{2,1,0:T(8,128)(2,1)}, bf16[8,1152,128]{2,1,0:T(8,128)(2,1)}, u32[]{:S(2)}, u32[]{:S(2)}) collective-permute-start(bf16[8,1152,128]{2,1,0:T(8,128)(2,1)} %shard_map.86), channel_id=1, source_target_pairs={{0,1},{1,0},{2,3},{3,2},{4,5},{5,4},{6,7},{7,6},{8,9},{9,8},{10,11... | collective-permute-start | bytes 7077896 | tf_op jit(solution)/shard_map/ppermute | solution.py:49
  70.0 26.3 %collective-permute-start.16 = (bf16[160,3072]{1,0:T(8,128)(2,1)S(1)}, bf16[160,3072]{1,0:T(8,128)(2,1)}, u32[]{:S(2)}, u32[]{:S(2)}) collective-permute-start(bf16[160,3072]{1,0:T(8,128)(2,1)S(1)} %pad_maximum_fusion.4.refs_5_), channel_id=1, source_target_pairs={{0,16},{16,0},{1,17},{17,1},{2,18},{18,2},{3,19},{19,3},{4,20},{20... | collective-permute-start | bytes 2949128 | tf_op jit(solution)/shard_map/ppermute | solution.py:49
  70.7 41.5 %collective-permute-start.14 = (bf16[96,3072]{1,0:T(8,128)(2,1)}, bf16[96,3072]{1,0:T(8,128)(2,1)}, u32[]{:S(2)}, u32[]{:S(2)}) collective-permute-start(bf16[96,3072]{1,0:T(8,128)(2,1)} %slice.104), channel_id=1, source_target_pairs={{0,64},{32,96},{64,0},{96,32},{1,65},{33,97},{65,1},{97,33},{2,66}... | collective-permute-start | bytes 1769480 | tf_op jit(solution)/shard_map/ppermute | solution.py:53
  72.0 40.2 %collective-permute-start.15 = (bf16[96,3072]{1,0:T(8,128)(2,1)}, bf16[96,3072]{1,0:T(8,128)(2,1)}, u32[]{:S(2)}, u32[]{:S(2)}) collective-permute-start(bf16[96,3072]{1,0:T(8,128)(2,1)} %collective-permute-done.5.refs_7_), channel_id=1, source_target_pairs={{0,16},{16,0},{1,17},{17,1},{2,18},{18,2},{3,19},{19,3},{4,20},{20... | collective-permute-start | bytes 1769480 | tf_op jit(solution)/shard_map/ppermute | solution.py:49
  98.2 20.1 %collective-permute-start.17 = (bf16[128,3072]{1,0:T(8,128)(2,1)}, bf16[128,3072]{1,0:T(8,128)(2,1)}, u32[]{:S(2)}, u32[]{:S(2)}) collective-permute-start(bf16[128,3072]{1,0:T(8,128)(2,1)} %pad_maximum_fusion.9), channel_id=1, source_target_pairs={{0,32},{32,64},{64,96},{96,0},{1,33},{33,65},{65,97},{97,1},{2,34}... | collective-permute-start | bytes 2359304 | tf_op jit(solution)/shard_map/ppermute | solution.py:53
  120.1 19.5 %all-to-all-start.1 = ((bf16[16,8,3840]{2,1,0:T(8,128)(2,1)}), bf16[16,8,3840]{2,1,0:T(8,128)(2,1)S(1)}, u32[]{:S(2)}, u32[]{:S(2)}) async-start(bf16[16,8,3840]{2,1,0:T(8,128)(2,1)} %pad_maximum_fusion.5), calls=%async_computation.1 | async-start | bytes 1966080 | tf_op jit(solution)/shard_map/all_to_all | solution.py:57
  123.9 40.1 %collective-permute-start.21 = (bf16[128,3072]{1,0:T(8,128)(2,1)}, bf16[128,3072]{1,0:T(8,128)(2,1)}, u32[]{:S(2)}, u32[]{:S(2)}) collective-permute-start(bf16[128,3072]{1,0:T(8,128)(2,1)} %pad_maximum_fusion.9), channel_id=1, source_target_pairs={{0,64},{32,96},{64,0},{96,32},{1,65},{33,97},{65,1},{97,33},{2,66}... | collective-permute-start | bytes 2359304 | tf_op jit(solution)/shard_map/ppermute | solution.py:53
  126.7 24.9 %collective-permute-start.19 = (bf16[96,3072]{1,0:T(8,128)(2,1)}, bf16[96,3072]{1,0:T(8,128)(2,1)}, u32[]{:S(2)}, u32[]{:S(2)}) collective-permute-start(bf16[96,3072]{1,0:T(8,128)(2,1)} %collective-permute-done.6.refs_8_), channel_id=1, source_target_pairs={{0,16},{16,0},{1,17},{17,1},{2,18},{18,2},{3,19},{19,3},{4,20},{20... | collective-permute-start | bytes 1769480 | tf_op jit(solution)/shard_map/ppermute | solution.py:49
  128.5 35.5 %collective-permute-start.20 = (bf16[96,3072]{1,0:T(8,128)(2,1)}, bf16[96,3072]{1,0:T(8,128)(2,1)}, u32[]{:S(2)}, u32[]{:S(2)}) collective-permute-start(bf16[96,3072]{1,0:T(8,128)(2,1)} %collective-permute-done.14.refs_9_), channel_id=1, source_target_pairs={{0,16},{16,0},{1,17},{17,1},{2,18},{18,2},{3,19},{19,3},{4,20},{20... | collective-permute-start | bytes 1769480 | tf_op jit(solution)/shard_map/ppermute | solution.py:49
  164.0 33.5 %collective-permute-start.22 = (bf16[160,3072]{1,0:T(8,128)(2,1)S(1)}, bf16[160,3072]{1,0:T(8,128)(2,1)S(1)}, u32[]{:S(2)}, u32[]{:S(2)}) collective-permute-start(bf16[160,3072]{1,0:T(8,128)(2,1)S(1)} %pad_maximum_fusion.6.refs_0_), channel_id=1, source_target_pairs={{0,16},{16,0},{1,17},{17,1},{2,18},{18,2},{3,19},{19,3},{4,20},{20... | collective-permute-start | bytes 2949128 | tf_op jit(solution)/shard_map/ppermute | solution.py:49
  166.8 27.0 %collective-permute-start.24 = (bf16[96,3072]{1,0:T(8,128)(2,1)S(1)}, bf16[96,3072]{1,0:T(8,128)(2,1)}, u32[]{:S(2)}, u32[]{:S(2)}) collective-permute-start(bf16[96,3072]{1,0:T(8,128)(2,1)S(1)} %slice.119), channel_id=1, source_target_pairs={{0,96},{32,0},{64,32},{96,64},{1,97},{33,1},{65,33},{97,65},{2,98}... | collective-permute-start | bytes 1769480 | tf_op jit(solution)/shard_map/ppermute | solution.py:53
  169.1 26.5 %collective-permute-start.25 = (bf16[96,3072]{1,0:T(8,128)(2,1)S(1)}, bf16[96,3072]{1,0:T(8,128)(2,1)}, u32[]{:S(2)}, u32[]{:S(2)}) collective-permute-start(bf16[96,3072]{1,0:T(8,128)(2,1)S(1)} %slice.119), channel_id=1, source_target_pairs={{0,64},{32,96},{64,0},{96,32},{1,65},{33,97},{65,1},{97,33},{2,66}... | collective-permute-start | bytes 1769480 | tf_op jit(solution)/shard_map/ppermute | solution.py:53
  182.8 19.9 %collective-permute-start.26 = (bf16[96,3072]{1,0:T(8,128)(2,1)S(1)}, bf16[96,3072]{1,0:T(8,128)(2,1)S(1)}, u32[]{:S(2)}, u32[]{:S(2)}) collective-permute-start(bf16[96,3072]{1,0:T(8,128)(2,1)S(1)} %collective-permute-done.23.refs_2_), channel_id=1, source_target_pairs={{0,16},{16,0},{1,17},{17,1},{2,18},{18,2},{3,19},{19,3},{4,20},{20... | collective-permute-start | bytes 1769480 | tf_op jit(solution)/shard_map/ppermute | solution.py:49
  193.9 38.0 %collective-permute-start.27 = (bf16[96,3072]{1,0:T(8,128)(2,1)}, bf16[96,3072]{1,0:T(8,128)(2,1)}, u32[]{:S(2)}, u32[]{:S(2)}) collective-permute-start(bf16[96,3072]{1,0:T(8,128)(2,1)} %collective-permute-done.24.refs_3_), channel_id=1, source_target_pairs={{0,16},{16,0},{1,17},{17,1},{2,18},{18,2},{3,19},{19,3},{4,20},{20... | collective-permute-start | bytes 1769480 | tf_op jit(solution)/shard_map/ppermute | solution.py:49
  195.6 38.2 %collective-permute-start.28 = (bf16[96,3072]{1,0:T(8,128)(2,1)}, bf16[96,3072]{1,0:T(8,128)(2,1)}, u32[]{:S(2)}, u32[]{:S(2)}) collective-permute-start(bf16[96,3072]{1,0:T(8,128)(2,1)} %collective-permute-done.25.refs_4_), channel_id=1, source_target_pairs={{0,16},{16,0},{1,17},{17,1},{2,18},{18,2},{3,19},{19,3},{4,20},{20... | collective-permute-start | bytes 1769480 | tf_op jit(solution)/shard_map/ppermute | solution.py:49
  198.6 35.7 %collective-permute-start.29 = (bf16[128,3072]{1,0:T(8,128)(2,1)S(1)}, bf16[128,3072]{1,0:T(8,128)(2,1)}, u32[]{:S(2)}, u32[]{:S(2)}) collective-permute-start(bf16[128,3072]{1,0:T(8,128)(2,1)S(1)} %pad_maximum_fusion.10), channel_id=1, source_target_pairs={{0,32},{32,64},{64,96},{96,0},{1,33},{33,65},{65,97},{97,1},{2,34}... | collective-permute-start | bytes 2359304 | tf_op jit(solution)/shard_map/ppermute | solution.py:53
  199.4 36.3 %collective-permute-start.30 = (bf16[128,3072]{1,0:T(8,128)(2,1)S(1)}, bf16[128,3072]{1,0:T(8,128)(2,1)}, u32[]{:S(2)}, u32[]{:S(2)}) collective-permute-start(bf16[128,3072]{1,0:T(8,128)(2,1)S(1)} %pad_maximum_fusion.10), channel_id=1, source_target_pairs={{0,96},{32,0},{64,32},{96,64},{1,97},{33,1},{65,33},{97,65},{2,98}... | collective-permute-start | bytes 2359304 | tf_op jit(solution)/shard_map/ppermute | solution.py:53
  202.7 34.7 %collective-permute-start.31 = (bf16[128,3072]{1,0:T(8,128)(2,1)S(1)}, bf16[128,3072]{1,0:T(8,128)(2,1)}, u32[]{:S(2)}, u32[]{:S(2)}) collective-permute-start(bf16[128,3072]{1,0:T(8,128)(2,1)S(1)} %pad_maximum_fusion.10), channel_id=1, source_target_pairs={{0,64},{32,96},{64,0},{96,32},{1,65},{33,97},{65,1},{97,33},{2,66}... | collective-permute-start | bytes 2359304 | tf_op jit(solution)/shard_map/ppermute | solution.py:53
  231.9 33.6 %collective-permute-start.32 = (bf16[96,3072]{1,0:T(8,128)(2,1)}, bf16[96,3072]{1,0:T(8,128)(2,1)}, u32[]{:S(2)}, u32[]{:S(2)}) collective-permute-start(bf16[96,3072]{1,0:T(8,128)(2,1)} %get-tuple-element.43), channel_id=1, source_target_pairs={{0,96},{32,0},{64,32},{96,64},{1,97},{33,1},{65,33},{97,65},{2,98}... | collective-permute-start | bytes 1769480 | tf_op jit(solution)/shard_map/ppermute | solution.py:53
  233.8 31.7 %collective-permute-start.33 = (bf16[96,3072]{1,0:T(8,128)(2,1)}, bf16[96,3072]{1,0:T(8,128)(2,1)}, u32[]{:S(2)}, u32[]{:S(2)}) collective-permute-start(bf16[96,3072]{1,0:T(8,128)(2,1)} %get-tuple-element.44), channel_id=1, source_target_pairs={{0,32},{32,64},{64,96},{96,0},{1,33},{33,65},{65,97},{97,1},{2,34}... | collective-permute-start | bytes 1769480 | tf_op jit(solution)/shard_map/ppermute | solution.py:53
  234.3 31.2 %collective-permute-start.34 = (bf16[96,3072]{1,0:T(8,128)(2,1)}, bf16[96,3072]{1,0:T(8,128)(2,1)}, u32[]{:S(2)}, u32[]{:S(2)}) collective-permute-start(bf16[96,3072]{1,0:T(8,128)(2,1)} %get-tuple-element.45), channel_id=1, source_target_pairs={{0,64},{32,96},{64,0},{96,32},{1,65},{33,97},{65,1},{97,33},{2,66}... | collective-permute-start | bytes 1769480 | tf_op jit(solution)/shard_map/ppermute | solution.py:53
  235.7 29.8 %collective-permute-start.35 = (bf16[64,3072]{1,0:T(8,128)(2,1)}, bf16[64,3072]{1,0:T(8,128)(2,1)S(1)}, u32[]{:S(2)}, u32[]{:S(2)}) collective-permute-start(bf16[64,3072]{1,0:T(8,128)(2,1)} %get-tuple-element.46), channel_id=1, source_target_pairs={{0,16},{16,0},{1,17},{17,1},{2,18},{18,2},{3,19},{19,3},{4,20},{20... | collective-permute-start | bytes 1179656 | tf_op jit(solution)/shard_map/ppermute | solution.py:49
  267.7 24.1 %collective-permute-start.37 = (bf16[96,3072]{1,0:T(8,128)(2,1)}, bf16[96,3072]{1,0:T(8,128)(2,1)S(1)}, u32[]{:S(2)}, u32[]{:S(2)}) collective-permute-start(bf16[96,3072]{1,0:T(8,128)(2,1)} %get-tuple-element.48), channel_id=1, source_target_pairs={{0,32},{32,64},{64,96},{96,0},{1,33},{33,65},{65,97},{97,1},{2,34}... | collective-permute-start | bytes 1769480 | tf_op jit(solution)/shard_map/ppermute | solution.py:53
  268.8 23.0 %collective-permute-start.36 = (bf16[96,3072]{1,0:T(8,128)(2,1)}, bf16[96,3072]{1,0:T(8,128)(2,1)S(1)}, u32[]{:S(2)}, u32[]{:S(2)}) collective-permute-start(bf16[96,3072]{1,0:T(8,128)(2,1)} %get-tuple-element.47), channel_id=1, source_target_pairs={{0,96},{32,0},{64,32},{96,64},{1,97},{33,1},{65,33},{97,65},{2,98}... | collective-permute-start | bytes 1769480 | tf_op jit(solution)/shard_map/ppermute | solution.py:53
  271.0 25.2 %collective-permute-start.40 = (bf16[192,3072]{1,0:T(8,128)(2,1)}, bf16[192,3072]{1,0:T(8,128)(2,1)S(1)}, u32[]{:S(2)}, u32[]{:S(2)}) collective-permute-start(bf16[192,3072]{1,0:T(8,128)(2,1)} %get-tuple-element.55), channel_id=1, source_target_pairs={{0,16},{16,0},{1,17},{17,1},{2,18},{18,2},{3,19},{19,3},{4,20},{20... | collective-permute-start | bytes 3538952 | tf_op jit(solution)/shard_map/ppermute | solution.py:49
  319.5 21.1 %all-to-all-start.2 = ((bf16[16,8,3840]{2,1,0:T(8,128)(2,1)}), bf16[16,8,3840]{2,1,0:T(8,128)(2,1)S(1)}, u32[]{:S(2)}, u32[]{:S(2)}) async-start(bf16[16,8,3840]{2,1,0:T(8,128)(2,1)} %pad_maximum_fusion.7), calls=%async_computation.2 | async-start | bytes 1966080 | tf_op jit(solution)/shard_map/all_to_all | solution.py:57
  360.2 39.6 %all-to-all-start.3 = ((bf16[64,144,128]{2,1,0:T(8,128)(2,1)}), bf16[64,144,128]{2,1,0:T(8,128)(2,1)}, u32[]{:S(2)}, u32[]{:S(2)}) async-start(bf16[64,144,128]{2,1,0:T(8,128)(2,1)} %shard_map.89), calls=%async_computation.3 | async-start | bytes 4718592 | tf_op jit(solution)/shard_map/all_to_all | solution.py:57
  (57 other events, 675.7 us)

commit v3 on v1

--- a/solution.py
+++ b/solution.py
@@ -156,9 +156,10 @@
     return [own, own_y] + [along_z(one, s) for s in (1, 3, 2)]
 
 
-def spread_far(near):
+def spread_far(near, *earlier):
     own, own_y, near_z, far_z, across = near
     pair = after(jnp.concatenate([own[HALF:], own_y[HALF:]], axis=0), near_z, far_z)
+    near_z = after(near_z, *earlier) if earlier else near_z
     first = [swap(block, "yh") for block in (near_z, far_z, across)]
     return first + [along_z(pair, s) for s in (1, 3, 2)]
 
@@ -180,31 +181,71 @@
     return jnp.concatenate([one, two], axis=0)
 
 
+def load(source, target, sem):
+    copy = pltpu.make_async_copy(source, target, sem)
+    copy.start()
+    return copy
+
+
+def act_kernel(counts, *refs):
+    count = len(counts)
+    cot_refs, outer_ref, out_ref = refs[:count], refs[count], refs[count + 1]
+    cot, outer_map, row_sem, map_sem = refs[count + 2 :]
+    hidden, features = outer_ref.shape
+    copies = [load(outer_ref, outer_map.at[pl.ds(0, hidden)], map_sem.at[0])]
+    for i, ref in enumerate(cot_refs):
+        copies.append(load(ref, cot.at[pl.ds(sum(counts[:i]), counts[i])], row_sem.at[i]))
+    outer_map[pl.ds(hidden, PADDED - hidden)] = jnp.zeros((PADDED - hidden, features), BF16)
+    for copy in copies:
+        copy.wait()
+    tall = sum(counts) // 2
+
+    @pl.loop(0, 2)
+    def _(step):
+        here = pl.ds(pl.multiple_of(step * tall, 16), tall)
+        out_ref[here] = contract(cot[here], outer_map[...], 1, 1).astype(BF16)
+
+
+def act_grads(cot_blocks, outer):
+    counts = [block.shape[0] for block in cot_blocks]
+    features = outer.shape[1]
+    total = sum(counts)
+    anywhere = pl.BlockSpec(memory_space=pl.ANY)
+    return pl.pallas_call(
+        lambda *refs: act_kernel(counts, *refs),
+        out_shape=jax.ShapeDtypeStruct((total, PADDED), BF16),
+        in_specs=[anywhere] * (len(counts) + 1),
+        out_specs=pl.BlockSpec(memory_space=pltpu.VMEM),
+        scratch_shapes=[
+            pltpu.VMEM((total, features), BF16),
+            pltpu.VMEM((PADDED, features), BF16),
+            pltpu.SemaphoreType.DMA((len(counts),)),
+            pltpu.SemaphoreType.DMA((1,)),
+        ],
+        compiler_params=pltpu.CompilerParams(vmem_limit_bytes=60 * 1024 * 1024),
+        cost_estimate=pl.CostEstimate(
+            flops=2 * total * features * PADDED,
+            bytes_accessed=2 * (total + PADDED) * features,
+            transcendentals=0,
+        ),
+    )(*cot_blocks, outer)
+
+
 def expert_kernel(counts, pieces_out, tall, *refs):
     count = len(counts)
     outs = len(pieces_out)
-    normed_refs, cot_refs = refs[:count], refs[count : 2 * count]
-    inner_ref, outer_ref = refs[2 * count : 2 * count + 2]
-    out_refs = refs[2 * count + 2 : 2 * count + 2 + outs]
-    (normed, cot, gate_map, up_map, outer_map, grad_gate, grad_up, result, row_sem, map_sem, out_sem) = refs[
-        2 * count + 2 + outs :
+    normed_refs = refs[:count]
+    act_ref, inner_ref = refs[count : count + 2]
+    out_refs = refs[count + 2 : count + 2 + outs]
+    (normed, acts, gate_map, up_map, grad_gate, grad_up, result, row_sem, act_sem, map_sem, out_sem) = refs[
+        count + 2 + outs :
     ]
-    hidden, features = outer_ref.shape
-    starts = [sum(counts[:i]) for i in range(count)]
-
-    def load(source, target, sem):
-        copy = pltpu.make_async_copy(source, target, sem)
-        copy.start()
-        return copy
-
-    def load_rows(block_refs, target, side):
-        return [
-            load(ref, target.at[pl.ds(starts[i], counts[i])], row_sem.at[side, i])
-            for i, ref in enumerate(block_refs)
-        ]
-
+    _, hidden, features = inner_ref.shape
     pieces = [(0, 256), (256, 256), (512, hidden - 512)]
-    rows_in = load_rows(normed_refs, normed, 0)
+    rows_in = [
+        load(ref, normed.at[pl.ds(sum(counts[:i]), counts[i])], row_sem.at[i])
+        for i, ref in enumerate(normed_refs)
+    ]
     maps_in = []
     for i, (start, size) in enumerate(pieces):
         at = pl.ds(start, size)
@@ -212,13 +253,12 @@
             [
                 load(inner_ref.at[0, at], gate_map.at[at], map_sem.at[0, i]),
                 load(inner_ref.at[1, at], up_map.at[at], map_sem.at[1, i]),
-                load(outer_ref.at[at], outer_map.at[at], map_sem.at[2, i]),
             ]
         )
         if i == 0:
-            rows_in += load_rows(cot_refs, cot, 1)
+            rows_in.append(load(act_ref, acts, act_sem.at[0]))
     blank = jnp.zeros((PADDED - hidden, features), BF16)
-    for ref in (gate_map, up_map, outer_map):
+    for ref in (gate_map, up_map):
         ref[pl.ds(hidden, PADDED - hidden)] = blank
     for copy in rows_in:
         copy.wait()
@@ -234,9 +274,8 @@
             here = pl.ds(pl.multiple_of(step * tall, 16), tall)
             gate_part = contract(normed[here], gate_map[at], 1, 1)
             up_part = contract(normed[here], up_map[at], 1, 1)
-            grad_act = contract(cot[here], outer_map[at], 1, 1)
             squash = 1.0 / (1.0 + jnp.exp(-gate_part))
-            scaled = grad_act * squash
+            scaled = acts[here, at].astype(F32) * squash
             grad_gate[here, at] = (scaled * up_part * (1.0 + gate_part * (1.0 - squash))).astype(BF16)
             grad_up[here, at] = (scaled * gate_part).astype(BF16)
 
@@ -270,10 +309,9 @@
         copy.wait()
 
 
-def experts(normed_blocks, cot_blocks, inner, outer, pieces_out, tall):
+def experts(normed_blocks, acts, inner, pieces_out, tall):
     counts = [block.shape[0] for block in normed_blocks]
     features = normed_blocks[0].shape[1]
-    hidden = outer.shape[0]
     total = sum(counts)
     anywhere = pl.BlockSpec(memory_space=pl.ANY)
     return pl.pallas_call(
@@ -281,28 +319,28 @@
         out_shape=[
             jax.ShapeDtypeStruct((sum(size for _, size in parts), features), BF16) for parts in pieces_out
         ],
-        in_specs=[anywhere] * (2 * len(counts) + 2),
+        in_specs=[anywhere] * (len(counts) + 2),
         out_specs=[anywhere] * len(pieces_out),
         scratch_shapes=[
             pltpu.VMEM((total, features), BF16),
-            pltpu.VMEM((total, features), BF16),
-            pltpu.VMEM((PADDED, features), BF16),
+            pltpu.VMEM((total, PADDED), BF16),
             pltpu.VMEM((PADDED, features), BF16),
             pltpu.VMEM((PADDED, features), BF16),
             pltpu.VMEM((total, PADDED), BF16),
             pltpu.VMEM((total, PADDED), BF16),
             pltpu.VMEM((total, features), BF16),
-            pltpu.SemaphoreType.DMA((2, len(counts))),
-            pltpu.SemaphoreType.DMA((3, 3)),
+            pltpu.SemaphoreType.DMA((len(counts),)),
+            pltpu.SemaphoreType.DMA((1,)),
+            pltpu.SemaphoreType.DMA((2, 3)),
             pltpu.SemaphoreType.DMA((features // 512, sum(len(parts) for parts in pieces_out))),
         ],
         compiler_params=pltpu.CompilerParams(vmem_limit_bytes=60 * 1024 * 1024),
         cost_estimate=pl.CostEstimate(
-            flops=10 * total * features * hidden,
-            bytes_accessed=6 * total * features + 6 * hidden * features,
-            transcendentals=total * hidden,
+            flops=8 * total * features * PADDED,
+            bytes_accessed=4 * total * features + 4 * PADDED * features,
+            transcendentals=total * PADDED,
         ),
-    )(*normed_blocks, *cot_blocks, inner, outer)
+    )(*normed_blocks, acts, inner)
 
 
 def param_kernel(scale, head_dim, core_ref, normed_ref, hidden_ref, grads_ref, out_ref, terms):
@@ -383,26 +421,25 @@
     normed_two, inverse_two = layer_norm(residual)
     normed_two_b = after(normed_two.astype(BF16), cot_near[4], cot_far[0], cot_far[1], cot_far[3], cot_far[4])
     main, extra = between_experts(contract(slots, normed_two_b, 1, 0).astype(BF16))
-    near = spread_near(jnp.concatenate([main, extra], axis=0))
-    near[4] = after(near[4], cot_far[2], cot_far[5])
+    near_acts = act_grads(cot_near, outer)
+    far_acts = act_grads(cot_far, outer)
+    near = spread_near(after(jnp.concatenate([main, extra], axis=0), near_acts, cot_far[2], cot_far[5]))
     h = HALF
     whole = EXPERTS * CAP
     rest = whole - h
     near_rows = experts(
         near,
-        cot_near,
+        near_acts,
         inner,
-        outer,
         [[(0, whole)], [(whole, h)], [(whole + h, rest)]] + [[(2 * whole + i * h, h)] for i in range(3)],
         2 * whole + 3 * h,
     )
-    far = spread_far(near)
+    far = spread_far(near, far_acts)
     far[0] = after(far[0], near_rows[0])
     far_rows = experts(
         far,
-        cot_far,
+        far_acts,
         inner,
-        outer,
         [[(i * h, h)] for i in range(3)]
         + [[(3 * h + (2 * i + r) * rest, rest) for i in range(3)] for r in (0, 1)],
         (h + 2 * rest) * 3 // 2,

time: 404 us -> 395 us (0.978)
  waiting for transfers between devices: 178 us -> 162 us
  starting transfers between devices: 93.3 us -> 97.9 us
    pallas_call x0 -> x2, Pallas kernels: none -> 15.5 us  [act_grads(): pl.pallas_call(lambda *refs: act_kernel(counts, *refs), out_shape=jax.Sha...]
    pallas_call x2, Pallas kernels: 55.1 us -> 41.6 us  [experts(): pl.pallas_call(lambda *refs: expert_kernel(counts, pieces_out, tall, *ref...]
    ppermute x27, waiting for transfers between devices: 66.7 us -> 53.2 us  [along_z(): return lax.ppermute(values, 'z', [(i, (i + shift) % 4) for i in range(4)])]
    all_to_all x4, waiting for transfers between devices: 60.6 us -> 51.9 us  [exchange(): return lax.all_to_all(blocks, axes, split_axis=0, concat_axis=0, tiled=True)]
    ppermute x19, waiting for transfers between devices: 51 us -> 56.9 us  [swap(): return lax.ppermute(values, axis, [(0, 1), (1, 0)])]
  transfers between devices with their start and end apart: 50 -> 50, of which waited for: 20 -> 26; matrix products, arithmetic and copies ran while one was open for 8% -> 9% of each run, Pallas kernels for 14% -> 15%
where the time goes in v3:
time: 395 us; the launch traced here: 387 us
  waiting for transfers between devices  162 us (41%)
  starting transfers between devices  97.9 us (25%)
  Pallas kernels  65.6 us (17%)
  other arithmetic  25.5 us (6%)
  matrix products  19.3 us (5%)
  local copies, waits for them, and re-layouts  15 us (4%)
    ppermute x19, waiting for transfers between devices, swap(): return lax.ppermute(values, axis, [(0, 1), (1, 0)])  56.9 us
    ppermute x27, waiting for transfers between devices, along_z(): return lax.ppermute(values, 'z', [(i, (i + shift) % 4) for i in range(4)])  53.2 us
    all_to_all x4, waiting for transfers between devices, exchange(): return lax.all_to_all(blocks, axes, split_axis=0, concat_axis=0, tiled=True)  51.9 us
    ppermute x27, starting transfers between devices, along_z(): return lax.ppermute(values, 'z', [(i, (i + shift) % 4) for i in range(4)])  45.6 us
    pallas_call x2, Pallas kernels, experts(): pl.pallas_call(lambda *refs: expert_kernel(counts, pieces_out, tall, *ref...  41.6 us
    ppermute x19, starting transfers between devices, swap(): return lax.ppermute(values, axis, [(0, 1), (1, 0)])  30.2 us
    all_to_all x4, starting transfers between devices, exchange(): return lax.all_to_all(blocks, axes, split_axis=0, concat_axis=0, tiled=True)  22.2 us
    pallas_call x2, Pallas kernels, act_grads(): pl.pallas_call(lambda *refs: act_kernel(counts, *refs), out_shape=jax.Sha...  15.5 us
  transfers between devices with their start and end apart: 50, of which 26 were waited for; matrix products, arithmetic and copies ran while one was open for 9% of the time, Pallas kernels for 15%

profile of v3, /device:TPU:0, one launch (start us, length us, event | category | flops | bytes accessed | tf_op | source)
XLA Modules:
  0.0 387.3 jit_solution(2978752224140448699)
XLA Ops:
  5.6 5.5 %all-to-all-start = ((bf16[16,8,3840]{2,1,0:T(8,128)(2,1)}), bf16[16,8,3840]{2,1,0:T(8,128)(2,1)S(1)}, u32[]{:S(2)}, u32[]{:S(2)}) async-start(bf16[16,8,3840]{2,1,0:T(8,128)(2,1)} %pad_maximum_fusion.3), calls=%async_computation | async-start | bytes 1966080 | tf_op jit(solution)/shard_map/all_to_all | solution.py:57
  19.9 2.9 collective-permute-start
  22.8 4.1 %all-to-all-done = bf16[16,8,3840]{2,1,0:T(8,128)(2,1)S(1)} async-done(((bf16[16,8,3840]{2,1,0:T(8,128)(2,1)}), bf16[16,8,3840]{2,1,0:T(8,128)(2,1)S(1)}, u32[]{:S(2)}, u32[]{:S(2)}) %all-to-all-start) | async-done | bytes 983072 | tf_op jit(solution)/shard_map/all_to_all | solution.py:57
  28.8 5.3 %collective-permute-done.refs_2_ = bf16[1152,128]{1,0:T(8,128)(2,1)} collective-permute-done((bf16[1152,128]{1,0:T(8,128)(2,1)}, bf16[1152,128]{1,0:T(8,128)(2,1)}, u32[]{:S(2)}, u32[]{:S(2)}) %collective-permute-start) | collective-permute-done | bytes 294944 | tf_op jit(solution)/shard_map/ppermute | solution.py:49
  43.1 18.7 %collective-permute-done.8.refs_6_ = bf16[576,128]{1,0:T(8,128)(2,1)S(1)} collective-permute-done((bf16[576,128]{1,0:T(8,128)(2,1)}, bf16[576,128]{1,0:T(8,128)(2,1)S(1)}, u32[]{:S(2)}, u32[]{:S(2)}) %collective-permute-start.8) | collective-permute-done | bytes 147488 | tf_op jit(solution)/shard_map/ppermute | solution.py:49
  61.8 4.1 %collective-permute-start.12 = (bf16[1152,128]{1,0:T(8,128)(2,1)}, bf16[1152,128]{1,0:T(8,128)(2,1)}, u32[]{:S(2)}, u32[]{:S(2)}) collective-permute-start(bf16[1152,128]{1,0:T(8,128)(2,1)} %pad_maximum_fusion.12), channel_id=1, source_target_pairs={{0,96},{32,0},{64,32},{96,64},{1,97},{33,1},{65,33},{97,65},{2,98}... | collective-permute-start | bytes 884744 | tf_op jit(solution)/shard_map/ppermute | solution.py:53
  71.1 3.1 collective-permute-done.9.refs_7_
  78.0 3.9 %shard_map.86 = bf16[8,1152,128]{2,1,0:T(8,128)(2,1)} custom-call(s32[2]{0:T(128)} %pad_add_fusion.refs_0_, bf16[1152,128]{1,0:T(8,128)(2,1)} %constant_dynamic-slice_fusion.2.refs_1_, bf16[1152,128]{1,0:T(8,128)(2,1)} %collective-permute-done.refs_2_, bf16[576,128]{1,0:T(8,128)(2,1)} %collective-permute-done.2.refs_3_, ...), custom_call_target="tpu_custom_call" | custom-call | tf_op jit(solution)/shard_map/pallas_call | solution.py:128
  87.6 3.7 collective-permute-start.18
  102.2 10.9 %collective-permute-done.17.refs_1_ = bf16[96,3072]{1,0:T(8,128)(2,1)} collective-permute-done((bf16[96,3072]{1,0:T(8,128)(2,1)}, bf16[96,3072]{1,0:T(8,128)(2,1)}, u32[]{:S(2)}, u32[]{:S(2)}) %collective-permute-start.17) | collective-permute-done | bytes 589856 | tf_op jit(solution)/shard_map/ppermute | solution.py:49
  113.0 3.5 collective-permute-done.18.refs_3_
  119.3 3.8 all-to-all-start.1
  126.1 7.5 %shard_map.87.refs_5_ = bf16[608,768]{1,0:T(8,128)(2,1)} custom-call(bf16[160,3072]{1,0:T(8,128)(2,1)} %copy-done.5, bf16[160,3072]{1,0:T(8,128)(2,1)} %copy-done.9, bf16[96,3072]{1,0:T(8,128)(2,1)} %copy-done.34, bf16[96,3072]{1,0:T(8,128)(2,1)} %copy-done.35, bf16[96,3072]{1,0:T(8,128)(2,1)} %collective-permute-done.15.refs_4_, bf16[672,3072]{1,0:T(8,128)(2,1)} %bitcast.124), custom_call_target="tpu_custom_call" | custom-call | flops 2868903936 | bytes 8454144 | tf_op jit(solution)/shard_map/pallas_call | solution.py:214
  133.6 5.3 %all-to-all-done.1 = bf16[16,8,3840]{2,1,0:T(8,128)(2,1)S(1)} async-done(((bf16[16,8,3840]{2,1,0:T(8,128)(2,1)}), bf16[16,8,3840]{2,1,0:T(8,128)(2,1)S(1)}, u32[]{:S(2)}, u32[]{:S(2)}) %all-to-all-start.1) | async-done | bytes 983072 | tf_op jit(solution)/shard_map/all_to_all | solution.py:57
  142.0 7.6 %collective-permute-done.20.refs_2_ = bf16[96,3072]{1,0:T(8,128)(2,1)} collective-permute-done((bf16[96,3072]{1,0:T(8,128)(2,1)}, bf16[96,3072]{1,0:T(8,128)(2,1)}, u32[]{:S(2)}, u32[]{:S(2)}) %collective-permute-start.20) | collective-permute-done | bytes 589856 | tf_op jit(solution)/shard_map/ppermute | solution.py:49
  156.3 8.1 %shard_map.89.refs_6_ = bf16[672,768]{1,0:T(8,128)(2,1)} custom-call(bf16[96,3072]{1,0:T(8,128)(2,1)} %collective-permute-done.16.refs_0_, bf16[96,3072]{1,0:T(8,128)(2,1)} %collective-permute-done.17.refs_1_, bf16[96,3072]{1,0:T(8,128)(2,1)} %collective-permute-done.20.refs_2_, bf16[128,3072]{1,0:T(8,128)(2,1)} %collective-permute-done.18.refs_3_, ...), custom_call_target="tpu_custom_call" | custom-call | flops 3170893824 | bytes 8847360 | tf_op jit(solution)/shard_map/pallas_call | solution.py:214
  164.4 4.1 %collective-permute-done.23.refs_2_ = bf16[96,3072]{1,0:T(8,128)(2,1)} collective-permute-done((bf16[96,3072]{1,0:T(8,128)(2,1)}, bf16[96,3072]{1,0:T(8,128)(2,1)}, u32[]{:S(2)}, u32[]{:S(2)}) %collective-permute-start.23) | collective-permute-done | bytes 589856 | tf_op jit(solution)/shard_map/ppermute | solution.py:53
  172.2 9.9 %collective-permute-done.25.refs_4_ = bf16[96,3072]{1,0:T(8,128)(2,1)} collective-permute-done((bf16[96,3072]{1,0:T(8,128)(2,1)}, bf16[96,3072]{1,0:T(8,128)(2,1)}, u32[]{:S(2)}, u32[]{:S(2)}) %collective-permute-start.25) | collective-permute-done | bytes 589856 | tf_op jit(solution)/shard_map/ppermute | solution.py:53
  190.5 18.6 %shard_map.88 = (bf16[160,3072]{1,0:T(8,128)(2,1)}, bf16[96,3072]{1,0:T(8,128)(2,1)}, bf16[64,3072]{1,0:T(8,128)(2,1)}, bf16[96,3072]{1,0:T(8,128)(2,1)}, bf16[9...) custom-call(bf16[160,3072]{1,0:T(8,128)(2,1)} %copy-done.4, bf16[160,3072]{1,0:T(8,128)(2,1)} %collective-permute-done.22.refs_1_, ...), custom_call_target="tpu_custom_call" | custom-call | flops 11475615744 | bytes 16908288 | tf_op jit(solution)/shard_map/pallas_call | solution.py:317
  220.9 2.9 collective-permute-done.31.refs_5_
  223.8 23.0 %shard_map.90 = (bf16[96,3072]{1,0:T(8,128)(2,1)}, bf16[96,3072]{1,0:T(8,128)(2,1)}, bf16[96,3072]{1,0:T(8,128)(2,1)}, bf16[192,3072]{1,0:T(8,128)(2,1)}, bf16[192,3072]{1,0:T(8,128)(2,1)}) custom-call(bf16[96,3072]{1,0:T(8,128)(2,1)} %copy-done.36, bf16[96,3072]{1,0:T(8,128)(2,1)} %collective-permute-done.27.refs_1_, ...), custom_call_target="tpu_custom_call" | custom-call | flops 12683575296 | bytes 17694720 | tf_op jit(solution)/shard_map/pallas_call | solution.py:317
  253.3 11.7 %collective-permute-done.38 = bf16[96,3072]{1,0:T(8,128)(2,1)S(1)} collective-permute-done((bf16[96,3072]{1,0:T(8,128)(2,1)}, bf16[96,3072]{1,0:T(8,128)(2,1)S(1)}, u32[]{:S(2)}, u32[]{:S(2)}) %collective-permute-start.38) | collective-permute-done | bytes 589856 | tf_op jit(solution)/shard_map/ppermute | solution.py:53
  264.9 8.2 %collective-permute-done.37 = bf16[96,3072]{1,0:T(8,128)(2,1)S(1)} collective-permute-done((bf16[96,3072]{1,0:T(8,128)(2,1)}, bf16[96,3072]{1,0:T(8,128)(2,1)S(1)}, u32[]{:S(2)}, u32[]{:S(2)}) %collective-permute-start.37) | collective-permute-done | bytes 589856 | tf_op jit(solution)/shard_map/ppermute | solution.py:53
  284.1 8.5 %collective-permute-done.39 = bf16[96,3072]{1,0:T(8,128)(2,1)S(1)} collective-permute-done((bf16[96,3072]{1,0:T(8,128)(2,1)S(1)}, bf16[96,3072]{1,0:T(8,128)(2,1)S(1)}, u32[]{:S(2)}, u32[]{:S(2)}) %collective-permute-start.39) | collective-permute-done | bytes 589856 | tf_op jit(solution)/shard_map/ppermute | solution.py:49
  294.4 4.8 %collective-permute-done.42 = bf16[64,3072]{1,0:T(8,128)(2,1)S(1)} collective-permute-done((bf16[64,3072]{1,0:T(8,128)(2,1)S(1)}, bf16[64,3072]{1,0:T(8,128)(2,1)S(1)}, u32[]{:S(2)}, u32[]{:S(2)}) %collective-permute-start.42) | collective-permute-done | bytes 393248 | tf_op jit(solution)/shard_map/ppermute | solution.py:53
  303.2 5.8 %all-to-all-start.2 = ((bf16[16,8,3840]{2,1,0:T(8,128)(2,1)}), bf16[16,8,3840]{2,1,0:T(8,128)(2,1)S(1)}, u32[]{:S(2)}, u32[]{:S(2)}) async-start(bf16[16,8,3840]{2,1,0:T(8,128)(2,1)} %pad_maximum_fusion.7), calls=%async_computation.2 | async-start | bytes 1966080 | tf_op jit(solution)/shard_map/all_to_all | solution.py:57
  310.4 14.4 %all-to-all-done.2 = bf16[16,8,3840]{2,1,0:T(8,128)(2,1)S(1)} async-done(((bf16[16,8,3840]{2,1,0:T(8,128)(2,1)}), bf16[16,8,3840]{2,1,0:T(8,128)(2,1)S(1)}, u32[]{:S(2)}, u32[]{:S(2)}) %all-to-all-start.2) | async-done | bytes 983072 | tf_op jit(solution)/shard_map/all_to_all | solution.py:57
  339.5 4.6 %shard_map.91 = bf16[64,144,128]{2,1,0:T(8,128)(2,1)} custom-call(s32[1]{0:T(128)} %bitcast.35.refs_0_, bf16[256,3072]{1,0:T(8,128)(2,1)S(1)} %pad_maximum_fusion.1.refs_1_, bf16[256,3072]{1,0:T(8,128)(2,1)S(1)} %pad_maximum_fusion.2.refs_2_, bf16[256,768]{1,0:T(8,128)(2,1)S(1)} %pad_maximum_fusion.11.refs_3_), custom_call_target="tpu_custom_call" | custom-call | flops 1207959552 | bytes 8388608 | tf_op jit(solution)/shard_map/pallas_call | solution.py:367
  344.1 7.1 %all-to-all-start.3 = ((bf16[64,144,128]{2,1,0:T(8,128)(2,1)}), bf16[64,144,128]{2,1,0:T(8,128)(2,1)}, u32[]{:S(2)}, u32[]{:S(2)}) async-start(bf16[64,144,128]{2,1,0:T(8,128)(2,1)} %shard_map.91), calls=%async_computation.3 | async-start | bytes 4718592 | tf_op jit(solution)/shard_map/all_to_all | solution.py:57
  351.3 3.3 fusion.79
  356.1 28.1 %all-to-all-done.3 = bf16[64,144,128]{2,1,0:T(8,128)(2,1)} async-done(((bf16[64,144,128]{2,1,0:T(8,128)(2,1)}), bf16[64,144,128]{2,1,0:T(8,128)(2,1)}, u32[]{:S(2)}, u32[]{:S(2)}) %all-to-all-start.3) | async-done | bytes 2359328 | tf_op jit(solution)/shard_map/all_to_all | solution.py:57
  384.3 2.6 convert_reduce_fusion
  (236 shorter events, 130.0 us)
Async XLA Ops:
  5.6 21.3 %all-to-all-start = ((bf16[16,8,3840]{2,1,0:T(8,128)(2,1)}), bf16[16,8,3840]{2,1,0:T(8,128)(2,1)S(1)}, u32[]{:S(2)}, u32[]{:S(2)}) async-start(bf16[16,8,3840]{2,1,0:T(8,128)(2,1)} %pad_maximum_fusion.3), calls=%async_computation | async-start | bytes 1966080 | tf_op jit(solution)/shard_map/all_to_all | solution.py:57
  12.0 22.1 %collective-permute-start.1 = (bf16[128,3072]{1,0:T(8,128)(2,1)S(1)}, bf16[128,3072]{1,0:T(8,128)(2,1)}, u32[]{:S(2)}, u32[]{:S(2)}) collective-permute-start(bf16[128,3072]{1,0:T(8,128)(2,1)S(1)} %fusion.13), channel_id=1, source_target_pairs={{0,1},{1,0},{2,3},{3,2},{4,5},{5,4},{6,7},{7,6},{8,9},{9,8},{10,11... | collective-permute-start | bytes 2359304 | tf_op jit(solution)/shard_map/ppermute | solution.py:49
  34.1 33.5 %collective-permute-start.5 = (bf16[160,3072]{1,0:T(8,128)(2,1)S(1)}, bf16[160,3072]{1,0:T(8,128)(2,1)S(1)}, u32[]{:S(2)}, u32[]{:S(2)}) collective-permute-start(bf16[160,3072]{1,0:T(8,128)(2,1)S(1)} %pad_maximum_fusion.4.refs_0_), channel_id=1, source_target_pairs={{0,16},{16,0},{1,17},{17,1},{2,18},{18,2},{3,19},{19,3},{4,20},{20... | collective-permute-start | bytes 2949128 | tf_op jit(solution)/shard_map/ppermute | solution.py:49
  35.4 30.4 %collective-permute-start.6 = (bf16[96,3072]{1,0:T(8,128)(2,1)S(1)}, bf16[96,3072]{1,0:T(8,128)(2,1)S(1)}, u32[]{:S(2)}, u32[]{:S(2)}) collective-permute-start(bf16[96,3072]{1,0:T(8,128)(2,1)S(1)} %slice.104), channel_id=1, source_target_pairs={{0,32},{32,64},{64,96},{96,0},{1,33},{33,65},{65,97},{97,1},{2,34}... | collective-permute-start | bytes 1769480 | tf_op jit(solution)/shard_map/ppermute | solution.py:53
  37.4 28.6 %collective-permute-start.7 = (bf16[96,3072]{1,0:T(8,128)(2,1)S(1)}, bf16[96,3072]{1,0:T(8,128)(2,1)S(1)}, u32[]{:S(2)}, u32[]{:S(2)}) collective-permute-start(bf16[96,3072]{1,0:T(8,128)(2,1)S(1)} %slice.104), channel_id=1, source_target_pairs={{0,96},{32,0},{64,32},{96,64},{1,97},{33,1},{65,33},{97,65},{2,98}... | collective-permute-start | bytes 1769480 | tf_op jit(solution)/shard_map/ppermute | solution.py:53
  38.7 23.0 %collective-permute-start.8 = (bf16[576,128]{1,0:T(8,128)(2,1)}, bf16[576,128]{1,0:T(8,128)(2,1)S(1)}, u32[]{:S(2)}, u32[]{:S(2)}) collective-permute-start(bf16[576,128]{1,0:T(8,128)(2,1)} %collective-permute-done.2.refs_3_), channel_id=1, source_target_pairs={{0,16},{16,0},{1,17},{17,1},{2,18},{18,2},{3,19},{19,3},{4,20},{20... | collective-permute-start | bytes 442376 | tf_op jit(solution)/shard_map/ppermute | solution.py:49
  43.0 33.0 %collective-permute-start.11 = (bf16[1152,128]{1,0:T(8,128)(2,1)}, bf16[1152,128]{1,0:T(8,128)(2,1)}, u32[]{:S(2)}, u32[]{:S(2)}) collective-permute-start(bf16[1152,128]{1,0:T(8,128)(2,1)} %pad_maximum_fusion.12), channel_id=1, source_target_pairs={{0,32},{32,64},{64,96},{96,0},{1,33},{33,65},{65,97},{97,1},{2,34}... | collective-permute-start | bytes 884744 | tf_op jit(solution)/shard_map/ppermute | solution.py:53
  82.1 20.1 %collective-permute-start.15 = (bf16[96,3072]{1,0:T(8,128)(2,1)}, bf16[96,3072]{1,0:T(8,128)(2,1)}, u32[]{:S(2)}, u32[]{:S(2)}) collective-permute-start(bf16[96,3072]{1,0:T(8,128)(2,1)} %copy-done.14), channel_id=1, source_target_pairs={{0,64},{32,96},{64,0},{96,32},{1,65},{33,97},{65,1},{97,33},{2,66}... | collective-permute-start | bytes 1769480 | tf_op jit(solution)/shard_map/ppermute | solution.py:53
  83.1 19.1 %collective-permute-start.16 = (bf16[96,3072]{1,0:T(8,128)(2,1)}, bf16[96,3072]{1,0:T(8,128)(2,1)}, u32[]{:S(2)}, u32[]{:S(2)}) collective-permute-start(bf16[96,3072]{1,0:T(8,128)(2,1)} %copy-done.34), channel_id=1, source_target_pairs={{0,16},{16,0},{1,17},{17,1},{2,18},{18,2},{3,19},{19,3},{4,20},{20... | collective-permute-start | bytes 1769480 | tf_op jit(solution)/shard_map/ppermute | solution.py:49
  85.1 27.9 %collective-permute-start.17 = (bf16[96,3072]{1,0:T(8,128)(2,1)}, bf16[96,3072]{1,0:T(8,128)(2,1)}, u32[]{:S(2)}, u32[]{:S(2)}) collective-permute-start(bf16[96,3072]{1,0:T(8,128)(2,1)} %copy-done.35), channel_id=1, source_target_pairs={{0,16},{16,0},{1,17},{17,1},{2,18},{18,2},{3,19},{19,3},{4,20},{20... | collective-permute-start | bytes 1769480 | tf_op jit(solution)/shard_map/ppermute | solution.py:49
  87.6 28.9 %collective-permute-start.18 = (bf16[128,3072]{1,0:T(8,128)(2,1)}, bf16[128,3072]{1,0:T(8,128)(2,1)}, u32[]{:S(2)}, u32[]{:S(2)}) collective-permute-start(bf16[128,3072]{1,0:T(8,128)(2,1)} %pad_maximum_fusion.9), channel_id=1, source_target_pairs={{0,32},{32,64},{64,96},{96,0},{1,33},{33,65},{65,97},{97,1},{2,34}... | collective-permute-start | bytes 2359304 | tf_op jit(solution)/shard_map/ppermute | solution.py:53
  91.3 26.3 %collective-permute-start.19 = (bf16[128,3072]{1,0:T(8,128)(2,1)}, bf16[128,3072]{1,0:T(8,128)(2,1)}, u32[]{:S(2)}, u32[]{:S(2)}) collective-permute-start(bf16[128,3072]{1,0:T(8,128)(2,1)} %pad_maximum_fusion.9), channel_id=1, source_target_pairs={{0,96},{32,0},{64,32},{96,64},{1,97},{33,1},{65,33},{97,65},{2,98}... | collective-permute-start | bytes 2359304 | tf_op jit(solution)/shard_map/ppermute | solution.py:53
  119.3 19.6 %all-to-all-start.1 = ((bf16[16,8,3840]{2,1,0:T(8,128)(2,1)}), bf16[16,8,3840]{2,1,0:T(8,128)(2,1)S(1)}, u32[]{:S(2)}, u32[]{:S(2)}) async-start(bf16[16,8,3840]{2,1,0:T(8,128)(2,1)} %pad_maximum_fusion.5), calls=%async_computation.1 | async-start | bytes 1966080 | tf_op jit(solution)/shard_map/all_to_all | solution.py:57
  123.1 26.5 %collective-permute-start.21 = (bf16[128,3072]{1,0:T(8,128)(2,1)}, bf16[128,3072]{1,0:T(8,128)(2,1)}, u32[]{:S(2)}, u32[]{:S(2)}) collective-permute-start(bf16[128,3072]{1,0:T(8,128)(2,1)} %pad_maximum_fusion.9), channel_id=1, source_target_pairs={{0,64},{32,96},{64,0},{96,32},{1,65},{33,97},{65,1},{97,33},{2,66}... | collective-permute-start | bytes 2359304 | tf_op jit(solution)/shard_map/ppermute | solution.py:53
  124.6 25.0 %collective-permute-start.20 = (bf16[96,3072]{1,0:T(8,128)(2,1)}, bf16[96,3072]{1,0:T(8,128)(2,1)}, u32[]{:S(2)}, u32[]{:S(2)}) collective-permute-start(bf16[96,3072]{1,0:T(8,128)(2,1)} %collective-permute-done.15.refs_4_), channel_id=1, source_target_pairs={{0,16},{16,0},{1,17},{17,1},{2,18},{18,2},{3,19},{19,3},{4,20},{20... | collective-permute-start | bytes 1769480 | tf_op jit(solution)/shard_map/ppermute | solution.py:49
  149.6 34.1 %collective-permute-start.22 = (bf16[160,3072]{1,0:T(8,128)(2,1)S(1)}, bf16[160,3072]{1,0:T(8,128)(2,1)}, u32[]{:S(2)}, u32[]{:S(2)}) collective-permute-start(bf16[160,3072]{1,0:T(8,128)(2,1)S(1)} %pad_maximum_fusion.6.refs_0_), channel_id=1, source_target_pairs={{0,16},{16,0},{1,17},{17,1},{2,18},{18,2},{3,19},{19,3},{4,20},{20... | collective-permute-start | bytes 2949128 | tf_op jit(solution)/shard_map/ppermute | solution.py:49
  155.5 26.6 %collective-permute-start.25 = (bf16[96,3072]{1,0:T(8,128)(2,1)}, bf16[96,3072]{1,0:T(8,128)(2,1)}, u32[]{:S(2)}, u32[]{:S(2)}) collective-permute-start(bf16[96,3072]{1,0:T(8,128)(2,1)} %slice.119), channel_id=1, source_target_pairs={{0,64},{32,96},{64,0},{96,32},{1,65},{33,97},{65,1},{97,33},{2,66}... | collective-permute-start | bytes 1769480 | tf_op jit(solution)/shard_map/ppermute | solution.py:53
  168.5 19.9 %collective-permute-start.26 = (bf16[96,3072]{1,0:T(8,128)(2,1)}, bf16[96,3072]{1,0:T(8,128)(2,1)S(1)}, u32[]{:S(2)}, u32[]{:S(2)}) collective-permute-start(bf16[96,3072]{1,0:T(8,128)(2,1)} %collective-permute-done.23.refs_2_), channel_id=1, source_target_pairs={{0,16},{16,0},{1,17},{17,1},{2,18},{18,2},{3,19},{19,3},{4,20},{20... | collective-permute-start | bytes 1769480 | tf_op jit(solution)/shard_map/ppermute | solution.py:49
  170.5 38.6 %collective-permute-start.27 = (bf16[96,3072]{1,0:T(8,128)(2,1)}, bf16[96,3072]{1,0:T(8,128)(2,1)}, u32[]{:S(2)}, u32[]{:S(2)}) collective-permute-start(bf16[96,3072]{1,0:T(8,128)(2,1)} %collective-permute-done.24.refs_3_), channel_id=1, source_target_pairs={{0,16},{16,0},{1,17},{17,1},{2,18},{18,2},{3,19},{19,3},{4,20},{20... | collective-permute-start | bytes 1769480 | tf_op jit(solution)/shard_map/ppermute | solution.py:49
  182.1 30.1 %collective-permute-start.28 = (bf16[96,3072]{1,0:T(8,128)(2,1)}, bf16[96,3072]{1,0:T(8,128)(2,1)}, u32[]{:S(2)}, u32[]{:S(2)}) collective-permute-start(bf16[96,3072]{1,0:T(8,128)(2,1)} %collective-permute-done.25.refs_4_), channel_id=1, source_target_pairs={{0,16},{16,0},{1,17},{17,1},{2,18},{18,2},{3,19},{19,3},{4,20},{20... | collective-permute-start | bytes 1769480 | tf_op jit(solution)/shard_map/ppermute | solution.py:49
  184.8 29.5 %collective-permute-start.29 = (bf16[128,3072]{1,0:T(8,128)(2,1)S(1)}, bf16[128,3072]{1,0:T(8,128)(2,1)}, u32[]{:S(2)}, u32[]{:S(2)}) collective-permute-start(bf16[128,3072]{1,0:T(8,128)(2,1)S(1)} %pad_maximum_fusion.10), channel_id=1, source_target_pairs={{0,32},{32,64},{64,96},{96,0},{1,33},{33,65},{65,97},{97,1},{2,34}... | collective-permute-start | bytes 2359304 | tf_op jit(solution)/shard_map/ppermute | solution.py:53
  186.0 32.3 %collective-permute-start.30 = (bf16[128,3072]{1,0:T(8,128)(2,1)S(1)}, bf16[128,3072]{1,0:T(8,128)(2,1)}, u32[]{:S(2)}, u32[]{:S(2)}) collective-permute-start(bf16[128,3072]{1,0:T(8,128)(2,1)S(1)} %pad_maximum_fusion.10), channel_id=1, source_target_pairs={{0,96},{32,0},{64,32},{96,64},{1,97},{33,1},{65,33},{97,65},{2,98}... | collective-permute-start | bytes 2359304 | tf_op jit(solution)/shard_map/ppermute | solution.py:53
  188.4 35.4 %collective-permute-start.31 = (bf16[128,3072]{1,0:T(8,128)(2,1)S(1)}, bf16[128,3072]{1,0:T(8,128)(2,1)}, u32[]{:S(2)}, u32[]{:S(2)}) collective-permute-start(bf16[128,3072]{1,0:T(8,128)(2,1)S(1)} %pad_maximum_fusion.10), channel_id=1, source_target_pairs={{0,64},{32,96},{64,0},{96,32},{1,65},{33,97},{65,1},{97,33},{2,66}... | collective-permute-start | bytes 2359304 | tf_op jit(solution)/shard_map/ppermute | solution.py:53
  209.0 37.8 %collective-permute-start.32 = (bf16[96,3072]{1,0:T(8,128)(2,1)}, bf16[96,3072]{1,0:T(8,128)(2,1)}, u32[]{:S(2)}, u32[]{:S(2)}) collective-permute-start(bf16[96,3072]{1,0:T(8,128)(2,1)} %get-tuple-element.45), channel_id=1, source_target_pairs={{0,96},{32,0},{64,32},{96,64},{1,97},{33,1},{65,33},{97,65},{2,98}... | collective-permute-start | bytes 1769480 | tf_op jit(solution)/shard_map/ppermute | solution.py:53
  212.2 34.7 %collective-permute-start.33 = (bf16[96,3072]{1,0:T(8,128)(2,1)}, bf16[96,3072]{1,0:T(8,128)(2,1)}, u32[]{:S(2)}, u32[]{:S(2)}) collective-permute-start(bf16[96,3072]{1,0:T(8,128)(2,1)} %get-tuple-element.46), channel_id=1, source_target_pairs={{0,32},{32,64},{64,96},{96,0},{1,33},{33,65},{65,97},{97,1},{2,34}... | collective-permute-start | bytes 1769480 | tf_op jit(solution)/shard_map/ppermute | solution.py:53
  214.3 32.6 %collective-permute-start.34 = (bf16[96,3072]{1,0:T(8,128)(2,1)}, bf16[96,3072]{1,0:T(8,128)(2,1)}, u32[]{:S(2)}, u32[]{:S(2)}) collective-permute-start(bf16[96,3072]{1,0:T(8,128)(2,1)} %get-tuple-element.47), channel_id=1, source_target_pairs={{0,64},{32,96},{64,0},{96,32},{1,65},{33,97},{65,1},{97,33},{2,66}... | collective-permute-start | bytes 1769480 | tf_op jit(solution)/shard_map/ppermute | solution.py:53
  218.3 28.5 %collective-permute-start.35 = (bf16[64,3072]{1,0:T(8,128)(2,1)}, bf16[64,3072]{1,0:T(8,128)(2,1)S(1)}, u32[]{:S(2)}, u32[]{:S(2)}) collective-permute-start(bf16[64,3072]{1,0:T(8,128)(2,1)} %get-tuple-element.48), channel_id=1, source_target_pairs={{0,16},{16,0},{1,17},{17,1},{2,18},{18,2},{3,19},{19,3},{4,20},{20... | collective-permute-start | bytes 1179656 | tf_op jit(solution)/shard_map/ppermute | solution.py:49
  248.1 25.0 %collective-permute-start.37 = (bf16[96,3072]{1,0:T(8,128)(2,1)}, bf16[96,3072]{1,0:T(8,128)(2,1)S(1)}, u32[]{:S(2)}, u32[]{:S(2)}) collective-permute-start(bf16[96,3072]{1,0:T(8,128)(2,1)} %get-tuple-element.50), channel_id=1, source_target_pairs={{0,32},{32,64},{64,96},{96,0},{1,33},{33,65},{65,97},{97,1},{2,34}... | collective-permute-start | bytes 1769480 | tf_op jit(solution)/shard_map/ppermute | solution.py:53
  250.1 25.1 %collective-permute-start.36 = (bf16[96,3072]{1,0:T(8,128)(2,1)}, bf16[96,3072]{1,0:T(8,128)(2,1)S(1)}, u32[]{:S(2)}, u32[]{:S(2)}) collective-permute-start(bf16[96,3072]{1,0:T(8,128)(2,1)} %get-tuple-element.49), channel_id=1, source_target_pairs={{0,96},{32,0},{64,32},{96,64},{1,97},{33,1},{65,33},{97,65},{2,98}... | collective-permute-start | bytes 1769480 | tf_op jit(solution)/shard_map/ppermute | solution.py:53
  251.3 27.6 %collective-permute-start.40 = (bf16[192,3072]{1,0:T(8,128)(2,1)}, bf16[192,3072]{1,0:T(8,128)(2,1)S(1)}, u32[]{:S(2)}, u32[]{:S(2)}) collective-permute-start(bf16[192,3072]{1,0:T(8,128)(2,1)} %get-tuple-element.57), channel_id=1, source_target_pairs={{0,16},{16,0},{1,17},{17,1},{2,18},{18,2},{3,19},{19,3},{4,20},{20... | collective-permute-start | bytes 3538952 | tf_op jit(solution)/shard_map/ppermute | solution.py:49
  303.2 21.5 %all-to-all-start.2 = ((bf16[16,8,3840]{2,1,0:T(8,128)(2,1)}), bf16[16,8,3840]{2,1,0:T(8,128)(2,1)S(1)}, u32[]{:S(2)}, u32[]{:S(2)}) async-start(bf16[16,8,3840]{2,1,0:T(8,128)(2,1)} %pad_maximum_fusion.7), calls=%async_computation.2 | async-start | bytes 1966080 | tf_op jit(solution)/shard_map/all_to_all | solution.py:57
  344.1 40.1 %all-to-all-start.3 = ((bf16[64,144,128]{2,1,0:T(8,128)(2,1)}), bf16[64,144,128]{2,1,0:T(8,128)(2,1)}, u32[]{:S(2)}, u32[]{:S(2)}) async-start(bf16[64,144,128]{2,1,0:T(8,128)(2,1)} %shard_map.91), calls=%async_computation.3 | async-start | bytes 4718592 | tf_op jit(solution)/shard_map/all_to_all | solution.py:57
  (58 other events, 664.5 us)

commit v4 on v3

--- a/solution.py
+++ b/solution.py
@@ -121,7 +121,7 @@
         + [[(s, 1, 0)] for s in (1, 3, 2)]
         + [[(s, 0, 1), (s, 1, 1)] for s in (1, 3, 2)]
     )
-    spread = spread_near(earlier)
+    spread = spread_near(earlier, *around_y)
     at = jnp.stack([lax.axis_index("z"), lax.axis_index("yh")]).astype(jnp.int32)
     at = after(at, *spread[1:4])
     anywhere = pl.BlockSpec(memory_space=pl.ANY)
@@ -150,9 +150,9 @@
     return packed[:, :features], extra
 
 
-def spread_near(own):
+def spread_near(own, *earlier):
     one = own[:HALF]
-    own_y = swap(own, "yh")
+    own_y = swap(after(own, *earlier) if earlier else own, "yh")
     return [own, own_y] + [along_z(one, s) for s in (1, 3, 2)]
 
 
@@ -442,7 +442,7 @@
         inner,
         [[(i * h, h)] for i in range(3)]
         + [[(3 * h + (2 * i + r) * rest, rest) for i in range(3)] for r in (0, 1)],
-        (h + 2 * rest) * 3 // 2,
+        (h + 2 * rest) * 3,
     )
     back_main, back_extra = between_experts(collect(near_rows, far_rows))
     cut = EXPERTS * MAIN

time: 395 us -> 393 us (level)
  waiting for transfers between devices: 162 us -> 167 us
  starting transfers between devices: 97.9 us -> 93.3 us
    ppermute x27, waiting for transfers between devices: 53.2 us -> 76.2 us  [along_z(): return lax.ppermute(values, 'z', [(i, (i + shift) % 4) for i in range(4)])]
    ppermute x19, waiting for transfers between devices: 56.9 us -> 44.3 us  [swap(): return lax.ppermute(values, axis, [(0, 1), (1, 0)])]
    all_to_all x4, waiting for transfers between devices: 51.9 us -> 46.1 us  [exchange(): return lax.all_to_all(blocks, axes, split_axis=0, concat_axis=0, tiled=True)]
  transfers between devices with their start and end apart: 50 -> 50, of which waited for: 26 -> 28; matrix products, arithmetic and copies ran while one was open for 9% -> 9% of each run, Pallas kernels for 15% -> 14%
where the time goes in v4:
time: 393 us; the launch traced here: 385 us
  waiting for transfers between devices  167 us (42%)
  starting transfers between devices  93.3 us (24%)
  Pallas kernels  62.8 us (16%)
  other arithmetic  25.6 us (7%)
  matrix products  19.4 us (5%)
  local copies, waits for them, and re-layouts  15.8 us (4%)
    ppermute x27, waiting for transfers between devices, along_z(): return lax.ppermute(values, 'z', [(i, (i + shift) % 4) for i in range(4)])  76.2 us
    all_to_all x4, waiting for transfers between devices, exchange(): return lax.all_to_all(blocks, axes, split_axis=0, concat_axis=0, tiled=True)  46.1 us
    ppermute x19, waiting for transfers between devices, swap(): return lax.ppermute(values, axis, [(0, 1), (1, 0)])  44.3 us
    ppermute x27, starting transfers between devices, along_z(): return lax.ppermute(values, 'z', [(i, (i + shift) % 4) for i in range(4)])  42.9 us
    pallas_call x2, Pallas kernels, experts(): pl.pallas_call(lambda *refs: expert_kernel(counts, pieces_out, tall, *ref...  38.7 us
    ppermute x19, starting transfers between devices, swap(): return lax.ppermute(values, axis, [(0, 1), (1, 0)])  27.5 us
    all_to_all x4, starting transfers between devices, exchange(): return lax.all_to_all(blocks, axes, split_axis=0, concat_axis=0, tiled=True)  22.9 us
    pallas_call x2, Pallas kernels, act_grads(): pl.pallas_call(lambda *refs: act_kernel(counts, *refs), out_shape=jax.Sha...  15.5 us
  transfers between devices with their start and end apart: 50, of which 28 were waited for; matrix products, arithmetic and copies ran while one was open for 9% of the time, Pallas kernels for 14%

profile of v4, /device:TPU:0, one launch (start us, length us, event | category | flops | bytes accessed | tf_op | source)
XLA Modules:
  0.0 385.4 jit_solution(1500971412029645623)
XLA Ops:
  5.6 5.5 %all-to-all-start = ((bf16[16,8,3840]{2,1,0:T(8,128)(2,1)}), bf16[16,8,3840]{2,1,0:T(8,128)(2,1)S(1)}, u32[]{:S(2)}, u32[]{:S(2)}) async-start(bf16[16,8,3840]{2,1,0:T(8,128)(2,1)} %pad_maximum_fusion.3), calls=%async_computation | async-start | bytes 1966080 | tf_op jit(solution)/shard_map/all_to_all | solution.py:57
  19.8 2.9 collective-permute-start
  30.7 4.2 %collective-permute-done.refs_2_ = bf16[1152,128]{1,0:T(8,128)(2,1)} collective-permute-done((bf16[1152,128]{1,0:T(8,128)(2,1)}, bf16[1152,128]{1,0:T(8,128)(2,1)}, u32[]{:S(2)}, u32[]{:S(2)}) %collective-permute-start) | collective-permute-done | bytes 294944 | tf_op jit(solution)/shard_map/ppermute | solution.py:49
  34.9 3.2 collective-permute-done.5.refs_6_
  38.1 3.2 collective-permute-done.6.refs_7_
  53.9 9.6 %collective-permute-done.9.refs_2_ = bf16[96,3072]{1,0:T(8,128)(2,1)} collective-permute-done((bf16[96,3072]{1,0:T(8,128)(2,1)}, bf16[96,3072]{1,0:T(8,128)(2,1)}, u32[]{:S(2)}, u32[]{:S(2)}) %collective-permute-start.9) | collective-permute-done | bytes 589856 | tf_op jit(solution)/shard_map/ppermute | solution.py:53
  70.4 5.3 %collective-permute-done.13.refs_11_ = bf16[1152,128]{1,0:T(8,128)(2,1)} collective-permute-done((bf16[1152,128]{1,0:T(8,128)(2,1)}, bf16[1152,128]{1,0:T(8,128)(2,1)}, u32[]{:S(2)}, u32[]{:S(2)}) %collective-permute-start.13) | collective-permute-done | bytes 294944 | tf_op jit(solution)/shard_map/ppermute | solution.py:53
  75.8 3.9 %shard_map.86 = bf16[8,1152,128]{2,1,0:T(8,128)(2,1)} custom-call(s32[2]{0:T(128)} %pad_add_fusion.refs_0_, bf16[1152,128]{1,0:T(8,128)(2,1)} %constant_dynamic-slice_fusion.2.refs_1_, bf16[1152,128]{1,0:T(8,128)(2,1)} %collective-permute-done.refs_2_, bf16[576,128]{1,0:T(8,128)(2,1)} %collective-permute-done.2.refs_3_, ...), custom_call_target="tpu_custom_call" | custom-call | tf_op jit(solution)/shard_map/pallas_call | solution.py:128
  81.1 3.1 collective-permute-start.16
  100.7 10.4 %collective-permute-done.17.refs_1_ = bf16[96,3072]{1,0:T(8,128)(2,1)} collective-permute-done((bf16[96,3072]{1,0:T(8,128)(2,1)}, bf16[96,3072]{1,0:T(8,128)(2,1)}, u32[]{:S(2)}, u32[]{:S(2)}) %collective-permute-start.17) | collective-permute-done | bytes 589856 | tf_op jit(solution)/shard_map/ppermute | solution.py:49
  111.1 3.2 collective-permute-done.18.refs_3_
  116.0 4.3 %all-to-all-start.1 = ((bf16[16,8,3840]{2,1,0:T(8,128)(2,1)}), bf16[16,8,3840]{2,1,0:T(8,128)(2,1)S(1)}, u32[]{:S(2)}, u32[]{:S(2)}) async-start(bf16[16,8,3840]{2,1,0:T(8,128)(2,1)} %pad_maximum_fusion.5), calls=%async_computation.1 | async-start | bytes 1966080 | tf_op jit(solution)/shard_map/all_to_all | solution.py:57
  125.0 7.5 %shard_map.87.refs_5_ = bf16[608,768]{1,0:T(8,128)(2,1)} custom-call(bf16[160,3072]{1,0:T(8,128)(2,1)} %copy-done.5, bf16[160,3072]{1,0:T(8,128)(2,1)} %collective-permute-done.8.refs_1_, bf16[96,3072]{1,0:T(8,128)(2,1)} %collective-permute-done.9.refs_2_, bf16[96,3072]{1,0:T(8,128)(2,1)} %collective-permute-done.10.refs_3_, ...), custom_call_target="tpu_custom_call" | custom-call | flops 2868903936 | bytes 8454144 | tf_op jit(solution)/shard_map/pallas_call | solution.py:214
  132.5 3.6 all-to-all-done.1
  139.2 8.7 %collective-permute-done.20.refs_2_ = bf16[96,3072]{1,0:T(8,128)(2,1)} collective-permute-done((bf16[96,3072]{1,0:T(8,128)(2,1)}, bf16[96,3072]{1,0:T(8,128)(2,1)}, u32[]{:S(2)}, u32[]{:S(2)}) %collective-permute-start.20) | collective-permute-done | bytes 589856 | tf_op jit(solution)/shard_map/ppermute | solution.py:49
  154.2 8.0 %shard_map.89.refs_6_ = bf16[672,768]{1,0:T(8,128)(2,1)} custom-call(bf16[96,3072]{1,0:T(8,128)(2,1)} %collective-permute-done.16.refs_0_, bf16[96,3072]{1,0:T(8,128)(2,1)} %collective-permute-done.17.refs_1_, bf16[96,3072]{1,0:T(8,128)(2,1)} %collective-permute-done.20.refs_2_, bf16[128,3072]{1,0:T(8,128)(2,1)} %collective-permute-done.18.refs_3_, ...), custom_call_target="tpu_custom_call" | custom-call | flops 3170893824 | bytes 8847360 | tf_op jit(solution)/shard_map/pallas_call | solution.py:214
  162.3 5.8 %collective-permute-done.23.refs_2_ = bf16[96,3072]{1,0:T(8,128)(2,1)} collective-permute-done((bf16[96,3072]{1,0:T(8,128)(2,1)}, bf16[96,3072]{1,0:T(8,128)(2,1)}, u32[]{:S(2)}, u32[]{:S(2)}) %collective-permute-start.23) | collective-permute-done | bytes 589856 | tf_op jit(solution)/shard_map/ppermute | solution.py:53
  169.3 9.5 %collective-permute-done.24.refs_3_ = bf16[96,3072]{1,0:T(8,128)(2,1)} collective-permute-done((bf16[96,3072]{1,0:T(8,128)(2,1)}, bf16[96,3072]{1,0:T(8,128)(2,1)}, u32[]{:S(2)}, u32[]{:S(2)}) %collective-permute-start.24) | collective-permute-done | bytes 589856 | tf_op jit(solution)/shard_map/ppermute | solution.py:53
  184.2 3.0 collective-permute-start.30
  188.9 18.6 %shard_map.88 = (bf16[160,3072]{1,0:T(8,128)(2,1)}, bf16[96,3072]{1,0:T(8,128)(2,1)}, bf16[64,3072]{1,0:T(8,128)(2,1)}, bf16[96,3072]{1,0:T(8,128)(2,1)}, bf16[9...) custom-call(bf16[160,3072]{1,0:T(8,128)(2,1)} %copy-done.4, bf16[160,3072]{1,0:T(8,128)(2,1)} %collective-permute-done.22.refs_1_, ...), custom_call_target="tpu_custom_call" | custom-call | flops 11475615744 | bytes 16908288 | tf_op jit(solution)/shard_map/pallas_call | solution.py:317
  211.7 7.0 %collective-permute-done.29.refs_3_ = bf16[128,3072]{1,0:T(8,128)(2,1)} collective-permute-done((bf16[128,3072]{1,0:T(8,128)(2,1)S(1)}, bf16[128,3072]{1,0:T(8,128)(2,1)}, u32[]{:S(2)}, u32[]{:S(2)}) %collective-permute-start.29) | collective-permute-done | bytes 786464 | tf_op jit(solution)/shard_map/ppermute | solution.py:53
  221.3 20.1 %shard_map.90 = (bf16[96,3072]{1,0:T(8,128)(2,1)}, bf16[96,3072]{1,0:T(8,128)(2,1)}, bf16[96,3072]{1,0:T(8,128)(2,1)}, bf16[192,3072]{1,0:T(8,128)(2,1)}, bf16[192,3072]{1,0:T(8,128)(2,1)}) custom-call(bf16[96,3072]{1,0:T(8,128)(2,1)} %copy-done.32, bf16[96,3072]{1,0:T(8,128)(2,1)} %collective-permute-done.27.refs_1_, ...), custom_call_target="tpu_custom_call" | custom-call | flops 12683575296 | bytes 17694720 | tf_op jit(solution)/shard_map/pallas_call | solution.py:317
  250.2 12.2 %collective-permute-done.38 = bf16[96,3072]{1,0:T(8,128)(2,1)S(1)} collective-permute-done((bf16[96,3072]{1,0:T(8,128)(2,1)}, bf16[96,3072]{1,0:T(8,128)(2,1)S(1)}, u32[]{:S(2)}, u32[]{:S(2)}) %collective-permute-start.38) | collective-permute-done | bytes 589856 | tf_op jit(solution)/shard_map/ppermute | solution.py:53
  262.4 10.7 %collective-permute-done.37 = bf16[96,3072]{1,0:T(8,128)(2,1)S(1)} collective-permute-done((bf16[96,3072]{1,0:T(8,128)(2,1)}, bf16[96,3072]{1,0:T(8,128)(2,1)S(1)}, u32[]{:S(2)}, u32[]{:S(2)}) %collective-permute-start.37) | collective-permute-done | bytes 589856 | tf_op jit(solution)/shard_map/ppermute | solution.py:53
  282.5 9.1 %collective-permute-done.39 = bf16[96,3072]{1,0:T(8,128)(2,1)S(1)} collective-permute-done((bf16[96,3072]{1,0:T(8,128)(2,1)S(1)}, bf16[96,3072]{1,0:T(8,128)(2,1)S(1)}, u32[]{:S(2)}, u32[]{:S(2)}) %collective-permute-start.39) | collective-permute-done | bytes 589856 | tf_op jit(solution)/shard_map/ppermute | solution.py:49
  293.5 3.6 collective-permute-done.42
  301.1 4.9 %all-to-all-start.2 = ((bf16[16,8,3840]{2,1,0:T(8,128)(2,1)}), bf16[16,8,3840]{2,1,0:T(8,128)(2,1)S(1)}, u32[]{:S(2)}, u32[]{:S(2)}) async-start(bf16[16,8,3840]{2,1,0:T(8,128)(2,1)} %pad_maximum_fusion.7), calls=%async_computation.2 | async-start | bytes 1966080 | tf_op jit(solution)/shard_map/all_to_all | solution.py:57
  307.4 14.4 %all-to-all-done.2 = bf16[16,8,3840]{2,1,0:T(8,128)(2,1)S(1)} async-done(((bf16[16,8,3840]{2,1,0:T(8,128)(2,1)}), bf16[16,8,3840]{2,1,0:T(8,128)(2,1)S(1)}, u32[]{:S(2)}, u32[]{:S(2)}) %all-to-all-start.2) | async-done | bytes 983072 | tf_op jit(solution)/shard_map/all_to_all | solution.py:57
  336.5 4.6 %shard_map.91 = bf16[64,144,128]{2,1,0:T(8,128)(2,1)} custom-call(s32[1]{0:T(128)} %bitcast.35.refs_0_, bf16[256,3072]{1,0:T(8,128)(2,1)S(1)} %pad_maximum_fusion.1.refs_1_, bf16[256,3072]{1,0:T(8,128)(2,1)S(1)} %pad_maximum_fusion.2.refs_2_, bf16[256,768]{1,0:T(8,128)(2,1)S(1)} %pad_maximum_fusion.11.refs_3_), custom_call_target="tpu_custom_call" | custom-call | flops 1207959552 | bytes 8388608 | tf_op jit(solution)/shard_map/pallas_call | solution.py:367
  341.2 8.2 %all-to-all-start.3 = ((bf16[64,144,128]{2,1,0:T(8,128)(2,1)}), bf16[64,144,128]{2,1,0:T(8,128)(2,1)}, u32[]{:S(2)}, u32[]{:S(2)}) async-start(bf16[64,144,128]{2,1,0:T(8,128)(2,1)} %shard_map.91), calls=%async_computation.3 | async-start | bytes 4718592 | tf_op jit(solution)/shard_map/all_to_all | solution.py:57
  349.4 3.3 fusion.79
  354.2 28.1 %all-to-all-done.3 = bf16[64,144,128]{2,1,0:T(8,128)(2,1)} async-done(((bf16[64,144,128]{2,1,0:T(8,128)(2,1)}), bf16[64,144,128]{2,1,0:T(8,128)(2,1)}, u32[]{:S(2)}, u32[]{:S(2)}) %all-to-all-start.3) | async-done | bytes 2359328 | tf_op jit(solution)/shard_map/all_to_all | solution.py:57
  (227 shorter events, 133.6 us)
Async XLA Ops:
  5.6 23.2 %all-to-all-start = ((bf16[16,8,3840]{2,1,0:T(8,128)(2,1)}), bf16[16,8,3840]{2,1,0:T(8,128)(2,1)S(1)}, u32[]{:S(2)}, u32[]{:S(2)}) async-start(bf16[16,8,3840]{2,1,0:T(8,128)(2,1)} %pad_maximum_fusion.3), calls=%async_computation | async-start | bytes 1966080 | tf_op jit(solution)/shard_map/all_to_all | solution.py:57
  12.0 22.9 %collective-permute-start.1 = (bf16[128,3072]{1,0:T(8,128)(2,1)S(1)}, bf16[128,3072]{1,0:T(8,128)(2,1)}, u32[]{:S(2)}, u32[]{:S(2)}) collective-permute-start(bf16[128,3072]{1,0:T(8,128)(2,1)S(1)} %fusion.13), channel_id=1, source_target_pairs={{0,1},{1,0},{2,3},{3,2},{4,5},{5,4},{6,7},{7,6},{8,9},{9,8},{10,11... | collective-permute-start | bytes 2359304 | tf_op jit(solution)/shard_map/ppermute | solution.py:49
  43.5 24.5 %collective-permute-start.8 = (bf16[160,3072]{1,0:T(8,128)(2,1)S(1)}, bf16[160,3072]{1,0:T(8,128)(2,1)}, u32[]{:S(2)}, u32[]{:S(2)}) collective-permute-start(bf16[160,3072]{1,0:T(8,128)(2,1)S(1)} %pad_maximum_fusion.4.refs_0_), channel_id=1, source_target_pairs={{0,16},{16,0},{1,17},{17,1},{2,18},{18,2},{3,19},{19,3},{4,20},{20... | collective-permute-start | bytes 2949128 | tf_op jit(solution)/shard_map/ppermute | solution.py:49
  47.6 18.7 %collective-permute-start.10 = (bf16[96,3072]{1,0:T(8,128)(2,1)}, bf16[96,3072]{1,0:T(8,128)(2,1)}, u32[]{:S(2)}, u32[]{:S(2)}) collective-permute-start(bf16[96,3072]{1,0:T(8,128)(2,1)} %slice.104), channel_id=1, source_target_pairs={{0,96},{32,0},{64,32},{96,64},{1,97},{33,1},{65,33},{97,65},{2,98}... | collective-permute-start | bytes 1769480 | tf_op jit(solution)/shard_map/ppermute | solution.py:53
  50.6 18.4 %collective-permute-start.11 = (bf16[1152,128]{1,0:T(8,128)(2,1)}, bf16[1152,128]{1,0:T(8,128)(2,1)S(1)}, u32[]{:S(2)}, u32[]{:S(2)}) collective-permute-start(bf16[1152,128]{1,0:T(8,128)(2,1)} %pad_maximum_fusion.12), channel_id=1, source_target_pairs={{0,32},{32,64},{64,96},{96,0},{1,33},{33,65},{65,97},{97,1},{2,34}... | collective-permute-start | bytes 884744 | tf_op jit(solution)/shard_map/ppermute | solution.py:53
  51.3 19.1 %collective-permute-start.12 = (bf16[1152,128]{1,0:T(8,128)(2,1)}, bf16[1152,128]{1,0:T(8,128)(2,1)S(1)}, u32[]{:S(2)}, u32[]{:S(2)}) collective-permute-start(bf16[1152,128]{1,0:T(8,128)(2,1)} %pad_maximum_fusion.12), channel_id=1, source_target_pairs={{0,96},{32,0},{64,32},{96,64},{1,97},{33,1},{65,33},{97,65},{2,98}... | collective-permute-start | bytes 884744 | tf_op jit(solution)/shard_map/ppermute | solution.py:53
  79.8 20.8 %collective-permute-start.15 = (bf16[96,3072]{1,0:T(8,128)(2,1)}, bf16[96,3072]{1,0:T(8,128)(2,1)}, u32[]{:S(2)}, u32[]{:S(2)}) collective-permute-start(bf16[96,3072]{1,0:T(8,128)(2,1)} %slice.104), channel_id=1, source_target_pairs={{0,64},{32,96},{64,0},{96,32},{1,65},{33,97},{65,1},{97,33},{2,66}... | collective-permute-start | bytes 1769480 | tf_op jit(solution)/shard_map/ppermute | solution.py:53
  81.1 19.5 %collective-permute-start.16 = (bf16[96,3072]{1,0:T(8,128)(2,1)}, bf16[96,3072]{1,0:T(8,128)(2,1)}, u32[]{:S(2)}, u32[]{:S(2)}) collective-permute-start(bf16[96,3072]{1,0:T(8,128)(2,1)} %collective-permute-done.9.refs_2_), channel_id=1, source_target_pairs={{0,16},{16,0},{1,17},{17,1},{2,18},{18,2},{3,19},{19,3},{4,20},{20... | collective-permute-start | bytes 1769480 | tf_op jit(solution)/shard_map/ppermute | solution.py:49
  84.3 26.8 %collective-permute-start.17 = (bf16[96,3072]{1,0:T(8,128)(2,1)}, bf16[96,3072]{1,0:T(8,128)(2,1)}, u32[]{:S(2)}, u32[]{:S(2)}) collective-permute-start(bf16[96,3072]{1,0:T(8,128)(2,1)} %collective-permute-done.10.refs_3_), channel_id=1, source_target_pairs={{0,16},{16,0},{1,17},{17,1},{2,18},{18,2},{3,19},{19,3},{4,20},{20... | collective-permute-start | bytes 1769480 | tf_op jit(solution)/shard_map/ppermute | solution.py:49
  86.7 27.6 %collective-permute-start.18 = (bf16[128,3072]{1,0:T(8,128)(2,1)}, bf16[128,3072]{1,0:T(8,128)(2,1)}, u32[]{:S(2)}, u32[]{:S(2)}) collective-permute-start(bf16[128,3072]{1,0:T(8,128)(2,1)} %pad_maximum_fusion.9), channel_id=1, source_target_pairs={{0,32},{32,64},{64,96},{96,0},{1,33},{33,65},{65,97},{97,1},{2,34}... | collective-permute-start | bytes 2359304 | tf_op jit(solution)/shard_map/ppermute | solution.py:53
  88.5 25.9 %collective-permute-start.19 = (bf16[128,3072]{1,0:T(8,128)(2,1)}, bf16[128,3072]{1,0:T(8,128)(2,1)}, u32[]{:S(2)}, u32[]{:S(2)}) collective-permute-start(bf16[128,3072]{1,0:T(8,128)(2,1)} %pad_maximum_fusion.9), channel_id=1, source_target_pairs={{0,96},{32,0},{64,32},{96,64},{1,97},{33,1},{65,33},{97,65},{2,98}... | collective-permute-start | bytes 2359304 | tf_op jit(solution)/shard_map/ppermute | solution.py:53
  116.0 20.1 %all-to-all-start.1 = ((bf16[16,8,3840]{2,1,0:T(8,128)(2,1)}), bf16[16,8,3840]{2,1,0:T(8,128)(2,1)S(1)}, u32[]{:S(2)}, u32[]{:S(2)}) async-start(bf16[16,8,3840]{2,1,0:T(8,128)(2,1)} %pad_maximum_fusion.5), calls=%async_computation.1 | async-start | bytes 1966080 | tf_op jit(solution)/shard_map/all_to_all | solution.py:57
  120.3 27.5 %collective-permute-start.21 = (bf16[128,3072]{1,0:T(8,128)(2,1)}, bf16[128,3072]{1,0:T(8,128)(2,1)}, u32[]{:S(2)}, u32[]{:S(2)}) collective-permute-start(bf16[128,3072]{1,0:T(8,128)(2,1)} %pad_maximum_fusion.9), channel_id=1, source_target_pairs={{0,64},{32,96},{64,0},{96,32},{1,65},{33,97},{65,1},{97,33},{2,66}... | collective-permute-start | bytes 2359304 | tf_op jit(solution)/shard_map/ppermute | solution.py:53
  122.2 25.7 %collective-permute-start.20 = (bf16[96,3072]{1,0:T(8,128)(2,1)}, bf16[96,3072]{1,0:T(8,128)(2,1)}, u32[]{:S(2)}, u32[]{:S(2)}) collective-permute-start(bf16[96,3072]{1,0:T(8,128)(2,1)} %collective-permute-done.15.refs_4_), channel_id=1, source_target_pairs={{0,16},{16,0},{1,17},{17,1},{2,18},{18,2},{3,19},{19,3},{4,20},{20... | collective-permute-start | bytes 1769480 | tf_op jit(solution)/shard_map/ppermute | solution.py:49
  147.9 34.5 %collective-permute-start.22 = (bf16[160,3072]{1,0:T(8,128)(2,1)S(1)}, bf16[160,3072]{1,0:T(8,128)(2,1)}, u32[]{:S(2)}, u32[]{:S(2)}) collective-permute-start(bf16[160,3072]{1,0:T(8,128)(2,1)S(1)} %pad_maximum_fusion.6.refs_0_), channel_id=1, source_target_pairs={{0,16},{16,0},{1,17},{17,1},{2,18},{18,2},{3,19},{19,3},{4,20},{20... | collective-permute-start | bytes 2949128 | tf_op jit(solution)/shard_map/ppermute | solution.py:49
  151.6 27.2 %collective-permute-start.24 = (bf16[96,3072]{1,0:T(8,128)(2,1)}, bf16[96,3072]{1,0:T(8,128)(2,1)}, u32[]{:S(2)}, u32[]{:S(2)}) collective-permute-start(bf16[96,3072]{1,0:T(8,128)(2,1)} %slice.119), channel_id=1, source_target_pairs={{0,96},{32,0},{64,32},{96,64},{1,97},{33,1},{65,33},{97,65},{2,98}... | collective-permute-start | bytes 1769480 | tf_op jit(solution)/shard_map/ppermute | solution.py:53
  153.7 26.8 %collective-permute-start.25 = (bf16[96,3072]{1,0:T(8,128)(2,1)}, bf16[96,3072]{1,0:T(8,128)(2,1)}, u32[]{:S(2)}, u32[]{:S(2)}) collective-permute-start(bf16[96,3072]{1,0:T(8,128)(2,1)} %slice.119), channel_id=1, source_target_pairs={{0,64},{32,96},{64,0},{96,32},{1,65},{33,97},{65,1},{97,33},{2,66}... | collective-permute-start | bytes 1769480 | tf_op jit(solution)/shard_map/ppermute | solution.py:53
  168.1 19.1 %collective-permute-start.26 = (bf16[96,3072]{1,0:T(8,128)(2,1)}, bf16[96,3072]{1,0:T(8,128)(2,1)S(1)}, u32[]{:S(2)}, u32[]{:S(2)}) collective-permute-start(bf16[96,3072]{1,0:T(8,128)(2,1)} %collective-permute-done.23.refs_2_), channel_id=1, source_target_pairs={{0,16},{16,0},{1,17},{17,1},{2,18},{18,2},{3,19},{19,3},{4,20},{20... | collective-permute-start | bytes 1769480 | tf_op jit(solution)/shard_map/ppermute | solution.py:49
  178.8 28.6 %collective-permute-start.27 = (bf16[96,3072]{1,0:T(8,128)(2,1)}, bf16[96,3072]{1,0:T(8,128)(2,1)}, u32[]{:S(2)}, u32[]{:S(2)}) collective-permute-start(bf16[96,3072]{1,0:T(8,128)(2,1)} %collective-permute-done.24.refs_3_), channel_id=1, source_target_pairs={{0,16},{16,0},{1,17},{17,1},{2,18},{18,2},{3,19},{19,3},{4,20},{20... | collective-permute-start | bytes 1769480 | tf_op jit(solution)/shard_map/ppermute | solution.py:49
  180.5 30.4 %collective-permute-start.28 = (bf16[96,3072]{1,0:T(8,128)(2,1)}, bf16[96,3072]{1,0:T(8,128)(2,1)}, u32[]{:S(2)}, u32[]{:S(2)}) collective-permute-start(bf16[96,3072]{1,0:T(8,128)(2,1)} %collective-permute-done.25.refs_4_), channel_id=1, source_target_pairs={{0,16},{16,0},{1,17},{17,1},{2,18},{18,2},{3,19},{19,3},{4,20},{20... | collective-permute-start | bytes 1769480 | tf_op jit(solution)/shard_map/ppermute | solution.py:49
  183.4 35.3 %collective-permute-start.29 = (bf16[128,3072]{1,0:T(8,128)(2,1)S(1)}, bf16[128,3072]{1,0:T(8,128)(2,1)}, u32[]{:S(2)}, u32[]{:S(2)}) collective-permute-start(bf16[128,3072]{1,0:T(8,128)(2,1)S(1)} %pad_maximum_fusion.10), channel_id=1, source_target_pairs={{0,32},{32,64},{64,96},{96,0},{1,33},{33,65},{65,97},{97,1},{2,34}... | collective-permute-start | bytes 2359304 | tf_op jit(solution)/shard_map/ppermute | solution.py:53
  184.2 34.5 %collective-permute-start.30 = (bf16[128,3072]{1,0:T(8,128)(2,1)S(1)}, bf16[128,3072]{1,0:T(8,128)(2,1)}, u32[]{:S(2)}, u32[]{:S(2)}) collective-permute-start(bf16[128,3072]{1,0:T(8,128)(2,1)S(1)} %pad_maximum_fusion.10), channel_id=1, source_target_pairs={{0,96},{32,0},{64,32},{96,64},{1,97},{33,1},{65,33},{97,65},{2,98}... | collective-permute-start | bytes 2359304 | tf_op jit(solution)/shard_map/ppermute | solution.py:53
  187.3 34.1 %collective-permute-start.31 = (bf16[128,3072]{1,0:T(8,128)(2,1)S(1)}, bf16[128,3072]{1,0:T(8,128)(2,1)}, u32[]{:S(2)}, u32[]{:S(2)}) collective-permute-start(bf16[128,3072]{1,0:T(8,128)(2,1)S(1)} %pad_maximum_fusion.10), channel_id=1, source_target_pairs={{0,64},{32,96},{64,0},{96,32},{1,65},{33,97},{65,1},{97,33},{2,66}... | collective-permute-start | bytes 2359304 | tf_op jit(solution)/shard_map/ppermute | solution.py:53
  207.5 36.2 %collective-permute-start.32 = (bf16[96,3072]{1,0:T(8,128)(2,1)}, bf16[96,3072]{1,0:T(8,128)(2,1)}, u32[]{:S(2)}, u32[]{:S(2)}) collective-permute-start(bf16[96,3072]{1,0:T(8,128)(2,1)} %get-tuple-element.47), channel_id=1, source_target_pairs={{0,96},{32,0},{64,32},{96,64},{1,97},{33,1},{65,33},{97,65},{2,98}... | collective-permute-start | bytes 1769480 | tf_op jit(solution)/shard_map/ppermute | solution.py:53
  210.9 33.5 %collective-permute-start.33 = (bf16[96,3072]{1,0:T(8,128)(2,1)}, bf16[96,3072]{1,0:T(8,128)(2,1)}, u32[]{:S(2)}, u32[]{:S(2)}) collective-permute-start(bf16[96,3072]{1,0:T(8,128)(2,1)} %get-tuple-element.48), channel_id=1, source_target_pairs={{0,32},{32,64},{64,96},{96,0},{1,33},{33,65},{65,97},{97,1},{2,34}... | collective-permute-start | bytes 1769480 | tf_op jit(solution)/shard_map/ppermute | solution.py:53
  218.7 25.7 %collective-permute-start.34 = (bf16[96,3072]{1,0:T(8,128)(2,1)}, bf16[96,3072]{1,0:T(8,128)(2,1)}, u32[]{:S(2)}, u32[]{:S(2)}) collective-permute-start(bf16[96,3072]{1,0:T(8,128)(2,1)} %get-tuple-element.49), channel_id=1, source_target_pairs={{0,64},{32,96},{64,0},{96,32},{1,65},{33,97},{65,1},{97,33},{2,66}... | collective-permute-start | bytes 1769480 | tf_op jit(solution)/shard_map/ppermute | solution.py:53
  218.7 22.8 %collective-permute-start.35 = (bf16[64,3072]{1,0:T(8,128)(2,1)}, bf16[64,3072]{1,0:T(8,128)(2,1)S(1)}, u32[]{:S(2)}, u32[]{:S(2)}) collective-permute-start(bf16[64,3072]{1,0:T(8,128)(2,1)} %get-tuple-element.50), channel_id=1, source_target_pairs={{0,16},{16,0},{1,17},{17,1},{2,18},{18,2},{3,19},{19,3},{4,20},{20... | collective-permute-start | bytes 1179656 | tf_op jit(solution)/shard_map/ppermute | solution.py:49
  245.6 27.6 %collective-permute-start.37 = (bf16[96,3072]{1,0:T(8,128)(2,1)}, bf16[96,3072]{1,0:T(8,128)(2,1)S(1)}, u32[]{:S(2)}, u32[]{:S(2)}) collective-permute-start(bf16[96,3072]{1,0:T(8,128)(2,1)} %get-tuple-element.52), channel_id=1, source_target_pairs={{0,32},{32,64},{64,96},{96,0},{1,33},{33,65},{65,97},{97,1},{2,34}... | collective-permute-start | bytes 1769480 | tf_op jit(solution)/shard_map/ppermute | solution.py:53
  248.2 25.4 %collective-permute-start.36 = (bf16[96,3072]{1,0:T(8,128)(2,1)}, bf16[96,3072]{1,0:T(8,128)(2,1)S(1)}, u32[]{:S(2)}, u32[]{:S(2)}) collective-permute-start(bf16[96,3072]{1,0:T(8,128)(2,1)} %get-tuple-element.51), channel_id=1, source_target_pairs={{0,96},{32,0},{64,32},{96,64},{1,97},{33,1},{65,33},{97,65},{2,98}... | collective-permute-start | bytes 1769480 | tf_op jit(solution)/shard_map/ppermute | solution.py:53
  248.8 27.9 %collective-permute-start.40 = (bf16[192,3072]{1,0:T(8,128)(2,1)}, bf16[192,3072]{1,0:T(8,128)(2,1)S(1)}, u32[]{:S(2)}, u32[]{:S(2)}) collective-permute-start(bf16[192,3072]{1,0:T(8,128)(2,1)} %get-tuple-element.59), channel_id=1, source_target_pairs={{0,16},{16,0},{1,17},{17,1},{2,18},{18,2},{3,19},{19,3},{4,20},{20... | collective-permute-start | bytes 3538952 | tf_op jit(solution)/shard_map/ppermute | solution.py:49
  301.1 20.7 %all-to-all-start.2 = ((bf16[16,8,3840]{2,1,0:T(8,128)(2,1)}), bf16[16,8,3840]{2,1,0:T(8,128)(2,1)S(1)}, u32[]{:S(2)}, u32[]{:S(2)}) async-start(bf16[16,8,3840]{2,1,0:T(8,128)(2,1)} %pad_maximum_fusion.7), calls=%async_computation.2 | async-start | bytes 1966080 | tf_op jit(solution)/shard_map/all_to_all | solution.py:57
  341.2 41.2 %all-to-all-start.3 = ((bf16[64,144,128]{2,1,0:T(8,128)(2,1)}), bf16[64,144,128]{2,1,0:T(8,128)(2,1)}, u32[]{:S(2)}, u32[]{:S(2)}) async-start(bf16[64,144,128]{2,1,0:T(8,128)(2,1)} %shard_map.91), calls=%async_computation.3 | async-start | bytes 4718592 | tf_op jit(solution)/shard_map/all_to_all | solution.py:57
  (53 other events, 595.8 us)

commit v5 on v4

--- a/solution.py
+++ b/solution.py
@@ -168,14 +168,12 @@
     kept, one_y, two_y, *one_z = near
     early = [along_z(block, -s) for block, s in zip(one_z, (1, 3, 2))]
     early_y = swap(two_y, "yh")
-    *one_yz, two_z, two_yz = far
-    (*one_yz, two_yz), early, early_y = lax.optimization_barrier(([*one_yz, two_yz], early, early_y))
+    one_yz, two_z, two_yz = far[:3], far[3:6], far[6:]
+    one_yz, two_yz, early, early_y = lax.optimization_barrier((one_yz, two_yz, early, early_y))
+    swapped = [swap(block, "yh") for block in two_yz]
     late = [along_z(block, -s) for block, s in zip(one_yz, (1, 3, 2))]
-    swapped = swap(two_yz, "yh")
+    back = [along_z(add_round(two_z[i], swapped[i]), -s) for i, s in enumerate((1, 3, 2))]
     across = swap(add_round(one_y, *late), "yh")
-    pairs = add_round(two_z, swapped)
-    rest = kept.shape[0] - HALF
-    back = [along_z(pairs[i * rest : (i + 1) * rest], -s) for i, s in enumerate((1, 3, 2))]
     one = add_round(kept[:HALF], across, *early)
     two = add_round(kept[HALF:], early_y, *back)
     return jnp.concatenate([one, two], axis=0)
@@ -441,7 +439,7 @@
         far_acts,
         inner,
         [[(i * h, h)] for i in range(3)]
-        + [[(3 * h + (2 * i + r) * rest, rest) for i in range(3)] for r in (0, 1)],
+        + [[(3 * h + (2 * i + r) * rest, rest)] for r in (0, 1) for i in range(3)],
         (h + 2 * rest) * 3,
     )
     back_main, back_extra = between_experts(collect(near_rows, far_rows))

time: 393 us -> 393 us (level)
  waiting for transfers between devices: 167 us -> 162 us
    ppermute x27, waiting for transfers between devices: 76.2 us -> 65 us  [along_z(): return lax.ppermute(values, 'z', [(i, (i + shift) % 4) for i in range(4)])]
    ppermute x19 -> x21, waiting for transfers between devices: 44.3 us -> 50.8 us  [swap(): return lax.ppermute(values, axis, [(0, 1), (1, 0)])]
    ppermute x19 -> x21, starting transfers between devices: 27.5 us -> 29.4 us  [swap(): return lax.ppermute(values, axis, [(0, 1), (1, 0)])]
  transfers between devices with their start and end apart: 50 -> 52, of which waited for: 28 -> 31; matrix products, arithmetic and copies ran while one was open for 9% -> 9% of each run, Pallas kernels for 14% -> 14%
where the time goes in v5:
time: 393 us; the launch traced here: 386 us
  waiting for transfers between devices  162 us (41%)
  starting transfers between devices  97.1 us (25%)
  Pallas kernels  62.7 us (16%)
  other arithmetic  28.6 us (7%)
  matrix products  19.4 us (5%)
  local copies, waits for them, and re-layouts  14.2 us (4%)
    ppermute x27, waiting for transfers between devices, along_z(): return lax.ppermute(values, 'z', [(i, (i + shift) % 4) for i in range(4)])  65 us
    ppermute x21, waiting for transfers between devices, swap(): return lax.ppermute(values, axis, [(0, 1), (1, 0)])  50.8 us
    all_to_all x4, waiting for transfers between devices, exchange(): return lax.all_to_all(blocks, axes, split_axis=0, concat_axis=0, tiled=True)  46.1 us
    ppermute x27, starting transfers between devices, along_z(): return lax.ppermute(values, 'z', [(i, (i + shift) % 4) for i in range(4)])  44.7 us
    pallas_call x2, Pallas kernels, experts(): pl.pallas_call(lambda *refs: expert_kernel(counts, pieces_out, tall, *ref...  38.7 us
    ppermute x21, starting transfers between devices, swap(): return lax.ppermute(values, axis, [(0, 1), (1, 0)])  29.4 us
    all_to_all x4, starting transfers between devices, exchange(): return lax.all_to_all(blocks, axes, split_axis=0, concat_axis=0, tiled=True)  23 us
    pallas_call x2, Pallas kernels, act_grads(): pl.pallas_call(lambda *refs: act_kernel(counts, *refs), out_shape=jax.Sha...  15.4 us
  transfers between devices with their start and end apart: 52, of which 31 were waited for; matrix products, arithmetic and copies ran while one was open for 9% of the time, Pallas kernels for 14%

profile of v5, /device:TPU:0, one launch (start us, length us, event | category | flops | bytes accessed | tf_op | source)
XLA Modules:
  0.0 385.9 jit_solution(3782508778193693024)
XLA Ops:
  5.6 5.5 %all-to-all-start = ((bf16[16,8,3840]{2,1,0:T(8,128)(2,1)}), bf16[16,8,3840]{2,1,0:T(8,128)(2,1)S(1)}, u32[]{:S(2)}, u32[]{:S(2)}) async-start(bf16[16,8,3840]{2,1,0:T(8,128)(2,1)} %pad_maximum_fusion.3), calls=%async_computation | async-start | bytes 1966080 | tf_op jit(solution)/shard_map/all_to_all | solution.py:57
  30.7 4.2 %collective-permute-done.refs_2_ = bf16[1152,128]{1,0:T(8,128)(2,1)} collective-permute-done((bf16[1152,128]{1,0:T(8,128)(2,1)}, bf16[1152,128]{1,0:T(8,128)(2,1)}, u32[]{:S(2)}, u32[]{:S(2)}) %collective-permute-start) | collective-permute-done | bytes 294944 | tf_op jit(solution)/shard_map/ppermute | solution.py:49
  53.8 9.6 %collective-permute-done.9.refs_2_ = bf16[96,3072]{1,0:T(8,128)(2,1)} collective-permute-done((bf16[96,3072]{1,0:T(8,128)(2,1)}, bf16[96,3072]{1,0:T(8,128)(2,1)}, u32[]{:S(2)}, u32[]{:S(2)}) %collective-permute-start.9) | collective-permute-done | bytes 589856 | tf_op jit(solution)/shard_map/ppermute | solution.py:53
  70.4 5.3 %collective-permute-done.13.refs_11_ = bf16[1152,128]{1,0:T(8,128)(2,1)} collective-permute-done((bf16[1152,128]{1,0:T(8,128)(2,1)}, bf16[1152,128]{1,0:T(8,128)(2,1)}, u32[]{:S(2)}, u32[]{:S(2)}) %collective-permute-start.13) | collective-permute-done | bytes 294944 | tf_op jit(solution)/shard_map/ppermute | solution.py:53
  75.7 3.9 %shard_map.86 = bf16[8,1152,128]{2,1,0:T(8,128)(2,1)} custom-call(s32[2]{0:T(128)} %pad_add_fusion.refs_0_, bf16[1152,128]{1,0:T(8,128)(2,1)} %constant_dynamic-slice_fusion.2.refs_1_, bf16[1152,128]{1,0:T(8,128)(2,1)} %collective-permute-done.refs_2_, bf16[576,128]{1,0:T(8,128)(2,1)} %collective-permute-done.2.refs_3_, ...), custom_call_target="tpu_custom_call" | custom-call | tf_op jit(solution)/shard_map/pallas_call | solution.py:128
  100.7 10.4 %collective-permute-done.17.refs_1_ = bf16[96,3072]{1,0:T(8,128)(2,1)} collective-permute-done((bf16[96,3072]{1,0:T(8,128)(2,1)}, bf16[96,3072]{1,0:T(8,128)(2,1)}, u32[]{:S(2)}, u32[]{:S(2)}) %collective-permute-start.17) | collective-permute-done | bytes 589856 | tf_op jit(solution)/shard_map/ppermute | solution.py:49
  111.1 3.2 collective-permute-done.18.refs_3_
  115.9 4.3 %all-to-all-start.1 = ((bf16[16,8,3840]{2,1,0:T(8,128)(2,1)}), bf16[16,8,3840]{2,1,0:T(8,128)(2,1)S(1)}, u32[]{:S(2)}, u32[]{:S(2)}) async-start(bf16[16,8,3840]{2,1,0:T(8,128)(2,1)} %pad_maximum_fusion.5), calls=%async_computation.1 | async-start | bytes 1966080 | tf_op jit(solution)/shard_map/all_to_all | solution.py:57
  124.9 7.5 %shard_map.87.refs_5_ = bf16[608,768]{1,0:T(8,128)(2,1)} custom-call(bf16[160,3072]{1,0:T(8,128)(2,1)} %copy-done.5, bf16[160,3072]{1,0:T(8,128)(2,1)} %collective-permute-done.8.refs_1_, bf16[96,3072]{1,0:T(8,128)(2,1)} %collective-permute-done.9.refs_2_, bf16[96,3072]{1,0:T(8,128)(2,1)} %collective-permute-done.10.refs_3_, ...), custom_call_target="tpu_custom_call" | custom-call | flops 2868903936 | bytes 8454144 | tf_op jit(solution)/shard_map/pallas_call | solution.py:212
  132.4 3.6 all-to-all-done.1
  139.1 8.7 %collective-permute-done.20.refs_2_ = bf16[96,3072]{1,0:T(8,128)(2,1)} collective-permute-done((bf16[96,3072]{1,0:T(8,128)(2,1)}, bf16[96,3072]{1,0:T(8,128)(2,1)}, u32[]{:S(2)}, u32[]{:S(2)}) %collective-permute-start.20) | collective-permute-done | bytes 589856 | tf_op jit(solution)/shard_map/ppermute | solution.py:49
  154.1 8.0 %shard_map.89.refs_6_ = bf16[672,768]{1,0:T(8,128)(2,1)} custom-call(bf16[96,3072]{1,0:T(8,128)(2,1)} %collective-permute-done.16.refs_0_, bf16[96,3072]{1,0:T(8,128)(2,1)} %collective-permute-done.17.refs_1_, bf16[96,3072]{1,0:T(8,128)(2,1)} %collective-permute-done.20.refs_2_, bf16[128,3072]{1,0:T(8,128)(2,1)} %collective-permute-done.18.refs_3_, ...), custom_call_target="tpu_custom_call" | custom-call | flops 3170893824 | bytes 8847360 | tf_op jit(solution)/shard_map/pallas_call | solution.py:212
  162.1 5.9 %collective-permute-done.23.refs_2_ = bf16[96,3072]{1,0:T(8,128)(2,1)} collective-permute-done((bf16[96,3072]{1,0:T(8,128)(2,1)}, bf16[96,3072]{1,0:T(8,128)(2,1)}, u32[]{:S(2)}, u32[]{:S(2)}) %collective-permute-start.23) | collective-permute-done | bytes 589856 | tf_op jit(solution)/shard_map/ppermute | solution.py:53
  169.2 9.5 %collective-permute-done.24.refs_3_ = bf16[96,3072]{1,0:T(8,128)(2,1)} collective-permute-done((bf16[96,3072]{1,0:T(8,128)(2,1)}, bf16[96,3072]{1,0:T(8,128)(2,1)}, u32[]{:S(2)}, u32[]{:S(2)}) %collective-permute-start.24) | collective-permute-done | bytes 589856 | tf_op jit(solution)/shard_map/ppermute | solution.py:53
  188.8 18.5 %shard_map.88 = (bf16[160,3072]{1,0:T(8,128)(2,1)}, bf16[96,3072]{1,0:T(8,128)(2,1)}, bf16[64,3072]{1,0:T(8,128)(2,1)}, bf16[96,3072]{1,0:T(8,128)(2,1)}, bf16[9...) custom-call(bf16[160,3072]{1,0:T(8,128)(2,1)} %copy-done.4, bf16[160,3072]{1,0:T(8,128)(2,1)} %collective-permute-done.22.refs_1_, ...), custom_call_target="tpu_custom_call" | custom-call | flops 11475615744 | bytes 16908288 | tf_op jit(solution)/shard_map/pallas_call | solution.py:315
  211.6 7.0 %collective-permute-done.29.refs_3_ = bf16[128,3072]{1,0:T(8,128)(2,1)} collective-permute-done((bf16[128,3072]{1,0:T(8,128)(2,1)S(1)}, bf16[128,3072]{1,0:T(8,128)(2,1)}, u32[]{:S(2)}, u32[]{:S(2)}) %collective-permute-start.29) | collective-permute-done | bytes 786464 | tf_op jit(solution)/shard_map/ppermute | solution.py:53
  221.2 20.2 %shard_map.90 = (bf16[96,3072]{1,0:T(8,128)(2,1)}, bf16[96,3072]{1,0:T(8,128)(2,1)}, bf16[96,3072]{1,0:T(8,128)(2,1)}, bf16[64,3072]{1,0:T(8,128)(2,1)}, bf16[64...) custom-call(bf16[96,3072]{1,0:T(8,128)(2,1)} %copy-done.31, ...), custom_call_target="tpu_custom_call" | custom-call | flops 12683575296 | bytes 17694720 | tf_op jit(solution)/shard_map/pallas_call | solution.py:315
  253.0 5.1 %collective-permute-done.44 = bf16[64,3072]{1,0:T(8,128)(2,1)S(1)} collective-permute-done((bf16[64,3072]{1,0:T(8,128)(2,1)}, bf16[64,3072]{1,0:T(8,128)(2,1)S(1)}, u32[]{:S(2)}, u32[]{:S(2)}) %collective-permute-start.44) | collective-permute-done | bytes 393248 | tf_op jit(solution)/shard_map/ppermute | solution.py:49
  258.1 3.2 collective-permute-start.36
  262.4 4.0 %collective-permute-done.42 = bf16[64,3072]{1,0:T(8,128)(2,1)S(1)} collective-permute-done((bf16[64,3072]{1,0:T(8,128)(2,1)}, bf16[64,3072]{1,0:T(8,128)(2,1)S(1)}, u32[]{:S(2)}, u32[]{:S(2)}) %collective-permute-start.42) | collective-permute-done | bytes 393248 | tf_op jit(solution)/shard_map/ppermute | solution.py:49
  268.8 4.3 %collective-permute-done.40 = bf16[64,3072]{1,0:T(8,128)(2,1)S(1)} collective-permute-done((bf16[64,3072]{1,0:T(8,128)(2,1)}, bf16[64,3072]{1,0:T(8,128)(2,1)S(1)}, u32[]{:S(2)}, u32[]{:S(2)}) %collective-permute-start.40) | collective-permute-done | bytes 393248 | tf_op jit(solution)/shard_map/ppermute | solution.py:49
  273.2 3.3 collective-permute-start.41
  276.5 3.5 collective-permute-done.37
  280.0 3.4 collective-permute-done.36
  284.5 3.8 collective-permute-done.45
  288.3 4.6 %collective-permute-done.43 = bf16[64,3072]{1,0:T(8,128)(2,1)S(1)} collective-permute-done((bf16[64,3072]{1,0:T(8,128)(2,1)S(1)}, bf16[64,3072]{1,0:T(8,128)(2,1)S(1)}, u32[]{:S(2)}, u32[]{:S(2)}) %collective-permute-start.43) | collective-permute-done | bytes 393248 | tf_op jit(solution)/shard_map/ppermute | solution.py:53
  301.3 3.6 all-to-all-start.2
  306.3 14.4 %all-to-all-done.2 = bf16[16,8,3840]{2,1,0:T(8,128)(2,1)S(1)} async-done(((bf16[16,8,3840]{2,1,0:T(8,128)(2,1)}), bf16[16,8,3840]{2,1,0:T(8,128)(2,1)S(1)}, u32[]{:S(2)}, u32[]{:S(2)}) %all-to-all-start.2) | async-done | bytes 983072 | tf_op jit(solution)/shard_map/all_to_all | solution.py:57
  335.7 4.7 %shard_map.91 = bf16[64,144,128]{2,1,0:T(8,128)(2,1)} custom-call(s32[1]{0:T(128)} %bitcast.35.refs_0_, bf16[256,3072]{1,0:T(8,128)(2,1)S(1)} %pad_maximum_fusion.1.refs_1_, bf16[256,3072]{1,0:T(8,128)(2,1)S(1)} %pad_maximum_fusion.2.refs_2_, bf16[256,768]{1,0:T(8,128)(2,1)S(1)} %pad_maximum_fusion.11.refs_3_), custom_call_target="tpu_custom_call" | custom-call | flops 1207959552 | bytes 8388608 | tf_op jit(solution)/shard_map/pallas_call | solution.py:365
  340.3 9.5 %all-to-all-start.3 = ((bf16[64,144,128]{2,1,0:T(8,128)(2,1)}), bf16[64,144,128]{2,1,0:T(8,128)(2,1)}, u32[]{:S(2)}, u32[]{:S(2)}) async-start(bf16[64,144,128]{2,1,0:T(8,128)(2,1)} %shard_map.91), calls=%async_computation.3 | async-start | bytes 4718592 | tf_op jit(solution)/shard_map/all_to_all | solution.py:57
  349.9 3.3 fusion.79
  354.7 28.1 %all-to-all-done.3 = bf16[64,144,128]{2,1,0:T(8,128)(2,1)} async-done(((bf16[64,144,128]{2,1,0:T(8,128)(2,1)}), bf16[64,144,128]{2,1,0:T(8,128)(2,1)}, u32[]{:S(2)}, u32[]{:S(2)}) %all-to-all-start.3) | async-done | bytes 2359328 | tf_op jit(solution)/shard_map/all_to_all | solution.py:57
  (230 shorter events, 149.8 us)
Async XLA Ops:
  5.6 23.2 %all-to-all-start = ((bf16[16,8,3840]{2,1,0:T(8,128)(2,1)}), bf16[16,8,3840]{2,1,0:T(8,128)(2,1)S(1)}, u32[]{:S(2)}, u32[]{:S(2)}) async-start(bf16[16,8,3840]{2,1,0:T(8,128)(2,1)} %pad_maximum_fusion.3), calls=%async_computation | async-start | bytes 1966080 | tf_op jit(solution)/shard_map/all_to_all | solution.py:57
  12.0 22.9 %collective-permute-start.1 = (bf16[128,3072]{1,0:T(8,128)(2,1)S(1)}, bf16[128,3072]{1,0:T(8,128)(2,1)}, u32[]{:S(2)}, u32[]{:S(2)}) collective-permute-start(bf16[128,3072]{1,0:T(8,128)(2,1)S(1)} %fusion.13), channel_id=1, source_target_pairs={{0,1},{1,0},{2,3},{3,2},{4,5},{5,4},{6,7},{7,6},{8,9},{9,8},{10,11... | collective-permute-start | bytes 2359304 | tf_op jit(solution)/shard_map/ppermute | solution.py:49
  43.5 24.5 %collective-permute-start.8 = (bf16[160,3072]{1,0:T(8,128)(2,1)S(1)}, bf16[160,3072]{1,0:T(8,128)(2,1)}, u32[]{:S(2)}, u32[]{:S(2)}) collective-permute-start(bf16[160,3072]{1,0:T(8,128)(2,1)S(1)} %pad_maximum_fusion.4.refs_0_), channel_id=1, source_target_pairs={{0,16},{16,0},{1,17},{17,1},{2,18},{18,2},{3,19},{19,3},{4,20},{20... | collective-permute-start | bytes 2949128 | tf_op jit(solution)/shard_map/ppermute | solution.py:49
  79.8 20.9 %collective-permute-start.15 = (bf16[96,3072]{1,0:T(8,128)(2,1)}, bf16[96,3072]{1,0:T(8,128)(2,1)}, u32[]{:S(2)}, u32[]{:S(2)}) collective-permute-start(bf16[96,3072]{1,0:T(8,128)(2,1)} %slice.95), channel_id=1, source_target_pairs={{0,64},{32,96},{64,0},{96,32},{1,65},{33,97},{65,1},{97,33},{2,66}... | collective-permute-start | bytes 1769480 | tf_op jit(solution)/shard_map/ppermute | solution.py:53
  81.1 19.6 %collective-permute-start.16 = (bf16[96,3072]{1,0:T(8,128)(2,1)}, bf16[96,3072]{1,0:T(8,128)(2,1)}, u32[]{:S(2)}, u32[]{:S(2)}) collective-permute-start(bf16[96,3072]{1,0:T(8,128)(2,1)} %collective-permute-done.9.refs_2_), channel_id=1, source_target_pairs={{0,16},{16,0},{1,17},{17,1},{2,18},{18,2},{3,19},{19,3},{4,20},{20... | collective-permute-start | bytes 1769480 | tf_op jit(solution)/shard_map/ppermute | solution.py:49
  84.2 26.8 %collective-permute-start.17 = (bf16[96,3072]{1,0:T(8,128)(2,1)}, bf16[96,3072]{1,0:T(8,128)(2,1)}, u32[]{:S(2)}, u32[]{:S(2)}) collective-permute-start(bf16[96,3072]{1,0:T(8,128)(2,1)} %collective-permute-done.10.refs_3_), channel_id=1, source_target_pairs={{0,16},{16,0},{1,17},{17,1},{2,18},{18,2},{3,19},{19,3},{4,20},{20... | collective-permute-start | bytes 1769480 | tf_op jit(solution)/shard_map/ppermute | solution.py:49
  86.7 27.5 %collective-permute-start.18 = (bf16[128,3072]{1,0:T(8,128)(2,1)}, bf16[128,3072]{1,0:T(8,128)(2,1)}, u32[]{:S(2)}, u32[]{:S(2)}) collective-permute-start(bf16[128,3072]{1,0:T(8,128)(2,1)} %pad_maximum_fusion.9), channel_id=1, source_target_pairs={{0,32},{32,64},{64,96},{96,0},{1,33},{33,65},{65,97},{97,1},{2,34}... | collective-permute-start | bytes 2359304 | tf_op jit(solution)/shard_map/ppermute | solution.py:53
  88.4 25.8 %collective-permute-start.19 = (bf16[128,3072]{1,0:T(8,128)(2,1)}, bf16[128,3072]{1,0:T(8,128)(2,1)}, u32[]{:S(2)}, u32[]{:S(2)}) collective-permute-start(bf16[128,3072]{1,0:T(8,128)(2,1)} %pad_maximum_fusion.9), channel_id=1, source_target_pairs={{0,96},{32,0},{64,32},{96,64},{1,97},{33,1},{65,33},{97,65},{2,98}... | collective-permute-start | bytes 2359304 | tf_op jit(solution)/shard_map/ppermute | solution.py:53
  115.9 20.1 %all-to-all-start.1 = ((bf16[16,8,3840]{2,1,0:T(8,128)(2,1)}), bf16[16,8,3840]{2,1,0:T(8,128)(2,1)S(1)}, u32[]{:S(2)}, u32[]{:S(2)}) async-start(bf16[16,8,3840]{2,1,0:T(8,128)(2,1)} %pad_maximum_fusion.5), calls=%async_computation.1 | async-start | bytes 1966080 | tf_op jit(solution)/shard_map/all_to_all | solution.py:57
  120.3 27.5 %collective-permute-start.21 = (bf16[128,3072]{1,0:T(8,128)(2,1)}, bf16[128,3072]{1,0:T(8,128)(2,1)}, u32[]{:S(2)}, u32[]{:S(2)}) collective-permute-start(bf16[128,3072]{1,0:T(8,128)(2,1)} %pad_maximum_fusion.9), channel_id=1, source_target_pairs={{0,64},{32,96},{64,0},{96,32},{1,65},{33,97},{65,1},{97,33},{2,66}... | collective-permute-start | bytes 2359304 | tf_op jit(solution)/shard_map/ppermute | solution.py:53
  122.1 25.7 %collective-permute-start.20 = (bf16[96,3072]{1,0:T(8,128)(2,1)}, bf16[96,3072]{1,0:T(8,128)(2,1)}, u32[]{:S(2)}, u32[]{:S(2)}) collective-permute-start(bf16[96,3072]{1,0:T(8,128)(2,1)} %collective-permute-done.15.refs_4_), channel_id=1, source_target_pairs={{0,16},{16,0},{1,17},{17,1},{2,18},{18,2},{3,19},{19,3},{4,20},{20... | collective-permute-start | bytes 1769480 | tf_op jit(solution)/shard_map/ppermute | solution.py:49
  147.8 34.5 %collective-permute-start.22 = (bf16[160,3072]{1,0:T(8,128)(2,1)S(1)}, bf16[160,3072]{1,0:T(8,128)(2,1)}, u32[]{:S(2)}, u32[]{:S(2)}) collective-permute-start(bf16[160,3072]{1,0:T(8,128)(2,1)S(1)} %pad_maximum_fusion.6.refs_0_), channel_id=1, source_target_pairs={{0,16},{16,0},{1,17},{17,1},{2,18},{18,2},{3,19},{19,3},{4,20},{20... | collective-permute-start | bytes 2949128 | tf_op jit(solution)/shard_map/ppermute | solution.py:49
  151.5 27.2 %collective-permute-start.24 = (bf16[96,3072]{1,0:T(8,128)(2,1)}, bf16[96,3072]{1,0:T(8,128)(2,1)}, u32[]{:S(2)}, u32[]{:S(2)}) collective-permute-start(bf16[96,3072]{1,0:T(8,128)(2,1)} %slice.110), channel_id=1, source_target_pairs={{0,96},{32,0},{64,32},{96,64},{1,97},{33,1},{65,33},{97,65},{2,98}... | collective-permute-start | bytes 1769480 | tf_op jit(solution)/shard_map/ppermute | solution.py:53
  153.6 26.8 %collective-permute-start.25 = (bf16[96,3072]{1,0:T(8,128)(2,1)}, bf16[96,3072]{1,0:T(8,128)(2,1)}, u32[]{:S(2)}, u32[]{:S(2)}) collective-permute-start(bf16[96,3072]{1,0:T(8,128)(2,1)} %slice.110), channel_id=1, source_target_pairs={{0,64},{32,96},{64,0},{96,32},{1,65},{33,97},{65,1},{97,33},{2,66}... | collective-permute-start | bytes 1769480 | tf_op jit(solution)/shard_map/ppermute | solution.py:53
  178.7 28.6 %collective-permute-start.27 = (bf16[96,3072]{1,0:T(8,128)(2,1)}, bf16[96,3072]{1,0:T(8,128)(2,1)}, u32[]{:S(2)}, u32[]{:S(2)}) collective-permute-start(bf16[96,3072]{1,0:T(8,128)(2,1)} %collective-permute-done.24.refs_3_), channel_id=1, source_target_pairs={{0,16},{16,0},{1,17},{17,1},{2,18},{18,2},{3,19},{19,3},{4,20},{20... | collective-permute-start | bytes 1769480 | tf_op jit(solution)/shard_map/ppermute | solution.py:49
  180.4 30.4 %collective-permute-start.28 = (bf16[96,3072]{1,0:T(8,128)(2,1)}, bf16[96,3072]{1,0:T(8,128)(2,1)}, u32[]{:S(2)}, u32[]{:S(2)}) collective-permute-start(bf16[96,3072]{1,0:T(8,128)(2,1)} %collective-permute-done.25.refs_4_), channel_id=1, source_target_pairs={{0,16},{16,0},{1,17},{17,1},{2,18},{18,2},{3,19},{19,3},{4,20},{20... | collective-permute-start | bytes 1769480 | tf_op jit(solution)/shard_map/ppermute | solution.py:49
  183.3 35.3 %collective-permute-start.29 = (bf16[128,3072]{1,0:T(8,128)(2,1)S(1)}, bf16[128,3072]{1,0:T(8,128)(2,1)}, u32[]{:S(2)}, u32[]{:S(2)}) collective-permute-start(bf16[128,3072]{1,0:T(8,128)(2,1)S(1)} %pad_maximum_fusion.10), channel_id=1, source_target_pairs={{0,32},{32,64},{64,96},{96,0},{1,33},{33,65},{65,97},{97,1},{2,34}... | collective-permute-start | bytes 2359304 | tf_op jit(solution)/shard_map/ppermute | solution.py:53
  184.1 34.6 %collective-permute-start.30 = (bf16[128,3072]{1,0:T(8,128)(2,1)S(1)}, bf16[128,3072]{1,0:T(8,128)(2,1)}, u32[]{:S(2)}, u32[]{:S(2)}) collective-permute-start(bf16[128,3072]{1,0:T(8,128)(2,1)S(1)} %pad_maximum_fusion.10), channel_id=1, source_target_pairs={{0,96},{32,0},{64,32},{96,64},{1,97},{33,1},{65,33},{97,65},{2,98}... | collective-permute-start | bytes 2359304 | tf_op jit(solution)/shard_map/ppermute | solution.py:53
  187.2 34.0 %collective-permute-start.31 = (bf16[128,3072]{1,0:T(8,128)(2,1)S(1)}, bf16[128,3072]{1,0:T(8,128)(2,1)}, u32[]{:S(2)}, u32[]{:S(2)}) collective-permute-start(bf16[128,3072]{1,0:T(8,128)(2,1)S(1)} %pad_maximum_fusion.10), channel_id=1, source_target_pairs={{0,64},{32,96},{64,0},{96,32},{1,65},{33,97},{65,1},{97,33},{2,66}... | collective-permute-start | bytes 2359304 | tf_op jit(solution)/shard_map/ppermute | solution.py:53
  207.4 36.2 %collective-permute-start.32 = (bf16[96,3072]{1,0:T(8,128)(2,1)}, bf16[96,3072]{1,0:T(8,128)(2,1)}, u32[]{:S(2)}, u32[]{:S(2)}) collective-permute-start(bf16[96,3072]{1,0:T(8,128)(2,1)} %get-tuple-element.55), channel_id=1, source_target_pairs={{0,96},{32,0},{64,32},{96,64},{1,97},{33,1},{65,33},{97,65},{2,98}... | collective-permute-start | bytes 1769480 | tf_op jit(solution)/shard_map/ppermute | solution.py:53
  210.8 33.5 %collective-permute-start.33 = (bf16[96,3072]{1,0:T(8,128)(2,1)}, bf16[96,3072]{1,0:T(8,128)(2,1)}, u32[]{:S(2)}, u32[]{:S(2)}) collective-permute-start(bf16[96,3072]{1,0:T(8,128)(2,1)} %get-tuple-element.56), channel_id=1, source_target_pairs={{0,32},{32,64},{64,96},{96,0},{1,33},{33,65},{65,97},{97,1},{2,34}... | collective-permute-start | bytes 1769480 | tf_op jit(solution)/shard_map/ppermute | solution.py:53
  218.7 25.6 %collective-permute-start.34 = (bf16[96,3072]{1,0:T(8,128)(2,1)}, bf16[96,3072]{1,0:T(8,128)(2,1)}, u32[]{:S(2)}, u32[]{:S(2)}) collective-permute-start(bf16[96,3072]{1,0:T(8,128)(2,1)} %get-tuple-element.57), channel_id=1, source_target_pairs={{0,64},{32,96},{64,0},{96,32},{1,65},{33,97},{65,1},{97,33},{2,66}... | collective-permute-start | bytes 1769480 | tf_op jit(solution)/shard_map/ppermute | solution.py:53
  218.7 22.7 %collective-permute-start.35 = (bf16[64,3072]{1,0:T(8,128)(2,1)}, bf16[64,3072]{1,0:T(8,128)(2,1)S(1)}, u32[]{:S(2)}, u32[]{:S(2)}) collective-permute-start(bf16[64,3072]{1,0:T(8,128)(2,1)} %get-tuple-element.58), channel_id=1, source_target_pairs={{0,16},{16,0},{1,17},{17,1},{2,18},{18,2},{3,19},{19,3},{4,20},{20... | collective-permute-start | bytes 1179656 | tf_op jit(solution)/shard_map/ppermute | solution.py:49
  245.7 20.7 %collective-permute-start.42 = (bf16[64,3072]{1,0:T(8,128)(2,1)}, bf16[64,3072]{1,0:T(8,128)(2,1)S(1)}, u32[]{:S(2)}, u32[]{:S(2)}) collective-permute-start(bf16[64,3072]{1,0:T(8,128)(2,1)} %get-tuple-element.69), channel_id=1, source_target_pairs={{0,16},{16,0},{1,17},{17,1},{2,18},{18,2},{3,19},{19,3},{4,20},{20... | collective-permute-start | bytes 1179656 | tf_op jit(solution)/shard_map/ppermute | solution.py:49
  247.8 25.2 %collective-permute-start.40 = (bf16[64,3072]{1,0:T(8,128)(2,1)}, bf16[64,3072]{1,0:T(8,128)(2,1)S(1)}, u32[]{:S(2)}, u32[]{:S(2)}) collective-permute-start(bf16[64,3072]{1,0:T(8,128)(2,1)} %get-tuple-element.67), channel_id=1, source_target_pairs={{0,16},{16,0},{1,17},{17,1},{2,18},{18,2},{3,19},{19,3},{4,20},{20... | collective-permute-start | bytes 1179656 | tf_op jit(solution)/shard_map/ppermute | solution.py:49
  249.3 23.9 %collective-permute-start.38 = (bf16[96,3072]{1,0:T(8,128)(2,1)}, bf16[96,3072]{1,0:T(8,128)(2,1)S(1)}, u32[]{:S(2)}, u32[]{:S(2)}) collective-permute-start(bf16[96,3072]{1,0:T(8,128)(2,1)} %get-tuple-element.61), channel_id=1, source_target_pairs={{0,64},{32,96},{64,0},{96,32},{1,65},{33,97},{65,1},{97,33},{2,66}... | collective-permute-start | bytes 1769480 | tf_op jit(solution)/shard_map/ppermute | solution.py:53
  250.3 29.6 %collective-permute-start.37 = (bf16[96,3072]{1,0:T(8,128)(2,1)}, bf16[96,3072]{1,0:T(8,128)(2,1)S(1)}, u32[]{:S(2)}, u32[]{:S(2)}) collective-permute-start(bf16[96,3072]{1,0:T(8,128)(2,1)} %get-tuple-element.60), channel_id=1, source_target_pairs={{0,32},{32,64},{64,96},{96,0},{1,33},{33,65},{65,97},{97,1},{2,34}... | collective-permute-start | bytes 1769480 | tf_op jit(solution)/shard_map/ppermute | solution.py:53
  258.1 25.3 %collective-permute-start.36 = (bf16[96,3072]{1,0:T(8,128)(2,1)}, bf16[96,3072]{1,0:T(8,128)(2,1)S(1)}, u32[]{:S(2)}, u32[]{:S(2)}) collective-permute-start(bf16[96,3072]{1,0:T(8,128)(2,1)} %get-tuple-element.59), channel_id=1, source_target_pairs={{0,96},{32,0},{64,32},{96,64},{1,97},{33,1},{65,33},{97,65},{2,98}... | collective-permute-start | bytes 1769480 | tf_op jit(solution)/shard_map/ppermute | solution.py:53
  266.5 21.8 %collective-permute-start.45 = (bf16[64,3072]{1,0:T(8,128)(2,1)S(1)}, bf16[64,3072]{1,0:T(8,128)(2,1)S(1)}, u32[]{:S(2)}, u32[]{:S(2)}) collective-permute-start(bf16[64,3072]{1,0:T(8,128)(2,1)S(1)} %add_convert_fusion.3), channel_id=1, source_target_pairs={{0,64},{32,96},{64,0},{96,32},{1,65},{33,97},{65,1},{97,33},{2,66}... | collective-permute-start | bytes 1179656 | tf_op jit(solution)/shard_map/ppermute | solution.py:53
  273.1 19.9 %collective-permute-start.43 = (bf16[64,3072]{1,0:T(8,128)(2,1)S(1)}, bf16[64,3072]{1,0:T(8,128)(2,1)S(1)}, u32[]{:S(2)}, u32[]{:S(2)}) collective-permute-start(bf16[64,3072]{1,0:T(8,128)(2,1)S(1)} %add_convert_fusion.4), channel_id=1, source_target_pairs={{0,32},{32,64},{64,96},{96,0},{1,33},{33,65},{65,97},{97,1},{2,34}... | collective-permute-start | bytes 1179656 | tf_op jit(solution)/shard_map/ppermute | solution.py:53
  273.2 21.3 %collective-permute-start.41 = (bf16[64,3072]{1,0:T(8,128)(2,1)S(1)}, bf16[64,3072]{1,0:T(8,128)(2,1)S(1)}, u32[]{:S(2)}, u32[]{:S(2)}) collective-permute-start(bf16[64,3072]{1,0:T(8,128)(2,1)S(1)} %add_convert_fusion.5), channel_id=1, source_target_pairs={{0,96},{32,0},{64,32},{96,64},{1,97},{33,1},{65,33},{97,65},{2,98}... | collective-permute-start | bytes 1179656 | tf_op jit(solution)/shard_map/ppermute | solution.py:53
  340.3 42.5 %all-to-all-start.3 = ((bf16[64,144,128]{2,1,0:T(8,128)(2,1)}), bf16[64,144,128]{2,1,0:T(8,128)(2,1)}, u32[]{:S(2)}, u32[]{:S(2)}) async-start(bf16[64,144,128]{2,1,0:T(8,128)(2,1)} %shard_map.91), calls=%async_computation.3 | async-start | bytes 4718592 | tf_op jit(solution)/shard_map/all_to_all | solution.py:57
  (54 other events, 635.0 us)

commit v6 on v4

--- a/solution.py
+++ b/solution.py
@@ -423,7 +423,7 @@
     main, extra = between_experts(contract(slots, normed_two_b, 1, 0).astype(BF16))
     near_acts = act_grads(cot_near, outer)
     far_acts = act_grads(cot_far, outer)
-    near = spread_near(after(jnp.concatenate([main, extra], axis=0), near_acts, cot_far[2], cot_far[5]))
+    near = spread_near(after(jnp.concatenate([main, extra], axis=0), near_acts, cot_far[5]))
     h = HALF
     whole = EXPERTS * CAP
     rest = whole - h

time: 393 us -> 386 us (0.982)
  waiting for transfers between devices: 167 us -> 158 us
    ppermute x19, waiting for transfers between devices: 44.3 us -> 36.1 us  [swap(): return lax.ppermute(values, axis, [(0, 1), (1, 0)])]
  transfers between devices with their start and end apart: 50 -> 50, of which waited for: 28 -> 27; matrix products, arithmetic and copies ran while one was open for 9% -> 9% of each run, Pallas kernels for 14% -> 14%
where the time goes in v6:
time: 386 us; the launch traced here: 379 us
  waiting for transfers between devices  158 us (41%)
  starting transfers between devices  95.9 us (25%)
  Pallas kernels  62.7 us (16%)
  other arithmetic  25.6 us (7%)
  matrix products  19.4 us (5%)
  local copies, waits for them, and re-layouts  15.8 us (4%)
    ppermute x27, waiting for transfers between devices, along_z(): return lax.ppermute(values, 'z', [(i, (i + shift) % 4) for i in range(4)])  75.5 us
    all_to_all x4, waiting for transfers between devices, exchange(): return lax.all_to_all(blocks, axes, split_axis=0, concat_axis=0, tiled=True)  46.1 us
    ppermute x27, starting transfers between devices, along_z(): return lax.ppermute(values, 'z', [(i, (i + shift) % 4) for i in range(4)])  43.9 us
    pallas_call x2, Pallas kernels, experts(): pl.pallas_call(lambda *refs: expert_kernel(counts, pieces_out, tall, *ref...  38.7 us
    ppermute x19, waiting for transfers between devices, swap(): return lax.ppermute(values, axis, [(0, 1), (1, 0)])  36.1 us
    ppermute x19, starting transfers between devices, swap(): return lax.ppermute(values, axis, [(0, 1), (1, 0)])  30.4 us
    all_to_all x4, starting transfers between devices, exchange(): return lax.all_to_all(blocks, axes, split_axis=0, concat_axis=0, tiled=True)  21.6 us
    pallas_call x2, Pallas kernels, act_grads(): pl.pallas_call(lambda *refs: act_kernel(counts, *refs), out_shape=jax.Sha...  15.5 us
  transfers between devices with their start and end apart: 50, of which 27 were waited for; matrix products, arithmetic and copies ran while one was open for 9% of the time, Pallas kernels for 14%

profile of v6, /device:TPU:0, one launch (start us, length us, event | category | flops | bytes accessed | tf_op | source)
XLA Modules:
  0.0 379.0 jit_solution(1659174694427323640)
XLA Ops:
  5.6 5.5 %all-to-all-start = ((bf16[16,8,3840]{2,1,0:T(8,128)(2,1)}), bf16[16,8,3840]{2,1,0:T(8,128)(2,1)S(1)}, u32[]{:S(2)}, u32[]{:S(2)}) async-start(bf16[16,8,3840]{2,1,0:T(8,128)(2,1)} %pad_maximum_fusion.3), calls=%async_computation | async-start | bytes 1966080 | tf_op jit(solution)/shard_map/all_to_all | solution.py:57
  30.7 4.2 %collective-permute-done.refs_2_ = bf16[1152,128]{1,0:T(8,128)(2,1)} collective-permute-done((bf16[1152,128]{1,0:T(8,128)(2,1)}, bf16[1152,128]{1,0:T(8,128)(2,1)}, u32[]{:S(2)}, u32[]{:S(2)}) %collective-permute-start) | collective-permute-done | bytes 294944 | tf_op jit(solution)/shard_map/ppermute | solution.py:49
  34.9 3.2 collective-permute-done.5.refs_6_
  38.1 3.2 collective-permute-done.6.refs_7_
  53.9 9.6 %collective-permute-done.9.refs_2_ = bf16[96,3072]{1,0:T(8,128)(2,1)} collective-permute-done((bf16[96,3072]{1,0:T(8,128)(2,1)}, bf16[96,3072]{1,0:T(8,128)(2,1)}, u32[]{:S(2)}, u32[]{:S(2)}) %collective-permute-start.9) | collective-permute-done | bytes 589856 | tf_op jit(solution)/shard_map/ppermute | solution.py:53
  70.4 5.3 %collective-permute-done.13.refs_11_ = bf16[1152,128]{1,0:T(8,128)(2,1)} collective-permute-done((bf16[1152,128]{1,0:T(8,128)(2,1)}, bf16[1152,128]{1,0:T(8,128)(2,1)}, u32[]{:S(2)}, u32[]{:S(2)}) %collective-permute-start.13) | collective-permute-done | bytes 294944 | tf_op jit(solution)/shard_map/ppermute | solution.py:53
  75.8 3.9 %shard_map.86 = bf16[8,1152,128]{2,1,0:T(8,128)(2,1)} custom-call(s32[2]{0:T(128)} %pad_add_fusion.refs_0_, bf16[1152,128]{1,0:T(8,128)(2,1)} %constant_dynamic-slice_fusion.2.refs_1_, bf16[1152,128]{1,0:T(8,128)(2,1)} %collective-permute-done.refs_2_, bf16[576,128]{1,0:T(8,128)(2,1)} %collective-permute-done.2.refs_3_, ...), custom_call_target="tpu_custom_call" | custom-call | tf_op jit(solution)/shard_map/pallas_call | solution.py:128
  81.1 3.1 collective-permute-start.16
  100.7 10.4 %collective-permute-done.17.refs_1_ = bf16[96,3072]{1,0:T(8,128)(2,1)} collective-permute-done((bf16[96,3072]{1,0:T(8,128)(2,1)}, bf16[96,3072]{1,0:T(8,128)(2,1)}, u32[]{:S(2)}, u32[]{:S(2)}) %collective-permute-start.17) | collective-permute-done | bytes 589856 | tf_op jit(solution)/shard_map/ppermute | solution.py:49
  111.1 3.2 collective-permute-done.18.refs_3_
  116.0 4.3 %all-to-all-start.1 = ((bf16[16,8,3840]{2,1,0:T(8,128)(2,1)}), bf16[16,8,3840]{2,1,0:T(8,128)(2,1)S(1)}, u32[]{:S(2)}, u32[]{:S(2)}) async-start(bf16[16,8,3840]{2,1,0:T(8,128)(2,1)} %pad_maximum_fusion.5), calls=%async_computation.1 | async-start | bytes 1966080 | tf_op jit(solution)/shard_map/all_to_all | solution.py:57
  125.0 7.5 %shard_map.87.refs_5_ = bf16[608,768]{1,0:T(8,128)(2,1)} custom-call(bf16[160,3072]{1,0:T(8,128)(2,1)} %copy-done.5, bf16[160,3072]{1,0:T(8,128)(2,1)} %collective-permute-done.8.refs_1_, bf16[96,3072]{1,0:T(8,128)(2,1)} %collective-permute-done.9.refs_2_, bf16[96,3072]{1,0:T(8,128)(2,1)} %collective-permute-done.10.refs_3_, ...), custom_call_target="tpu_custom_call" | custom-call | flops 2868903936 | bytes 8454144 | tf_op jit(solution)/shard_map/pallas_call | solution.py:214
  132.5 3.6 all-to-all-done.1
  149.5 8.0 %shard_map.89.refs_6_ = bf16[672,768]{1,0:T(8,128)(2,1)} custom-call(bf16[96,3072]{1,0:T(8,128)(2,1)} %collective-permute-done.16.refs_0_, bf16[96,3072]{1,0:T(8,128)(2,1)} %collective-permute-done.17.refs_1_, bf16[96,3072]{1,0:T(8,128)(2,1)} %collective-permute-done.25.refs_2_, bf16[128,3072]{1,0:T(8,128)(2,1)} %collective-permute-done.18.refs_3_, ...), custom_call_target="tpu_custom_call" | custom-call | flops 3170893824 | bytes 8847360 | tf_op jit(solution)/shard_map/pallas_call | solution.py:214
  157.6 5.3 %collective-permute-done.22.refs_2_ = bf16[96,3072]{1,0:T(8,128)(2,1)} collective-permute-done((bf16[96,3072]{1,0:T(8,128)(2,1)}, bf16[96,3072]{1,0:T(8,128)(2,1)}, u32[]{:S(2)}, u32[]{:S(2)}) %collective-permute-start.22) | collective-permute-done | bytes 589856 | tf_op jit(solution)/shard_map/ppermute | solution.py:53
  163.6 10.0 %collective-permute-done.23.refs_3_ = bf16[96,3072]{1,0:T(8,128)(2,1)} collective-permute-done((bf16[96,3072]{1,0:T(8,128)(2,1)}, bf16[96,3072]{1,0:T(8,128)(2,1)}, u32[]{:S(2)}, u32[]{:S(2)}) %collective-permute-start.23) | collective-permute-done | bytes 589856 | tf_op jit(solution)/shard_map/ppermute | solution.py:53
  178.3 3.7 collective-permute-start.30
  183.7 18.5 %shard_map.88 = (bf16[160,3072]{1,0:T(8,128)(2,1)}, bf16[96,3072]{1,0:T(8,128)(2,1)}, bf16[64,3072]{1,0:T(8,128)(2,1)}, bf16[96,3072]{1,0:T(8,128)(2,1)}, bf16[9...) custom-call(bf16[160,3072]{1,0:T(8,128)(2,1)} %copy-done.4, bf16[160,3072]{1,0:T(8,128)(2,1)} %collective-permute-done.21.refs_1_, ...), custom_call_target="tpu_custom_call" | custom-call | flops 11475615744 | bytes 16908288 | tf_op jit(solution)/shard_map/pallas_call | solution.py:317
  208.0 4.3 %collective-permute-done.29.refs_3_ = bf16[128,3072]{1,0:T(8,128)(2,1)} collective-permute-done((bf16[128,3072]{1,0:T(8,128)(2,1)S(1)}, bf16[128,3072]{1,0:T(8,128)(2,1)}, u32[]{:S(2)}, u32[]{:S(2)}) %collective-permute-start.29) | collective-permute-done | bytes 786464 | tf_op jit(solution)/shard_map/ppermute | solution.py:53
  213.6 20.1 %shard_map.90 = (bf16[96,3072]{1,0:T(8,128)(2,1)}, bf16[96,3072]{1,0:T(8,128)(2,1)}, bf16[96,3072]{1,0:T(8,128)(2,1)}, bf16[192,3072]{1,0:T(8,128)(2,1)}, bf16[192,3072]{1,0:T(8,128)(2,1)}) custom-call(bf16[96,3072]{1,0:T(8,128)(2,1)} %copy-done.32, bf16[96,3072]{1,0:T(8,128)(2,1)} %collective-permute-done.27.refs_1_, ...), custom_call_target="tpu_custom_call" | custom-call | flops 12683575296 | bytes 17694720 | tf_op jit(solution)/shard_map/pallas_call | solution.py:317
  233.8 3.3 collective-permute-done.32
  245.0 10.7 %collective-permute-done.38 = bf16[96,3072]{1,0:T(8,128)(2,1)S(1)} collective-permute-done((bf16[96,3072]{1,0:T(8,128)(2,1)}, bf16[96,3072]{1,0:T(8,128)(2,1)S(1)}, u32[]{:S(2)}, u32[]{:S(2)}) %collective-permute-start.38) | collective-permute-done | bytes 589856 | tf_op jit(solution)/shard_map/ppermute | solution.py:53
  255.7 11.3 %collective-permute-done.37 = bf16[96,3072]{1,0:T(8,128)(2,1)S(1)} collective-permute-done((bf16[96,3072]{1,0:T(8,128)(2,1)}, bf16[96,3072]{1,0:T(8,128)(2,1)S(1)}, u32[]{:S(2)}, u32[]{:S(2)}) %collective-permute-start.37) | collective-permute-done | bytes 589856 | tf_op jit(solution)/shard_map/ppermute | solution.py:53
  268.5 3.1 collective-permute-start.39
  276.3 8.9 %collective-permute-done.39 = bf16[96,3072]{1,0:T(8,128)(2,1)S(1)} collective-permute-done((bf16[96,3072]{1,0:T(8,128)(2,1)S(1)}, bf16[96,3072]{1,0:T(8,128)(2,1)S(1)}, u32[]{:S(2)}, u32[]{:S(2)}) %collective-permute-start.39) | collective-permute-done | bytes 589856 | tf_op jit(solution)/shard_map/ppermute | solution.py:49
  287.1 4.8 %collective-permute-done.42 = bf16[64,3072]{1,0:T(8,128)(2,1)S(1)} collective-permute-done((bf16[64,3072]{1,0:T(8,128)(2,1)S(1)}, bf16[64,3072]{1,0:T(8,128)(2,1)S(1)}, u32[]{:S(2)}, u32[]{:S(2)}) %collective-permute-start.42) | collective-permute-done | bytes 393248 | tf_op jit(solution)/shard_map/ppermute | solution.py:53
  296.0 4.4 %all-to-all-start.2 = ((bf16[16,8,3840]{2,1,0:T(8,128)(2,1)}), bf16[16,8,3840]{2,1,0:T(8,128)(2,1)S(1)}, u32[]{:S(2)}, u32[]{:S(2)}) async-start(bf16[16,8,3840]{2,1,0:T(8,128)(2,1)} %pad_maximum_fusion.7), calls=%async_computation.2 | async-start | bytes 1966080 | tf_op jit(solution)/shard_map/all_to_all | solution.py:57
  301.8 14.4 %all-to-all-done.2 = bf16[16,8,3840]{2,1,0:T(8,128)(2,1)S(1)} async-done(((bf16[16,8,3840]{2,1,0:T(8,128)(2,1)}), bf16[16,8,3840]{2,1,0:T(8,128)(2,1)S(1)}, u32[]{:S(2)}, u32[]{:S(2)}) %all-to-all-start.2) | async-done | bytes 983072 | tf_op jit(solution)/shard_map/all_to_all | solution.py:57
  330.9 4.6 %shard_map.91 = bf16[64,144,128]{2,1,0:T(8,128)(2,1)} custom-call(s32[1]{0:T(128)} %bitcast.35.refs_0_, bf16[256,3072]{1,0:T(8,128)(2,1)S(1)} %pad_maximum_fusion.1.refs_1_, bf16[256,3072]{1,0:T(8,128)(2,1)S(1)} %pad_maximum_fusion.2.refs_2_, bf16[256,768]{1,0:T(8,128)(2,1)S(1)} %pad_maximum_fusion.11.refs_3_), custom_call_target="tpu_custom_call" | custom-call | flops 1207959552 | bytes 8388608 | tf_op jit(solution)/shard_map/pallas_call | solution.py:367
  335.6 7.3 %all-to-all-start.3 = ((bf16[64,144,128]{2,1,0:T(8,128)(2,1)}), bf16[64,144,128]{2,1,0:T(8,128)(2,1)}, u32[]{:S(2)}, u32[]{:S(2)}) async-start(bf16[64,144,128]{2,1,0:T(8,128)(2,1)} %shard_map.91), calls=%async_computation.3 | async-start | bytes 4718592 | tf_op jit(solution)/shard_map/all_to_all | solution.py:57
  342.9 3.3 fusion.79
  347.8 28.1 %all-to-all-done.3 = bf16[64,144,128]{2,1,0:T(8,128)(2,1)} async-done(((bf16[64,144,128]{2,1,0:T(8,128)(2,1)}), bf16[64,144,128]{2,1,0:T(8,128)(2,1)}, u32[]{:S(2)}, u32[]{:S(2)}) %all-to-all-start.3) | async-done | bytes 2359328 | tf_op jit(solution)/shard_map/all_to_all | solution.py:57
  (227 shorter events, 135.5 us)
Async XLA Ops:
  5.6 23.2 %all-to-all-start = ((bf16[16,8,3840]{2,1,0:T(8,128)(2,1)}), bf16[16,8,3840]{2,1,0:T(8,128)(2,1)S(1)}, u32[]{:S(2)}, u32[]{:S(2)}) async-start(bf16[16,8,3840]{2,1,0:T(8,128)(2,1)} %pad_maximum_fusion.3), calls=%async_computation | async-start | bytes 1966080 | tf_op jit(solution)/shard_map/all_to_all | solution.py:57
  12.0 22.9 %collective-permute-start.1 = (bf16[128,3072]{1,0:T(8,128)(2,1)S(1)}, bf16[128,3072]{1,0:T(8,128)(2,1)}, u32[]{:S(2)}, u32[]{:S(2)}) collective-permute-start(bf16[128,3072]{1,0:T(8,128)(2,1)S(1)} %fusion.13), channel_id=1, source_target_pairs={{0,1},{1,0},{2,3},{3,2},{4,5},{5,4},{6,7},{7,6},{8,9},{9,8},{10,11... | collective-permute-start | bytes 2359304 | tf_op jit(solution)/shard_map/ppermute | solution.py:49
  43.5 24.5 %collective-permute-start.8 = (bf16[160,3072]{1,0:T(8,128)(2,1)S(1)}, bf16[160,3072]{1,0:T(8,128)(2,1)}, u32[]{:S(2)}, u32[]{:S(2)}) collective-permute-start(bf16[160,3072]{1,0:T(8,128)(2,1)S(1)} %pad_maximum_fusion.4.refs_0_), channel_id=1, source_target_pairs={{0,16},{16,0},{1,17},{17,1},{2,18},{18,2},{3,19},{19,3},{4,20},{20... | collective-permute-start | bytes 2949128 | tf_op jit(solution)/shard_map/ppermute | solution.py:49
  47.6 18.7 %collective-permute-start.10 = (bf16[96,3072]{1,0:T(8,128)(2,1)}, bf16[96,3072]{1,0:T(8,128)(2,1)}, u32[]{:S(2)}, u32[]{:S(2)}) collective-permute-start(bf16[96,3072]{1,0:T(8,128)(2,1)} %slice.104), channel_id=1, source_target_pairs={{0,96},{32,0},{64,32},{96,64},{1,97},{33,1},{65,33},{97,65},{2,98}... | collective-permute-start | bytes 1769480 | tf_op jit(solution)/shard_map/ppermute | solution.py:53
  51.3 19.1 %collective-permute-start.12 = (bf16[1152,128]{1,0:T(8,128)(2,1)}, bf16[1152,128]{1,0:T(8,128)(2,1)S(1)}, u32[]{:S(2)}, u32[]{:S(2)}) collective-permute-start(bf16[1152,128]{1,0:T(8,128)(2,1)} %pad_maximum_fusion.12), channel_id=1, source_target_pairs={{0,96},{32,0},{64,32},{96,64},{1,97},{33,1},{65,33},{97,65},{2,98}... | collective-permute-start | bytes 884744 | tf_op jit(solution)/shard_map/ppermute | solution.py:53
  79.8 20.8 %collective-permute-start.15 = (bf16[96,3072]{1,0:T(8,128)(2,1)}, bf16[96,3072]{1,0:T(8,128)(2,1)}, u32[]{:S(2)}, u32[]{:S(2)}) collective-permute-start(bf16[96,3072]{1,0:T(8,128)(2,1)} %slice.104), channel_id=1, source_target_pairs={{0,64},{32,96},{64,0},{96,32},{1,65},{33,97},{65,1},{97,33},{2,66}... | collective-permute-start | bytes 1769480 | tf_op jit(solution)/shard_map/ppermute | solution.py:53
  81.1 19.5 %collective-permute-start.16 = (bf16[96,3072]{1,0:T(8,128)(2,1)}, bf16[96,3072]{1,0:T(8,128)(2,1)}, u32[]{:S(2)}, u32[]{:S(2)}) collective-permute-start(bf16[96,3072]{1,0:T(8,128)(2,1)} %collective-permute-done.9.refs_2_), channel_id=1, source_target_pairs={{0,16},{16,0},{1,17},{17,1},{2,18},{18,2},{3,19},{19,3},{4,20},{20... | collective-permute-start | bytes 1769480 | tf_op jit(solution)/shard_map/ppermute | solution.py:49
  84.3 26.8 %collective-permute-start.17 = (bf16[96,3072]{1,0:T(8,128)(2,1)}, bf16[96,3072]{1,0:T(8,128)(2,1)}, u32[]{:S(2)}, u32[]{:S(2)}) collective-permute-start(bf16[96,3072]{1,0:T(8,128)(2,1)} %collective-permute-done.10.refs_3_), channel_id=1, source_target_pairs={{0,16},{16,0},{1,17},{17,1},{2,18},{18,2},{3,19},{19,3},{4,20},{20... | collective-permute-start | bytes 1769480 | tf_op jit(solution)/shard_map/ppermute | solution.py:49
  86.7 27.6 %collective-permute-start.18 = (bf16[128,3072]{1,0:T(8,128)(2,1)}, bf16[128,3072]{1,0:T(8,128)(2,1)}, u32[]{:S(2)}, u32[]{:S(2)}) collective-permute-start(bf16[128,3072]{1,0:T(8,128)(2,1)} %pad_maximum_fusion.9), channel_id=1, source_target_pairs={{0,32},{32,64},{64,96},{96,0},{1,33},{33,65},{65,97},{97,1},{2,34}... | collective-permute-start | bytes 2359304 | tf_op jit(solution)/shard_map/ppermute | solution.py:53
  88.5 25.9 %collective-permute-start.19 = (bf16[128,3072]{1,0:T(8,128)(2,1)}, bf16[128,3072]{1,0:T(8,128)(2,1)}, u32[]{:S(2)}, u32[]{:S(2)}) collective-permute-start(bf16[128,3072]{1,0:T(8,128)(2,1)} %pad_maximum_fusion.9), channel_id=1, source_target_pairs={{0,96},{32,0},{64,32},{96,64},{1,97},{33,1},{65,33},{97,65},{2,98}... | collective-permute-start | bytes 2359304 | tf_op jit(solution)/shard_map/ppermute | solution.py:53
  116.0 20.1 %all-to-all-start.1 = ((bf16[16,8,3840]{2,1,0:T(8,128)(2,1)}), bf16[16,8,3840]{2,1,0:T(8,128)(2,1)S(1)}, u32[]{:S(2)}, u32[]{:S(2)}) async-start(bf16[16,8,3840]{2,1,0:T(8,128)(2,1)} %pad_maximum_fusion.5), calls=%async_computation.1 | async-start | bytes 1966080 | tf_op jit(solution)/shard_map/all_to_all | solution.py:57
  120.3 21.7 %collective-permute-start.20 = (bf16[128,3072]{1,0:T(8,128)(2,1)}, bf16[128,3072]{1,0:T(8,128)(2,1)}, u32[]{:S(2)}, u32[]{:S(2)}) collective-permute-start(bf16[128,3072]{1,0:T(8,128)(2,1)} %pad_maximum_fusion.9), channel_id=1, source_target_pairs={{0,64},{32,96},{64,0},{96,32},{1,65},{33,97},{65,1},{97,33},{2,66}... | collective-permute-start | bytes 2359304 | tf_op jit(solution)/shard_map/ppermute | solution.py:53
  122.2 27.3 %collective-permute-start.25 = (bf16[96,3072]{1,0:T(8,128)(2,1)}, bf16[96,3072]{1,0:T(8,128)(2,1)}, u32[]{:S(2)}, u32[]{:S(2)}) collective-permute-start(bf16[96,3072]{1,0:T(8,128)(2,1)} %collective-permute-done.15.refs_4_), channel_id=1, source_target_pairs={{0,16},{16,0},{1,17},{17,1},{2,18},{18,2},{3,19},{19,3},{4,20},{20... | collective-permute-start | bytes 1769480 | tf_op jit(solution)/shard_map/ppermute | solution.py:49
  142.0 35.1 %collective-permute-start.21 = (bf16[160,3072]{1,0:T(8,128)(2,1)S(1)}, bf16[160,3072]{1,0:T(8,128)(2,1)}, u32[]{:S(2)}, u32[]{:S(2)}) collective-permute-start(bf16[160,3072]{1,0:T(8,128)(2,1)S(1)} %pad_maximum_fusion.6.refs_0_), channel_id=1, source_target_pairs={{0,16},{16,0},{1,17},{17,1},{2,18},{18,2},{3,19},{19,3},{4,20},{20... | collective-permute-start | bytes 2949128 | tf_op jit(solution)/shard_map/ppermute | solution.py:49
  146.8 26.8 %collective-permute-start.23 = (bf16[96,3072]{1,0:T(8,128)(2,1)}, bf16[96,3072]{1,0:T(8,128)(2,1)}, u32[]{:S(2)}, u32[]{:S(2)}) collective-permute-start(bf16[96,3072]{1,0:T(8,128)(2,1)} %slice.119), channel_id=1, source_target_pairs={{0,96},{32,0},{64,32},{96,64},{1,97},{33,1},{65,33},{97,65},{2,98}... | collective-permute-start | bytes 1769480 | tf_op jit(solution)/shard_map/ppermute | solution.py:53
  148.9 26.0 %collective-permute-start.24 = (bf16[96,3072]{1,0:T(8,128)(2,1)}, bf16[96,3072]{1,0:T(8,128)(2,1)}, u32[]{:S(2)}, u32[]{:S(2)}) collective-permute-start(bf16[96,3072]{1,0:T(8,128)(2,1)} %slice.119), channel_id=1, source_target_pairs={{0,64},{32,96},{64,0},{96,32},{1,65},{33,97},{65,1},{97,33},{2,66}... | collective-permute-start | bytes 1769480 | tf_op jit(solution)/shard_map/ppermute | solution.py:53
  162.9 19.2 %collective-permute-start.26 = (bf16[96,3072]{1,0:T(8,128)(2,1)}, bf16[96,3072]{1,0:T(8,128)(2,1)S(1)}, u32[]{:S(2)}, u32[]{:S(2)}) collective-permute-start(bf16[96,3072]{1,0:T(8,128)(2,1)} %collective-permute-done.22.refs_2_), channel_id=1, source_target_pairs={{0,16},{16,0},{1,17},{17,1},{2,18},{18,2},{3,19},{19,3},{4,20},{20... | collective-permute-start | bytes 1769480 | tf_op jit(solution)/shard_map/ppermute | solution.py:49
  173.6 28.6 %collective-permute-start.27 = (bf16[96,3072]{1,0:T(8,128)(2,1)}, bf16[96,3072]{1,0:T(8,128)(2,1)}, u32[]{:S(2)}, u32[]{:S(2)}) collective-permute-start(bf16[96,3072]{1,0:T(8,128)(2,1)} %collective-permute-done.23.refs_3_), channel_id=1, source_target_pairs={{0,16},{16,0},{1,17},{17,1},{2,18},{18,2},{3,19},{19,3},{4,20},{20... | collective-permute-start | bytes 1769480 | tf_op jit(solution)/shard_map/ppermute | solution.py:49
  174.9 31.9 %collective-permute-start.28 = (bf16[96,3072]{1,0:T(8,128)(2,1)}, bf16[96,3072]{1,0:T(8,128)(2,1)}, u32[]{:S(2)}, u32[]{:S(2)}) collective-permute-start(bf16[96,3072]{1,0:T(8,128)(2,1)} %collective-permute-done.24.refs_4_), channel_id=1, source_target_pairs={{0,16},{16,0},{1,17},{17,1},{2,18},{18,2},{3,19},{19,3},{4,20},{20... | collective-permute-start | bytes 1769480 | tf_op jit(solution)/shard_map/ppermute | solution.py:49
  178.3 34.1 %collective-permute-start.29 = (bf16[128,3072]{1,0:T(8,128)(2,1)S(1)}, bf16[128,3072]{1,0:T(8,128)(2,1)}, u32[]{:S(2)}, u32[]{:S(2)}) collective-permute-start(bf16[128,3072]{1,0:T(8,128)(2,1)S(1)} %pad_maximum_fusion.10), channel_id=1, source_target_pairs={{0,32},{32,64},{64,96},{96,0},{1,33},{33,65},{65,97},{97,1},{2,34}... | collective-permute-start | bytes 2359304 | tf_op jit(solution)/shard_map/ppermute | solution.py:53
  178.3 34.0 %collective-permute-start.30 = (bf16[128,3072]{1,0:T(8,128)(2,1)S(1)}, bf16[128,3072]{1,0:T(8,128)(2,1)}, u32[]{:S(2)}, u32[]{:S(2)}) collective-permute-start(bf16[128,3072]{1,0:T(8,128)(2,1)S(1)} %pad_maximum_fusion.10), channel_id=1, source_target_pairs={{0,96},{32,0},{64,32},{96,64},{1,97},{33,1},{65,33},{97,65},{2,98}... | collective-permute-start | bytes 2359304 | tf_op jit(solution)/shard_map/ppermute | solution.py:53
  182.1 31.5 %collective-permute-start.31 = (bf16[128,3072]{1,0:T(8,128)(2,1)S(1)}, bf16[128,3072]{1,0:T(8,128)(2,1)}, u32[]{:S(2)}, u32[]{:S(2)}) collective-permute-start(bf16[128,3072]{1,0:T(8,128)(2,1)S(1)} %pad_maximum_fusion.10), channel_id=1, source_target_pairs={{0,64},{32,96},{64,0},{96,32},{1,65},{33,97},{65,1},{97,33},{2,66}... | collective-permute-start | bytes 2359304 | tf_op jit(solution)/shard_map/ppermute | solution.py:53
  202.3 34.8 %collective-permute-start.32 = (bf16[96,3072]{1,0:T(8,128)(2,1)}, bf16[96,3072]{1,0:T(8,128)(2,1)}, u32[]{:S(2)}, u32[]{:S(2)}) collective-permute-start(bf16[96,3072]{1,0:T(8,128)(2,1)} %get-tuple-element.47), channel_id=1, source_target_pairs={{0,96},{32,0},{64,32},{96,64},{1,97},{33,1},{65,33},{97,65},{2,98}... | collective-permute-start | bytes 1769480 | tf_op jit(solution)/shard_map/ppermute | solution.py:53
  206.9 30.9 %collective-permute-start.33 = (bf16[96,3072]{1,0:T(8,128)(2,1)}, bf16[96,3072]{1,0:T(8,128)(2,1)}, u32[]{:S(2)}, u32[]{:S(2)}) collective-permute-start(bf16[96,3072]{1,0:T(8,128)(2,1)} %get-tuple-element.48), channel_id=1, source_target_pairs={{0,32},{32,64},{64,96},{96,0},{1,33},{33,65},{65,97},{97,1},{2,34}... | collective-permute-start | bytes 1769480 | tf_op jit(solution)/shard_map/ppermute | solution.py:53
  212.4 25.4 %collective-permute-start.34 = (bf16[96,3072]{1,0:T(8,128)(2,1)}, bf16[96,3072]{1,0:T(8,128)(2,1)}, u32[]{:S(2)}, u32[]{:S(2)}) collective-permute-start(bf16[96,3072]{1,0:T(8,128)(2,1)} %get-tuple-element.49), channel_id=1, source_target_pairs={{0,64},{32,96},{64,0},{96,32},{1,65},{33,97},{65,1},{97,33},{2,66}... | collective-permute-start | bytes 1769480 | tf_op jit(solution)/shard_map/ppermute | solution.py:53
  212.4 21.4 %collective-permute-start.35 = (bf16[64,3072]{1,0:T(8,128)(2,1)}, bf16[64,3072]{1,0:T(8,128)(2,1)S(1)}, u32[]{:S(2)}, u32[]{:S(2)}) collective-permute-start(bf16[64,3072]{1,0:T(8,128)(2,1)} %get-tuple-element.50), channel_id=1, source_target_pairs={{0,16},{16,0},{1,17},{17,1},{2,18},{18,2},{3,19},{19,3},{4,20},{20... | collective-permute-start | bytes 1179656 | tf_op jit(solution)/shard_map/ppermute | solution.py:49
  238.9 28.1 %collective-permute-start.37 = (bf16[96,3072]{1,0:T(8,128)(2,1)}, bf16[96,3072]{1,0:T(8,128)(2,1)S(1)}, u32[]{:S(2)}, u32[]{:S(2)}) collective-permute-start(bf16[96,3072]{1,0:T(8,128)(2,1)} %get-tuple-element.52), channel_id=1, source_target_pairs={{0,32},{32,64},{64,96},{96,0},{1,33},{33,65},{65,97},{97,1},{2,34}... | collective-permute-start | bytes 1769480 | tf_op jit(solution)/shard_map/ppermute | solution.py:53
  241.6 25.5 %collective-permute-start.36 = (bf16[96,3072]{1,0:T(8,128)(2,1)}, bf16[96,3072]{1,0:T(8,128)(2,1)S(1)}, u32[]{:S(2)}, u32[]{:S(2)}) collective-permute-start(bf16[96,3072]{1,0:T(8,128)(2,1)} %get-tuple-element.51), channel_id=1, source_target_pairs={{0,96},{32,0},{64,32},{96,64},{1,97},{33,1},{65,33},{97,65},{2,98}... | collective-permute-start | bytes 1769480 | tf_op jit(solution)/shard_map/ppermute | solution.py:53
  243.3 28.3 %collective-permute-start.40 = (bf16[192,3072]{1,0:T(8,128)(2,1)}, bf16[192,3072]{1,0:T(8,128)(2,1)S(1)}, u32[]{:S(2)}, u32[]{:S(2)}) collective-permute-start(bf16[192,3072]{1,0:T(8,128)(2,1)} %get-tuple-element.59), channel_id=1, source_target_pairs={{0,16},{16,0},{1,17},{17,1},{2,18},{18,2},{3,19},{19,3},{4,20},{20... | collective-permute-start | bytes 3538952 | tf_op jit(solution)/shard_map/ppermute | solution.py:49
  273.1 18.8 %collective-permute-start.42 = (bf16[64,3072]{1,0:T(8,128)(2,1)S(1)}, bf16[64,3072]{1,0:T(8,128)(2,1)S(1)}, u32[]{:S(2)}, u32[]{:S(2)}) collective-permute-start(bf16[64,3072]{1,0:T(8,128)(2,1)S(1)} %get-tuple-element.70), channel_id=1, source_target_pairs={{0,32},{32,64},{64,96},{96,0},{1,33},{33,65},{65,97},{97,1},{2,34}... | collective-permute-start | bytes 1179656 | tf_op jit(solution)/shard_map/ppermute | solution.py:53
  296.0 20.2 %all-to-all-start.2 = ((bf16[16,8,3840]{2,1,0:T(8,128)(2,1)}), bf16[16,8,3840]{2,1,0:T(8,128)(2,1)S(1)}, u32[]{:S(2)}, u32[]{:S(2)}) async-start(bf16[16,8,3840]{2,1,0:T(8,128)(2,1)} %pad_maximum_fusion.7), calls=%async_computation.2 | async-start | bytes 1966080 | tf_op jit(solution)/shard_map/all_to_all | solution.py:57
  335.6 40.3 %all-to-all-start.3 = ((bf16[64,144,128]{2,1,0:T(8,128)(2,1)}), bf16[64,144,128]{2,1,0:T(8,128)(2,1)}, u32[]{:S(2)}, u32[]{:S(2)}) async-start(bf16[64,144,128]{2,1,0:T(8,128)(2,1)} %shard_map.91), calls=%async_computation.3 | async-start | bytes 4718592 | tf_op jit(solution)/shard_map/all_to_all | solution.py:57
  (53 other events, 587.8 us)
